TPU v7x, 256 devices: a whole 4x4x8 slice. The times are simulated.
256 devices in a mesh: row: 8 (over y_hi, x), col: 2 (over y_lo), chan: 16 (over z, core).
Axes of the slice: x: 4, y: 4 (y_hi: 2, y_lo: 2; y = y_hi * 2 + y_lo), z: 8, core: 2. Of those that a mesh axis runs over, the one named last changes fastest.
Arguments:
- visibilities: float32 [2, 64, 2, 1024, 1024], P(None, 'chan', None, 'row', 'col'), parts along dimension 1, as said below
- stations: float32 [2, 16384], P(None, 'chan'), parts along dimension 1, may hold values from -300 to 300
- pixels: int32 [16384], P('chan'), parts along dimension 0, may hold values from 0 to 1048575
- flux: float32 [64, 2, 1024], P('chan'), parts along dimension 0, may hold values from 0.01 to 0.1
- freqs: float32 [64], P('chan'), parts along dimension 0, may hold values from 0.8 to 1.25
- flags: int32 [64, 1024], P('chan'), parts along dimension 0, may hold values 0 or 1
Outputs:
- gains: float32 [2, 64, 2, 1024], P(None, 'chan'), parts along dimension 1
- residual: float32 [2, 64, 2, 1024, 1024], P(None, 'chan', None, 'row', 'col'), parts along dimension 1
There are 16 independent parts, one for each index of `chan`. A program takes and returns all parts, laid end to end along the dimension named above; each array names one. Nothing has to cross between parts.
Inputs may be any that keep to these rules, and one draw needn't show every extreme that they name: For each channel and polarisation the matrix visibilities[0] + i visibilities[1] over the two station dimensions is Hermitian up to float32 rounding.
All inputs are finite; a program needn't handle non-finite values.
Results may differ from a plain program's by a relative error of at most 0.0047.
Values sent between devices are 32-bit elements; how exact they have to be, the bound alone decides.
No kernel may reach another device: no remote copies, remote signals or barrier semaphores. Data moves between devices by JAX's collectives and lax.ppermute only.
A program may use at most 64 MiB of HBM per device.

v0:
```python
import math

import jax
import jax.numpy as jnp
from jax import lax
from jax.sharding import PartitionSpec as P

ITERS = 8
SIDE = 1024


two_pi = 2.0 * math.pi


def directions(pixels):
    across = (pixels % SIDE).astype(jnp.float32)
    down = (pixels // SIDE).astype(jnp.float32)
    lvals = (across + 0.5) / SIDE * 0.5 - 0.25
    mvals = (down + 0.5) / SIDE * 0.5 - 0.25
    return (lvals, mvals)


def steering(coord_u, coord_v, lvals, mvals, ratio):
    phase = two_pi * ratio * (coord_u[:, None] * lvals[None, :] + coord_v[:, None] * mvals[None, :])
    return (jnp.cos(phase), jnp.sin(phase))


def predict(cos_rows, sin_rows, cos_cols, sin_cols, flux_one):
    left = jnp.concatenate(
        [cos_rows[None] * flux_one[:, None, :], sin_rows[None] * flux_one[:, None, :]], -1
    ).astype(jnp.bfloat16)
    right = jnp.concatenate(
        [jnp.concatenate([cos_cols, sin_cols], 1), jnp.concatenate([sin_cols, -cos_cols], 1)], 0
    ).astype(jnp.bfloat16)
    out = jnp.einsum("prk,ck->prc", left, right, preferred_element_type=jnp.float32)
    width = cos_cols.shape[0]
    return (out[..., :width], out[..., width:])


def partial_sums(vis_re, vis_im, m_re, m_im, g_re_q, g_im_q, w_q):
    gre = g_re_q[..., None]
    gim = g_im_q[..., None]
    weight = w_q[:, None, :, None]
    z_re = gre * m_re - gim * m_im
    z_im = gre * m_im + gim * m_re
    num_re = jnp.sum(weight * (vis_re * z_re + vis_im * z_im), axis=2)
    num_im = jnp.sum(weight * (vis_re * z_im - vis_im * z_re), axis=2)
    den = jnp.sum(weight * (z_re * z_re + z_im * z_im), axis=2)
    return (num_re, num_im, den)


def update(g_re, g_im, num_re, num_im, den, weight, step):
    wide = weight[:, None, :]
    scale = wide / (den + 1.0 - wide)
    new_re = num_re * scale
    new_im = num_im * scale
    if step % 2 == 1:
        return (0.5 * (new_re + g_re), 0.5 * (new_im + g_im))
    return (new_re, new_im)


def corrected(vis_re, vis_im, m_re, m_im, g_re_p, g_im_p, g_re_q, g_im_q):
    gqr = g_re_q[:, :, None, :]
    gqi = g_im_q[:, :, None, :]
    a_re = m_re * gqr + m_im * gqi
    a_im = m_im * gqr - m_re * gqi
    gpr = g_re_p[..., None]
    gpi = g_im_p[..., None]
    return (vis_re - (gpr * a_re - gpi * a_im), vis_im - (gpr * a_im + gpi * a_re))


def body(visibilities, stations, pixels, flux, freqs, flags):
    row_count = visibilities.shape[3]
    col_count = visibilities.shape[4]
    total = stations.shape[1]
    channels = visibilities.shape[1]
    row_start = lax.axis_index("row") * row_count
    col_start = lax.axis_index("col") * col_count
    lvals, mvals = directions(pixels)
    u_rows = lax.dynamic_slice_in_dim(stations[0], row_start, row_count)
    v_rows = lax.dynamic_slice_in_dim(stations[1], row_start, row_count)
    u_cols = lax.dynamic_slice_in_dim(stations[0], col_start, col_count)
    v_cols = lax.dynamic_slice_in_dim(stations[1], col_start, col_count)
    model_re = []
    model_im = []
    for chan_index in range(channels):
        cos_rows, sin_rows = steering(u_rows, v_rows, lvals, mvals, freqs[chan_index])
        cos_cols, sin_cols = steering(u_cols, v_cols, lvals, mvals, freqs[chan_index])
        part_re, part_im = predict(cos_rows, sin_rows, cos_cols, sin_cols, flux[chan_index])
        model_re.append(part_re)
        model_im.append(part_im)
    m_re = jnp.stack(model_re)
    m_im = jnp.stack(model_im)
    vis_re = visibilities[0]
    vis_im = visibilities[1]
    weight = flags.astype(jnp.float32)
    w_rows = lax.dynamic_slice_in_dim(weight, row_start, row_count, 1)
    full_shape = (channels, m_re.shape[1], total)
    g_re = jnp.broadcast_to(weight[:, None, :], full_shape)
    g_im = jnp.zeros(full_shape, jnp.float32)
    for step in range(ITERS):
        g_re_rows = lax.dynamic_slice_in_dim(g_re, row_start, row_count, 2)
        g_im_rows = lax.dynamic_slice_in_dim(g_im, row_start, row_count, 2)
        num_re, num_im, den = partial_sums(vis_re, vis_im, m_re, m_im, g_re_rows, g_im_rows, w_rows)
        blank = jnp.zeros(full_shape, jnp.float32)
        placed_re = lax.dynamic_update_slice_in_dim(blank, num_re, col_start, 2)
        placed_im = lax.dynamic_update_slice_in_dim(blank, num_im, col_start, 2)
        placed_den = lax.dynamic_update_slice_in_dim(blank, den, col_start, 2)
        sum_re, sum_im, sum_den = lax.psum((placed_re, placed_im, placed_den), ("row", "col"))
        g_re, g_im = update(g_re, g_im, sum_re, sum_im, sum_den, weight, step)
    g_re_rows = lax.dynamic_slice_in_dim(g_re, row_start, row_count, 2)
    g_im_rows = lax.dynamic_slice_in_dim(g_im, row_start, row_count, 2)
    g_re_cols = lax.dynamic_slice_in_dim(g_re, col_start, col_count, 2)
    g_im_cols = lax.dynamic_slice_in_dim(g_im, col_start, col_count, 2)
    res_re, res_im = corrected(
        vis_re, vis_im, m_re, m_im, g_re_rows, g_im_rows, g_re_cols, g_im_cols
    )
    return (jnp.stack([g_re, g_im]), jnp.stack([res_re, res_im]))


def solution(mesh):
    in_specs = (
        P(None, "chan", None, "row", "col"),
        P(None, "chan"),
        P("chan"),
        P("chan", None, None),
        P("chan"),
        P("chan", None),
    )
    out_specs = (P(None, "chan", None, None), P(None, "chan", None, "row", "col"))
    return jax.shard_map(body, mesh=mesh, in_specs=in_specs, out_specs=out_specs, check_vma=False)
```

profile of v0, /device:TPU:32, one launch (start us, length us, event | category | flops | bytes accessed | tf_op | source)
XLA Modules:
  0.0 867.7 jit_solution(17854704493877938843)
XLA Ops:
  8.1 1.5 fusion.151
  13.6 7.4 fusion.105
  21.0 31.2 %fusion.87 = (bf16[512,1024]{1,0:T(8,128)(2,1)S(1)}, bf16[512,1024]{1,0:T(8,128)(2,1)S(1)}, bf16[512,1024]{1,0:T(8,128)(2,1)S(1)}, bf16[512,1024]{1,0:T(8,128)(2...) fusion(f32[1024]{0:T(1024)S(1)} %get-tuple-element.130, ...), kind=kLoop, calls=%fused_computation.165 | loop fusion | flops 12058624 | bytes 12595216 | tf_op jit(solution)/shard_map/convert.28
  59.3 1.3 slice_bitcast_fusion.10
  63.3 1.4 fusion.30
  66.8 95.6 %all-reduce.31.cloned.1.call-done = (f32[4,2,1024]{2,1,0:T(2,128)}, f32[4,2,1024]{2,1,0:T(2,128)}, f32[4,2,1024]{2,1,0:T(2,128)}) async-done(((f32[4,2,1024]{2,1,0:T(2,128)}, f32[4,2,1024]{2,1,0:T(2,128)}, f32[4,2,1024]{2,1,0:T(2,128)}), (f32[4,2,1024]{2,1,0:T(2,128)}, f32[4,2,1024]{2,1,0:T(2,128)}, f32[4,2,1024]{2,1,0:T(2,128)})) %all-reduce.31.cloned.1.call-update) | async-done | bytes 98320 | tf_op jit(solution)/shard_map/psum | solution.py:109
  164.0 2.1 multiply_subtract_fusion.7
  166.5 1.3 fusion.36
  168.7 92.2 %all-reduce.29.cloned.1.call-done = (f32[4,2,1024]{2,1,0:T(2,128)}, f32[4,2,1024]{2,1,0:T(2,128)}, f32[4,2,1024]{2,1,0:T(2,128)}) async-done(((f32[4,2,1024]{2,1,0:T(2,128)}, f32[4,2,1024]{2,1,0:T(2,128)}, f32[4,2,1024]{2,1,0:T(2,128)}), (f32[4,2,1024]{2,1,0:T(2,128)}, f32[4,2,1024]{2,1,0:T(2,128)}, f32[4,2,1024]{2,1,0:T(2,128)})) %all-reduce.29.cloned.1.call-update) | async-done | bytes 98320 | tf_op jit(solution)/shard_map/psum | solution.py:109
  262.3 1.8 multiply_subtract_fusion.6
  267.0 92.2 %all-reduce.27.cloned.1.call-done = (f32[4,2,1024]{2,1,0:T(2,128)}, f32[4,2,1024]{2,1,0:T(2,128)}, f32[4,2,1024]{2,1,0:T(2,128)}) async-done(((f32[4,2,1024]{2,1,0:T(2,128)}, f32[4,2,1024]{2,1,0:T(2,128)}, f32[4,2,1024]{2,1,0:T(2,128)}), (f32[4,2,1024]{2,1,0:T(2,128)}, f32[4,2,1024]{2,1,0:T(2,128)}, f32[4,2,1024]{2,1,0:T(2,128)})) %all-reduce.27.cloned.1.call-update) | async-done | bytes 98320 | tf_op jit(solution)/shard_map/psum | solution.py:109
  360.8 1.8 multiply_subtract_fusion.5
  365.4 92.2 %all-reduce.25.cloned.1.call-done = (f32[4,2,1024]{2,1,0:T(2,128)}, f32[4,2,1024]{2,1,0:T(2,128)}, f32[4,2,1024]{2,1,0:T(2,128)}) async-done(((f32[4,2,1024]{2,1,0:T(2,128)}, f32[4,2,1024]{2,1,0:T(2,128)}, f32[4,2,1024]{2,1,0:T(2,128)}), (f32[4,2,1024]{2,1,0:T(2,128)}, f32[4,2,1024]{2,1,0:T(2,128)}, f32[4,2,1024]{2,1,0:T(2,128)})) %all-reduce.25.cloned.1.call-update) | async-done | bytes 98320 | tf_op jit(solution)/shard_map/psum | solution.py:109
  459.1 1.8 multiply_subtract_fusion.4
  463.7 92.2 %all-reduce.23.cloned.1.call-done = (f32[4,2,1024]{2,1,0:T(2,128)}, f32[4,2,1024]{2,1,0:T(2,128)}, f32[4,2,1024]{2,1,0:T(2,128)}) async-done(((f32[4,2,1024]{2,1,0:T(2,128)}, f32[4,2,1024]{2,1,0:T(2,128)}, f32[4,2,1024]{2,1,0:T(2,128)}), (f32[4,2,1024]{2,1,0:T(2,128)}, f32[4,2,1024]{2,1,0:T(2,128)}, f32[4,2,1024]{2,1,0:T(2,128)})) %all-reduce.23.cloned.1.call-update) | async-done | bytes 98320 | tf_op jit(solution)/shard_map/psum | solution.py:109
  557.5 1.8 multiply_subtract_fusion.3
  562.2 92.2 %all-reduce.21.cloned.1.call-done = (f32[4,2,1024]{2,1,0:T(2,128)}, f32[4,2,1024]{2,1,0:T(2,128)}, f32[4,2,1024]{2,1,0:T(2,128)}) async-done(((f32[4,2,1024]{2,1,0:T(2,128)}, f32[4,2,1024]{2,1,0:T(2,128)}, f32[4,2,1024]{2,1,0:T(2,128)}), (f32[4,2,1024]{2,1,0:T(2,128)}, f32[4,2,1024]{2,1,0:T(2,128)}, f32[4,2,1024]{2,1,0:T(2,128)})) %all-reduce.21.cloned.1.call-update) | async-done | bytes 98320 | tf_op jit(solution)/shard_map/psum | solution.py:109
  655.8 1.8 multiply_subtract_fusion.2
  660.5 92.2 %all-reduce.19.cloned.1.call-done = (f32[4,2,1024]{2,1,0:T(2,128)}, f32[4,2,1024]{2,1,0:T(2,128)}, f32[4,2,1024]{2,1,0:T(2,128)}) async-done(((f32[4,2,1024]{2,1,0:T(2,128)}, f32[4,2,1024]{2,1,0:T(2,128)}, f32[4,2,1024]{2,1,0:T(2,128)}), (f32[4,2,1024]{2,1,0:T(2,128)}, f32[4,2,1024]{2,1,0:T(2,128)}, f32[4,2,1024]{2,1,0:T(2,128)})) %all-reduce.19.cloned.1.call-update) | async-done | bytes 98320 | tf_op jit(solution)/shard_map/psum | solution.py:109
  754.3 2.1 multiply_subtract_fusion.1
  756.8 1.3 fusion.72
  758.9 92.2 %all-reduce.17.cloned.1.call-done = (f32[4,2,1024]{2,1,0:T(2,128)}, f32[4,2,1024]{2,1,0:T(2,128)}, f32[4,2,1024]{2,1,0:T(2,128)}) async-done(((f32[4,2,1024]{2,1,0:T(2,128)}, f32[4,2,1024]{2,1,0:T(2,128)}, f32[4,2,1024]{2,1,0:T(2,128)}), (f32[4,2,1024]{2,1,0:T(2,128)}, f32[4,2,1024]{2,1,0:T(2,128)}, f32[4,2,1024]{2,1,0:T(2,128)})) %all-reduce.17.cloned.1.call-update) | async-done | bytes 98320 | tf_op jit(solution)/shard_map/psum | solution.py:109
  852.1 3.0 subtract_subtract_fusion
  857.5 2.6 pad_maximum_fusion
  (205 shorter events, 44.7 us)
Async XLA Ops:
  7.2 155.2 %all-reduce.31.cloned.1.call-start = ((), (), s32[]{:S(2)}) async-start(), calls=%async_computation.7 | async-start | bytes 196608 | tf_op jit(solution)/shard_map/psum | solution.py:109
  60.8 2.5 copy-start
  66.8 194.1 %all-reduce.29.cloned.1.call-start = ((), (), s32[]{:S(2)}) async-start(), calls=%async_computation.6 | async-start | bytes 196608 | tf_op jit(solution)/shard_map/psum | solution.py:109
  164.0 2.5 copy-start.1
  168.6 190.5 %all-reduce.27.cloned.1.call-start = ((), (), s32[]{:S(2)}) async-start(), calls=%async_computation.5 | async-start | bytes 196608 | tf_op jit(solution)/shard_map/psum | solution.py:109
  262.3 2.5 copy-start.2
  266.9 190.7 %all-reduce.25.cloned.1.call-start = ((), (), s32[]{:S(2)}) async-start(), calls=%async_computation.4 | async-start | bytes 196608 | tf_op jit(solution)/shard_map/psum | solution.py:109
  360.8 2.5 copy-start.3
  365.4 190.5 %all-reduce.23.cloned.1.call-start = ((), (), s32[]{:S(2)}) async-start(), calls=%async_computation.3 | async-start | bytes 196608 | tf_op jit(solution)/shard_map/psum | solution.py:109
  459.1 2.5 copy-start.4
  463.7 190.7 %all-reduce.21.cloned.1.call-start = ((), (), s32[]{:S(2)}) async-start(), calls=%async_computation.2 | async-start | bytes 196608 | tf_op jit(solution)/shard_map/psum | solution.py:109
  557.5 2.5 copy-start.5
  562.1 190.5 %all-reduce.19.cloned.1.call-start = ((), (), s32[]{:S(2)}) async-start(), calls=%async_computation.1 | async-start | bytes 196608 | tf_op jit(solution)/shard_map/psum | solution.py:109
  655.8 2.5 copy-start.6
  660.4 190.7 %all-reduce.17.cloned.1.call-start = ((), (), s32[]{:S(2)}) async-start(), calls=%async_computation | async-start | bytes 196608 | tf_op jit(solution)/shard_map/psum | solution.py:109
  756.8 95.2 %copy-start.11 = (f32[1,1,2,128,512]{4,3,2,1,0:T(8,128)S(1)}, f32[1,1,2,128,512]{4,3,2,1,0:T(8,128)}, u32[]{:S(2)}) copy-start(f32[1,1,2,128,512]{4,3,2,1,0:T(8,128)} %get-tuple-element.71) | copy-start | bytes 1572868
  756.8 95.2 %copy-start.12 = (f32[1,1,2,128,512]{4,3,2,1,0:T(8,128)S(1)}, f32[1,1,2,128,512]{4,3,2,1,0:T(8,128)}, u32[]{:S(2)}) copy-start(f32[1,1,2,128,512]{4,3,2,1,0:T(8,128)} %get-tuple-element.72) | copy-start | bytes 1572868
  852.0 3.8 copy-start.8
  852.0 3.9 copy-start.13
  852.0 4.0 copy-start.14
  852.0 4.2 copy-start.15
  852.1 4.3 copy-start.16
  852.1 4.4 copy-start.17
  852.1 4.6 copy-start.18
  (28 other events, 21.2 us)
Sparse Core Ops, SparseCore 0:
  66.9 95.4 all-reduce.30
  168.7 92.0 all-reduce.28
  267.0 92.0 all-reduce.26
  365.5 92.0 all-reduce.24
  463.8 92.0 all-reduce.22
  562.2 92.0 all-reduce.20
  660.5 92.0 all-reduce.18
  759.0 92.0 all-reduce.16
where the time goes:
time: 869 us; the launch traced here: 868 us
  waiting for transfers between devices  741 us (85%)
  other arithmetic  84 us (10%)
  local copies, waits for them, and re-layouts  19.4 us (2%)
  between operations  17.8 us (2%)
    psum x8, waiting for transfers between devices, body(): lax.psum((placed_re, placed_im, placed_den), ('row', 'col'))  741 us
    another operation x5, other arithmetic  32 us
  transfers between devices with their start and end apart: 8, of which 8 were waited for; matrix products, arithmetic and copies ran while one was open for 0% of the time, Pallas kernels for 0%

commit v1 on v0

v1 whole, which is shorter than its diff:
```python
import functools

import jax
import jax.numpy as jnp
from jax import lax
from jax.experimental import pallas as pl
from jax.experimental.pallas import tpu as pltpu
from jax.sharding import PartitionSpec as P

ITERS = 8
SIDE = 1024
T = 128

SIN = (4.442867982256445, -7.307445413087933, 3.5948021037170865, -0.7844036262695797)
COS = (1.4142134965650144, -6.978850988238961, 5.739461170681741, -1.8835629873024078, 0.3106981918128224)
MAGIC = 12582912.0
F32 = jnp.float32
BF16 = jnp.bfloat16
VMEM_LIMIT = 56 * 1024 * 1024


def poly(y, coeffs):
    out = coeffs[-1]
    for c in reversed(coeffs[:-1]):
        out = out * y + c
    return out


def cos_sin(turns):
    r = turns - ((turns + MAGIC) - MAGIC)
    y = r * r
    s = r * poly(y, SIN)
    c = poly(y, COS)
    return 1.0 - s * s, s * c


def lm_rows(pix):
    across = (pix & (SIDE - 1)).astype(F32)
    down = (pix >> 10).astype(F32)
    lv = (across + 0.5) / SIDE * 0.5 - 0.25
    mv = (down + 0.5) / SIDE * 0.5 - 0.25
    return lv, mv


def spread(rows, out_ref):
    for t in range(8):
        out_ref[t * T:(t + 1) * T, :] = jnp.broadcast_to(rows[t:t + 1, :], (T, T)).T


def dot(a, b, dims):
    return lax.dot_general(a, b, (dims, ((), ())), preferred_element_type=F32)


def own_model(freqs, st, pix, flux, out_re, out_im, ub, vb, left, right):
    cp = lax.axis_index("row")
    f = freqs[cp // 2]
    lv, mv = lm_rows(pix[...])
    spread(st[0] * f, ub)
    spread(st[1] * f, vb)
    fx = flux[cp]

    def step(g, _):
        r = pl.multiple_of(g * 16, 16)
        u = ub[pl.ds(r, 16), :]
        v = vb[pl.ds(r, 16), :]
        for k in range(8):
            c, s = cos_sin(u * lv[k:k + 1, :] + v * mv[k:k + 1, :])
            w = fx[k:k + 1, :]
            lo, hi = k * T, (k + 1) * T
            left[pl.ds(r, 16), lo:hi] = (c * w).astype(BF16)
            left[pl.ds(r, 16), 1024 + lo:1024 + hi] = (s * w).astype(BF16)
            cb = c.astype(BF16)
            right[pl.ds(r, 16), lo:hi] = cb
            right[pl.ds(r, 16), 1024 + lo:1024 + hi] = s.astype(BF16)
            right[pl.ds(r, 16), 2048 + lo:2048 + hi] = -cb
        return 0

    lax.fori_loop(0, 64, step, 0)

    def mm(n, _):
        ns = pl.ds(pl.multiple_of(n * 512, 512), 512)
        for m in range(4):
            rows = slice(m * 256, (m + 1) * 256)
            a = left[rows, :]
            out_re[rows, ns] = dot(a, right[ns, 0:2048], ((1,), (1,)))
            out_im[rows, ns] = dot(a, right[ns, 1024:3072], ((1,), (1,)))
        return 0

    lax.fori_loop(0, 2, mm, 0)


def block_model(freqs, st, pix, flux, out_re, out_im, ub, vb, lb, mb, left, right):
    i, j = lax.axis_index("row"), lax.axis_index("col")
    lv, mv = lm_rows(pix[...])
    spread(lv, lb)
    spread(mv, mb)
    ub[...] = jnp.broadcast_to(st[0, pl.ds(i, 1), :], (T, T)).T
    vb[...] = jnp.broadcast_to(st[1, pl.ds(i, 1), :], (T, T)).T

    def chan(ch, _):
        f = freqs[ch]
        f0 = flux[2 * ch]
        f1 = flux[2 * ch + 1]

        def rows(g, _):
            r = pl.multiple_of(g * 16, 16)
            u = ub[pl.ds(r, 16), :] * f
            v = vb[pl.ds(r, 16), :] * f
            for k in range(8):
                c, s = cos_sin(u * lv[k:k + 1, :] + v * mv[k:k + 1, :])
                lo, hi = k * T, (k + 1) * T
                for p, fx in enumerate((f0, f1)):
                    w = fx[k:k + 1, :]
                    rr = pl.multiple_of(r + p * T, 16)
                    left[pl.ds(rr, 16), lo:hi] = (c * w).astype(BF16)
                    left[pl.ds(rr, 16), 1024 + lo:1024 + hi] = (s * w).astype(BF16)
            return 0

        lax.fori_loop(0, 8, rows, 0)

        def cols(g, _):
            r = pl.multiple_of(g * 16, 16)
            lk = lb[pl.ds(r, 16), :]
            mk = mb[pl.ds(r, 16), :]
            for q in range(4):
                u = st[0, pl.ds(4 * j + q, 1), :] * f
                v = st[1, pl.ds(4 * j + q, 1), :] * f
                c, s = cos_sin(lk * u + mk * v)
                cb = c.astype(BF16)
                lanes = slice(q * T, (q + 1) * T)
                right[pl.ds(r, 16), lanes] = cb
                right[pl.ds(pl.multiple_of(r + 1024, 16), 16), lanes] = s.astype(BF16)
                right[pl.ds(pl.multiple_of(r + 2048, 16), 16), lanes] = -cb
            return 0

        lax.fori_loop(0, 64, cols, 0)
        for n in range(2):
            lanes = slice(n * 256, (n + 1) * 256)
            re = dot(left[...], right[0:2048, lanes], ((1,), (0,)))
            im = dot(left[...], right[1024:3072, lanes], ((1,), (0,)))
            for p in range(2):
                out_re[2 * ch + p, :, lanes] = re[p * T:(p + 1) * T]
                out_im[2 * ch + p, :, lanes] = im[p * T:(p + 1) * T]
        return 0

    lax.fori_loop(0, 4, chan, 0)


def pack(vis, out):
    i, j = lax.axis_index("row"), lax.axis_index("col")
    r, half = i % 4, i // 4
    off = jnp.where((half == 1) & (j == 0), 1, 0)

    def block(z, n):
        lane = pl.multiple_of(((r + n) % 4) * T, T)
        return vis[z, 0, :, pl.ds(lane, T)]

    for z in range(2):
        out[0, z, 0:T, :] = block(z, off)
        out[0, z, T:2 * T, :] = block(z, off + 1)

    @pl.when(r < 2)
    def _():
        for z in range(2):
            out[0, z, 2 * T:, :] = block(z, 2)[0:64]

    @pl.when(r >= 2)
    def _():
        for z in range(2):
            turned = block(z, 2).T[64:T]
            out[0, z, 2 * T:, :] = -turned if z else turned


def gain_solve(flags, near, far, m_re, m_im, out, cc, halves, diag):
    cp, j = lax.axis_index("row"), lax.axis_index("col")
    w = flags[pl.ds(cp // 2, 1), :].astype(F32)
    eye = lax.broadcasted_iota(jnp.int32, (T, T), 0) == lax.broadcasted_iota(jnp.int32, (T, T), 1)

    def products(row, col, vr, vi):
        rs = pl.ds(pl.multiple_of(row * T, T), T)
        cs = pl.ds(pl.multiple_of(col * T, T), T)
        mr = m_re[rs, cs]
        mi = m_im[rs, cs]
        return vr * mr + vi * mi, vr * mi - vi * mr, mr * mr + mi * mi

    def put(row, col, parts):
        cs = pl.ds(pl.multiple_of(col * T, T), T)
        for n, part in enumerate(parts):
            cc[pl.ds(pl.multiple_of(n * 1024 + row * T, T), T), cs] = part.astype(BF16)

    def fill(row, col, vr, vi):
        put(row, col, products(row, col, vr, vi))
        put(col, row, products(col, row, vr.T, -vi.T))

    for buf, jj in ((near, j), (far, 1 - j)):
        side = 0 if buf is near else 1

        def diagonal(r, _):
            a = 4 * jj + r
            parts = products(a, a, buf[a, 0, 0:T, :], buf[a, 1, 0:T, :])
            for n, part in enumerate(parts):
                diag[pl.ds(8 * n + a, 1), :] = jnp.sum(jnp.where(eye, part, 0.0), axis=0, keepdims=True)
            put(a, a, [jnp.where(eye, 0.0, part) for part in parts])
            fill(a, 4 * jj + (r + 1) % 4, buf[a, 0, T:2 * T, :], buf[a, 1, T:2 * T, :])
            for z in range(2):
                halves[z, 2 * side + r % 2, pl.ds(pl.multiple_of((r // 2) * 64, 64), 64), :] = buf[a, z, 2 * T:, :]
            return 0

        lax.fori_loop(0, 4, diagonal, 0)

        def across(p, _):
            fill(4 * jj + p, 4 * jj + p + 2, halves[0, 2 * side + p], halves[1, 2 * side + p])
            return 0

        lax.fori_loop(0, 2, across, 0)
        off = jnp.where(jj == 0, 1, 0)

        def outer(r, _):
            a = 4 * (1 - jj) + r
            fill(a, 4 * jj + (r + off) % 4, buf[a, 0, 0:T, :], buf[a, 1, 0:T, :])
            fill(a, 4 * jj + (r + off + 1) % 4, buf[a, 0, T:2 * T, :], buf[a, 1, T:2 * T, :])
            return 0

        lax.fori_loop(0, 4, outer, 0)

    def row_of(n):
        return jnp.concatenate([diag[8 * n + t:8 * n + t + 1, :] for t in range(8)], 1)

    d_re, d_im, d_den = row_of(0), row_of(1), row_of(2)
    sub = lax.broadcasted_iota(jnp.int32, (16, 1024), 0)

    def split(x):
        return x, x - x.astype(BF16).astype(F32)

    def stack(*rows):
        out = jnp.zeros((16, 1024), F32)
        for n, x in rows:
            out = jnp.where(sub == n, x, out)
        return out

    def one(step, carry):
        g_re, g_im = carry
        hr, hr_lo = split(w * g_re)
        hi, hi_lo = split(w * g_im)
        hd, hd_lo = split(w * (g_re * g_re + g_im * g_im))
        left = jnp.concatenate(
            [
                stack((0, hr), (1, hi), (3, hr_lo), (4, hi_lo)),
                stack((0, -hi), (1, hr), (3, -hi_lo), (4, hr_lo)),
                stack((2, hd), (5, hd_lo)),
            ],
            1,
        ).astype(BF16)
        sums = dot(left, cc[...], ((1,), (0,)))
        num_re = sums[0:1] + sums[3:4] + (hr * d_re - hi * d_im)
        num_im = sums[1:2] + sums[4:5] + (hr * d_im + hi * d_re)
        den = sums[2:3] + sums[5:6] + hd * d_den
        scale = w / (den + 1.0 - w)
        n_re = num_re * scale
        n_im = num_im * scale
        odd = (step % 2) == 1
        return (
            jnp.where(odd, 0.5 * (n_re + g_re), n_re),
            jnp.where(odd, 0.5 * (n_im + g_im), n_im),
        )

    g_re, g_im = lax.fori_loop(0, ITERS, one, (w, jnp.zeros((1, 1024), F32)))
    for n in range(out.shape[0]):
        out[n, 0:1, :] = g_re
        out[n, 1:2, :] = g_im


def residual(vis, m_re, m_im, gall, res, gains):
    i, j = lax.axis_index("row"), lax.axis_index("col")
    active = lax.axis_index("chan") % 2
    cp = pl.program_id(0)

    @pl.when(cp == 0)
    def _():
        for n in range(8):
            for z in range(2):
                gains[z, n // 2, n % 2:n % 2 + 1, :] = gall[2 * n + active, z:z + 1, :]

    src = 2 * cp + active

    def lanes_of(z, t):
        return gall[src, z:z + 1, pl.ds(pl.multiple_of(t * T, T), T)]

    gpr = jnp.broadcast_to(lanes_of(0, i), (T, T)).T
    gpi = jnp.broadcast_to(lanes_of(1, i), (T, T)).T
    for q in range(4):
        lanes = slice(q * T, (q + 1) * T)
        gqr = lanes_of(0, 4 * j + q)
        gqi = lanes_of(1, 4 * j + q)
        mr = m_re[0, :, lanes]
        mi = m_im[0, :, lanes]
        ar = mr * gqr + mi * gqi
        ai = mi * gqr - mr * gqi
        res[0, 0, :, lanes] = vis[0, 0, :, lanes] - (gpr * ar - gpi * ai)
        res[1, 0, :, lanes] = vis[1, 0, :, lanes] - (gpr * ai + gpi * ar)


SMEM = pl.BlockSpec(memory_space=pltpu.SMEM)
VMEM = pl.BlockSpec(memory_space=pltpu.VMEM)


def shape(*dims):
    return jax.ShapeDtypeStruct(dims, F32)


def body(rows, cols, chans, visibilities, stations, pixels, flux, freqs, flags):
    vis = visibilities.reshape(2, 8, T, 512)
    st = stations.reshape(2, 8, T)
    pix = pixels.reshape(8, T)
    fx = flux.reshape(8, 8, T)
    params = pltpu.CompilerParams(vmem_limit_bytes=VMEM_LIMIT)

    with jax.named_scope("pack"):
        packed = pl.pallas_call(
            pack,
            grid=(8,),
            out_shape=shape(8, 2, 320, T),
            in_specs=[pl.BlockSpec((2, 1, T, 512), lambda n: (0, n, 0, 0))],
            out_specs=pl.BlockSpec((1, 2, 320, T), lambda n: (n, 0, 0, 0)),
            compiler_params=params,
            cost_estimate=pl.CostEstimate(flops=1 << 20, bytes_accessed=7 << 20, transcendentals=0),
        )(vis)
    with jax.named_scope("to_the_rows"):
        near = lax.all_to_all(packed, "row", 0, 0, tiled=True)

    with jax.named_scope("own_model"):
        m_re, m_im = pl.pallas_call(
            own_model,
            out_shape=(shape(1024, 1024), shape(1024, 1024)),
            in_specs=[SMEM, VMEM, VMEM, VMEM],
            out_specs=(VMEM, VMEM),
            scratch_shapes=[
                pltpu.VMEM((1024, T), F32),
                pltpu.VMEM((1024, T), F32),
                pltpu.VMEM((1024, 2048), BF16),
                pltpu.VMEM((1024, 3072), BF16),
            ],
            compiler_params=params,
            cost_estimate=pl.CostEstimate(flops=8 << 30, bytes_accessed=8 << 20, transcendentals=2 << 20),
        )(freqs, st, pix, fx)
    near, m_re, m_im = lax.optimization_barrier((near, m_re, m_im))

    with jax.named_scope("to_the_active_column"):
        pairs = []
        for z in range(chans):
            for r in range(rows):
                to = z % 2
                pairs.append((((r * cols) + 1 - to) * chans + z, ((r * cols) + to) * chans + z))
        far = lax.ppermute(near, ("row", "col", "chan"), pairs)

    with jax.named_scope("block_model"):
        b_re, b_im = pl.pallas_call(
            block_model,
            out_shape=(shape(8, T, 512), shape(8, T, 512)),
            in_specs=[SMEM, VMEM, VMEM, VMEM],
            out_specs=(VMEM, VMEM),
            scratch_shapes=[
                pltpu.VMEM((T, T), F32),
                pltpu.VMEM((T, T), F32),
                pltpu.VMEM((1024, T), F32),
                pltpu.VMEM((1024, T), F32),
                pltpu.VMEM((256, 2048), BF16),
                pltpu.VMEM((3072, 512), BF16),
            ],
            compiler_params=params,
            cost_estimate=pl.CostEstimate(flops=4 << 30, bytes_accessed=4 << 20, transcendentals=5 << 20),
        )(freqs, st, pix, fx)
    far, b_re, b_im = lax.optimization_barrier((far, b_re, b_im))

    with jax.named_scope("gain_solve"):
        g = pl.pallas_call(
            gain_solve,
            out_shape=shape(rows * cols, 2, 1024),
            in_specs=[VMEM] * 5,
            out_specs=VMEM,
            scratch_shapes=[
                pltpu.VMEM((3072, 1024), BF16),
                pltpu.VMEM((2, 4, T, T), F32),
                pltpu.VMEM((24, T), F32),
            ],
            compiler_params=params,
            cost_estimate=pl.CostEstimate(flops=800 << 20, bytes_accessed=14 << 20, transcendentals=0),
        )(flags, near, far, m_re, m_im)

    with jax.named_scope("gather_gains"):
        gall = lax.all_to_all(g, ("row", "col"), 0, 0, tiled=True)

    with jax.named_scope("residual"):
        res, gains = pl.pallas_call(
            residual,
            grid=(8,),
            out_shape=(shape(2, 8, T, 512), shape(2, 4, 2, 1024)),
            in_specs=[
                pl.BlockSpec((2, 1, T, 512), lambda n: (0, n, 0, 0)),
                pl.BlockSpec((1, T, 512), lambda n: (n, 0, 0)),
                pl.BlockSpec((1, T, 512), lambda n: (n, 0, 0)),
                VMEM,
            ],
            out_specs=(
                pl.BlockSpec((2, 1, T, 512), lambda n: (0, n, 0, 0)),
                pl.BlockSpec((2, 4, 2, 1024), lambda n: (0, 0, 0, 0)),
            ),
            compiler_params=params,
            cost_estimate=pl.CostEstimate(flops=32 << 20, bytes_accessed=12 << 20, transcendentals=0),
        )(vis, b_re, b_im, gall)
    return gains, res.reshape(2, 4, 2, T, 512)


def solution(mesh):
    in_specs = (
        P(None, "chan", None, "row", "col"),
        P(None, "chan"),
        P("chan"),
        P("chan", None, None),
        P("chan"),
        P("chan", None),
    )
    out_specs = (P(None, "chan", None, None), P(None, "chan", None, "row", "col"))
    run = functools.partial(body, mesh.shape["row"], mesh.shape["col"], mesh.shape["chan"])
    return jax.shard_map(run, mesh=mesh, in_specs=in_specs, out_specs=out_specs, check_vma=False)
```

time: 869 us -> 126 us (0.14)
  waiting for transfers between devices: 741 us -> 25.3 us
  other arithmetic: 84 us -> 0 us
  Pallas kernels: 0 us -> 70.9 us
  between operations: 17.8 us -> 0.65 us
  blocking collectives: 0 us -> 17 us
  local copies, waits for them, and re-layouts: 19.4 us -> 2.8 us
    psum x8 -> x0, waiting for transfers between devices: 741 us -> none  [body(): lax.psum((placed_re, placed_im, placed_den), ('row', 'col'))]
    pallas_call x0 -> x5, Pallas kernels: none -> 70.9 us  [the longest x1 21.3 us: body(): pl.pallas_call(block_model, out_shape=(shape(8, T, 512), shape(8, T, 512)...]
    another operation x7 -> x0, other arithmetic: 35.3 us -> none
    sub x10 -> x0, other arithmetic: 17.9 us -> none  [the longest x7 13.3 us: partial_sums(): z_re = gre * m_re - gim * m_im]
    all_to_all x0 -> x1, blocking collectives: none -> 17 us  [body(): gall = lax.all_to_all(g, ('row', 'col'), 0, 0, tiled=True)]
    all_to_all x0 -> x1, waiting for transfers between devices: none -> 14.3 us  [body(): near = lax.all_to_all(packed, 'row', 0, 0, tiled=True)]
    reduce_sum x9 -> x0, other arithmetic: 11.8 us -> none  [the longest x8 10.5 us: partial_sums(): num_re = jnp.sum(weight * (vis_re * z_re + vis_im * z_im), axis=2)]
    ppermute x0 -> x1, waiting for transfers between devices: none -> 11 us  [body(): far = lax.ppermute(near, ('row', 'col', 'chan'), pairs)]
  transfers between devices with their start and end apart: 8 -> 2, of which waited for: 8 -> 2; matrix products, arithmetic and copies ran while one was open for 0% -> 1% of each run, Pallas kernels for 0% -> 32%
where the time goes in v1:
time: 126 us; the launch traced here: 125 us
  Pallas kernels  70.9 us (56%)
  waiting for transfers between devices  25.3 us (20%)
  blocking collectives  17 us (13%)
  starting transfers between devices  8.68 us (7%)
  local copies, waits for them, and re-layouts  2.8 us (2%)
    pallas_call x1, Pallas kernels, body(): pl.pallas_call(block_model, out_shape=(shape(8, T, 512), shape(8, T, 512)...  21.3 us
    pallas_call x1, Pallas kernels, body(): pl.pallas_call(own_model, out_shape=(shape(1024, 1024), shape(1024, 1024)...  18.5 us
    all_to_all x1, blocking collectives, body(): gall = lax.all_to_all(g, ('row', 'col'), 0, 0, tiled=True)  17 us
    pallas_call x1, Pallas kernels, body(): pl.pallas_call(gain_solve, out_shape=shape(rows * cols, 2, 1024), in_spec...  16.8 us
    all_to_all x1, waiting for transfers between devices, body(): near = lax.all_to_all(packed, 'row', 0, 0, tiled=True)  14.3 us
    ppermute x1, waiting for transfers between devices, body(): far = lax.ppermute(near, ('row', 'col', 'chan'), pairs)  11 us
    pallas_call x1, Pallas kernels, body(): pl.pallas_call(residual, grid=(8,), out_shape=(shape(2, 8, T, 512), shape...  7.93 us
    all_to_all x1, starting transfers between devices, body(): near = lax.all_to_all(packed, 'row', 0, 0, tiled=True)  7.39 us
  transfers between devices with their start and end apart: 2, of which 2 were waited for; matrix products, arithmetic and copies ran while one was open for 1% of the time, Pallas kernels for 32%

profile of v1, /device:TPU:32, one launch (start us, length us, event | category | flops | bytes accessed | tf_op | source)
XLA Modules:
  0.0 125.3 jit_solution(7884906257489110902)
XLA Ops:
  0.6 6.4 %pack.1 = f32[8,2,320,128]{3,2,1,0:T(8,128)} custom-call(f32[2,8,128,512]{3,2,1,0:T(8,128)} %bitcast.7), custom_call_target="tpu_custom_call" | custom-call | flops 1048576 | bytes 7340032 | tf_op jit(solution)/shard_map/pack/pallas_call | solution.py:319
  7.0 0.0 copy-start.3
  7.0 0.0 copy-start.2
  7.0 7.4 %all-to-all-start = ((f32[8,2,320,128]{3,2,1,0:T(8,128)}), f32[8,2,320,128]{3,2,1,0:T(8,128)S(1)}, u32[]{:S(2)}, u32[]{:S(2)}) async-start(f32[8,2,320,128]{3,2,1,0:T(8,128)} %pack.1), calls=%async_computation | async-start | bytes 5242880 | tf_op jit(solution)/shard_map/to_the_rows/all_to_all | solution.py:329
  14.4 0.0 copy-done.3
  14.4 0.6 copy.10
  15.0 0.0 copy-done.2
  15.0 0.6 reshape.22.flux
  15.6 18.5 %own_model.1 = (f32[1024,1024]{1,0:T(8,128)}, f32[1024,1024]{1,0:T(8,128)}) custom-call(f32[4]{0:T(128)} %freqs.3, f32[2,8,128]{2,1,0:T(8,128)} %bitcast.10, s32[8,128]{1,0:T(8,128)} %bitcast.13, f32[8,8,128]{2,1,0:T(8,128)} %reshape.22.flux), custom_call_target="tpu_custom_call" | custom-call | flops 8589934592 | bytes 8388608 | tf_op jit(solution)/shard_map/own_model/pallas_call | solution.py:332
  34.1 14.3 %all-to-all-done.near = f32[8,2,320,128]{3,2,1,0:T(8,128)S(1)} async-done(((f32[8,2,320,128]{3,2,1,0:T(8,128)}), f32[8,2,320,128]{3,2,1,0:T(8,128)S(1)}, u32[]{:S(2)}, u32[]{:S(2)}) %all-to-all-start) | async-done | bytes 2621472 | tf_op jit(solution)/shard_map/to_the_rows/all_to_all | solution.py:329
  48.4 0.0 copy-start
  48.4 1.3 %collective-permute-start = (f32[8,2,320,128]{3,2,1,0:T(8,128)S(1)}, f32[8,2,320,128]{3,2,1,0:T(8,128)S(1)}, u32[]{:S(2)}, u32[]{:S(2)}) collective-permute-start(f32[8,2,320,128]{3,2,1,0:T(8,128)S(1)} %all-to-all-done.near), channel_id=1, source_target_pairs={{16,0},{48,32},{80,64},{112,96},{144,128},{176,160},{208,192},{240... | collective-permute-start | bytes 7864328 | tf_op jit(solution)/shard_map/to_the_active_column/ppermute | solution.py:354
  49.7 21.3 %block_model.1 = (f32[8,128,512]{2,1,0:T(8,128)}, f32[8,128,512]{2,1,0:T(8,128)}) custom-call(f32[4]{0:T(128)} %freqs.3, f32[2,8,128]{2,1,0:T(8,128)} %bitcast.11, s32[8,128]{1,0:T(8,128)} %bitcast.14, f32[8,8,128]{2,1,0:T(8,128)} %reshape.22.flux), custom_call_target="tpu_custom_call" | custom-call | flops 4294967296 | bytes 4194304 | tf_op jit(solution)/shard_map/block_model/pallas_call | solution.py:357
  71.0 0.0 copy-done
  71.0 11.0 %collective-permute-done.far = f32[8,2,320,128]{3,2,1,0:T(8,128)S(1)} collective-permute-done((f32[8,2,320,128]{3,2,1,0:T(8,128)S(1)}, f32[8,2,320,128]{3,2,1,0:T(8,128)S(1)}, u32[]{:S(2)}, u32[]{:S(2)}) %collective-permute-start) | collective-permute-done | bytes 2621472 | tf_op jit(solution)/shard_map/to_the_active_column/ppermute | solution.py:354
  82.0 0.0 copy-start.1
  82.0 1.5 %copy-done.1 = f32[8,2,320,128]{3,2,1,0:T(8,128)} copy-done((f32[8,2,320,128]{3,2,1,0:T(8,128)}, f32[8,2,320,128]{3,2,1,0:T(8,128)S(1)}, u32[]{:S(2)}) %copy-start.1) | copy-done | bytes 2621464
  83.5 16.8 %gain_solve.1 = f32[16,2,1024]{2,1,0:T(2,128)} custom-call(s32[4,1024]{1,0:T(4,128)} %flags.1, f32[8,2,320,128]{3,2,1,0:T(8,128)} %copy-done, f32[8,2,320,128]{3,2,1,0:T(8,128)} %copy-done.1, f32[1024,1024]{1,0:T(8,128)} %get-tuple-element.22.m_re, f32[1024,1024]{1,0:T(8,128)} %get-tuple-element.23.m_im), custom_call_target="tpu_custom_call" | custom-call | flops 838860800 | bytes 14680064 | tf_op jit(solution)/shard_map/gain_solve/pallas_call | solution.py:376
  100.4 17.0 %all_to_all.10.gall = f32[16,2,1024]{2,1,0:T(2,128)} all-to-all(f32[16,2,1024]{2,1,0:T(2,128)} %gain_solve.1), channel_id=1, replica_groups=mesh['row'=8,'col'=2,'chan'=16] {'row','col'}, dimensions={0} | all-to-all | bytes 262144 | tf_op jit(solution)/shard_map/gather_gains/all_to_all | solution.py:391
  117.3 7.9 %residual.1 = (f32[2,8,128,512]{3,2,1,0:T(8,128)}, f32[2,4,2,1024]{3,2,1,0:T(2,128)}) custom-call(f32[2,8,128,512]{3,2,1,0:T(8,128)} %bitcast.8, f32[8,128,512]{2,1,0:T(8,128)} %get-tuple-element.19.m_re, f32[8,128,512]{2,1,0:T(8,128)} %get-tuple-element.20.m_im, f32[16,2,1024]{2,1,0:T(2,128)} %all_to_all.10.gall), custom_call_target="tpu_custom_call" | custom-call | flops 33554432 | bytes 12582912 | tf_op jit(solution)/shard_map/residual/pallas_call | solution.py:394
Async XLA Ops:
  7.0 7.4 %copy-start.3 = (f32[2,1024]{1,0:T(2,128)S(1)}, f32[2,1024]{1,0:T(2,128)}, u32[]{:S(2)}) copy-start(f32[2,1024]{1,0:T(2,128)} %param.7) | copy-start | bytes 24580
  7.0 8.0 %copy-start.2 = (f32[4,2,1024]{2,1,0:T(2,128)S(1)}, f32[4,2,1024]{2,1,0:T(2,128)}, u32[]{:S(2)}) copy-start(f32[4,2,1024]{2,1,0:T(2,128)} %param.9) | copy-start | bytes 98308
  7.0 41.5 %all-to-all-start = ((f32[8,2,320,128]{3,2,1,0:T(8,128)}), f32[8,2,320,128]{3,2,1,0:T(8,128)S(1)}, u32[]{:S(2)}, u32[]{:S(2)}) async-start(f32[8,2,320,128]{3,2,1,0:T(8,128)} %pack.1), calls=%async_computation | async-start | bytes 5242880 | tf_op jit(solution)/shard_map/to_the_rows/all_to_all | solution.py:329
  48.4 22.6 %copy-start = (f32[8,2,320,128]{3,2,1,0:T(8,128)}, f32[8,2,320,128]{3,2,1,0:T(8,128)S(1)}, u32[]{:S(2)}) copy-start(f32[8,2,320,128]{3,2,1,0:T(8,128)S(1)} %all-to-all-done.near) | copy-start | bytes 7864324
  48.4 33.5 %collective-permute-start = (f32[8,2,320,128]{3,2,1,0:T(8,128)S(1)}, f32[8,2,320,128]{3,2,1,0:T(8,128)S(1)}, u32[]{:S(2)}, u32[]{:S(2)}) collective-permute-start(f32[8,2,320,128]{3,2,1,0:T(8,128)S(1)} %all-to-all-done.near), channel_id=1, source_target_pairs={{16,0},{48,32},{80,64},{112,96},{144,128},{176,160},{208,192},{240... | collective-permute-start | bytes 7864328 | tf_op jit(solution)/shard_map/to_the_active_column/ppermute | solution.py:354
  82.0 1.5 %copy-start.1 = (f32[8,2,320,128]{3,2,1,0:T(8,128)}, f32[8,2,320,128]{3,2,1,0:T(8,128)S(1)}, u32[]{:S(2)}) copy-start(f32[8,2,320,128]{3,2,1,0:T(8,128)S(1)} %collective-permute-done.far) | copy-start | bytes 7864324

commit v2 on v1

v2 whole, which is shorter than its diff:
```python
import functools

import jax
import jax.numpy as jnp
from jax import lax
from jax.experimental import pallas as pl
from jax.experimental.pallas import tpu as pltpu
from jax.sharding import PartitionSpec as P

ITERS = 8
SIDE = 1024
T = 128

SIN = (4.442867982256445, -7.307445413087933, 3.5948021037170865, -0.7844036262695797)
COS = (1.4142134965650144, -6.978850988238961, 5.739461170681741, -1.8835629873024078, 0.3106981918128224)
MAGIC = 12582912.0
F32 = jnp.float32
BF16 = jnp.bfloat16
HALF = 160


def poly(y, coeffs):
    out = coeffs[-1]
    for c in reversed(coeffs[:-1]):
        out = out * y + c
    return out


def cos_sin(turns):
    r = turns - ((turns + MAGIC) - MAGIC)
    y = r * r
    s = r * poly(y, SIN)
    c = poly(y, COS)
    return 1.0 - s * s, s * c


def lm_rows(pix):
    across = (pix & (SIDE - 1)).astype(F32)
    down = (pix >> 10).astype(F32)
    lv = (across + 0.5) / SIDE * 0.5 - 0.25
    mv = (down + 0.5) / SIDE * 0.5 - 0.25
    return lv, mv


def spread(rows, out_ref):
    for t in range(8):
        out_ref[t * T:(t + 1) * T, :] = jnp.broadcast_to(rows[t:t + 1, :], (T, T)).T


def dot(a, b, dims):
    return lax.dot_general(a, b, (dims, ((), ())), preferred_element_type=F32)


def own_model(freqs, st, pix, flux, own_re, own_im, ub, vb, left, right, oo, sem):
    i = lax.axis_index("row")

    @pl.when(lax.axis_index("col") == lax.axis_index("chan") % 2)
    def _():
        f = freqs[i // 2]
        lv, mv = lm_rows(pix[...])
        spread(st[0] * f, ub)
        spread(st[1] * f, vb)
        fx = flux[i]

        def waves(g, _):
            r = pl.multiple_of(g * 16, 16)
            u = ub[pl.ds(r, 16), :]
            v = vb[pl.ds(r, 16), :]
            for k in range(8):
                c, s = cos_sin(u * lv[k:k + 1, :] + v * mv[k:k + 1, :])
                w = fx[k:k + 1, :]
                lo, hi = k * T, (k + 1) * T
                left[pl.ds(r, 16), lo:hi] = (c * w).astype(BF16)
                left[pl.ds(r, 16), 1024 + lo:1024 + hi] = (s * w).astype(BF16)
                cb = c.astype(BF16)
                right[pl.ds(r, 16), lo:hi] = cb
                right[pl.ds(r, 16), 1024 + lo:1024 + hi] = s.astype(BF16)
                right[pl.ds(r, 16), 2048 + lo:2048 + hi] = -cb
            return 0

        lax.fori_loop(0, 64, waves, 0)

        def copies(m):
            rs = pl.ds(pl.multiple_of(m * 256, 256), 256)
            return [pltpu.make_async_copy(oo.at[z, rs], (own_re, own_im)[z].at[rs], sem.at[z, m]) for z in range(2)]

        def rows(m, _):
            rs = pl.ds(pl.multiple_of(m * 256, 256), 256)
            for n in range(2):
                cs = slice(n * 512, (n + 1) * 512)
                for z in range(2):
                    oo[z, rs, cs] = dot(left[rs, :], right[cs, z * 1024:z * 1024 + 2048], ((1,), (1,)))
            for copy in copies(m):
                copy.start()
            return 0

        lax.fori_loop(0, 4, rows, 0)
        for m in range(4):
            for copy in copies(m):
                copy.wait()


def block_model(freqs, st, pix, flux, blk_re, blk_im, rub, rvb, lb, mb, left, right, bo, sem):
    i, j = lax.axis_index("row"), lax.axis_index("col")
    lv, mv = lm_rows(pix[...])
    spread(lv, lb)
    spread(mv, mb)
    rub[...] = jnp.broadcast_to(st[0, pl.ds(i, 1), :], (T, T)).T
    rvb[...] = jnp.broadcast_to(st[1, pl.ds(i, 1), :], (T, T)).T

    def copies(ch):
        rs = pl.ds(2 * ch, 2)
        return [pltpu.make_async_copy(bo.at[z, rs], (blk_re, blk_im)[z].at[rs], sem.at[z, ch]) for z in range(2)]

    def chan(ch, _):
        f = freqs[ch]
        fluxes = [flux[2 * ch + p] for p in range(2)]
        us = [st[0, pl.ds(4 * j + q, 1), :] * f for q in range(4)]
        vs = [st[1, pl.ds(4 * j + q, 1), :] * f for q in range(4)]

        def rows(g, _):
            r = pl.multiple_of(g * 16, 16)
            u = rub[pl.ds(r, 16), :] * f
            v = rvb[pl.ds(r, 16), :] * f
            for k in range(8):
                c, s = cos_sin(u * lv[k:k + 1, :] + v * mv[k:k + 1, :])
                lo, hi = k * T, (k + 1) * T
                for p in range(2):
                    w = fluxes[p][k:k + 1, :]
                    rs = pl.ds(pl.multiple_of(r + p * T, 16), 16)
                    left[rs, lo:hi] = (c * w).astype(BF16)
                    left[rs, 1024 + lo:1024 + hi] = (s * w).astype(BF16)
            return 0

        lax.fori_loop(0, 8, rows, 0)

        def cols(g, _):
            r = pl.multiple_of(g * 16, 16)
            lk = lb[pl.ds(r, 16), :]
            mk = mb[pl.ds(r, 16), :]
            for q in range(4):
                c, s = cos_sin(lk * us[q] + mk * vs[q])
                cb = c.astype(BF16)
                lanes = slice(q * T, (q + 1) * T)
                right[pl.ds(r, 16), lanes] = cb
                right[pl.ds(pl.multiple_of(r + 1024, 16), 16), lanes] = s.astype(BF16)
                right[pl.ds(pl.multiple_of(r + 2048, 16), 16), lanes] = -cb
            return 0

        lax.fori_loop(0, 64, cols, 0, unroll=2)
        for n in range(2):
            lanes = slice(n * 256, (n + 1) * 256)
            for z in range(2):
                out = dot(left[...], right[z * 1024:z * 1024 + 2048, lanes], ((1,), (0,)))
                for p in range(2):
                    bo[z, 2 * ch + p, :, lanes] = out[p * T:(p + 1) * T]
        for copy in copies(ch):
            copy.start()
        return 0

    lax.fori_loop(0, 4, chan, 0)
    for ch in range(4):
        for copy in copies(ch):
            copy.wait()


def pack(vis, packed, vin, chunk, in_sem, one_sem, two_sem):
    i, j = lax.axis_index("row"), lax.axis_index("col")
    r, half = i % 4, i // 4
    off = jnp.where((half == 1) & (j == 0), 1, 0)
    turn = jnp.where(j == lax.axis_index("chan") % 2, 0, 4)
    loads = [pltpu.make_async_copy(vis.at[:, k], vin.at[k], in_sem.at[k]) for k in range(8)]
    stores = []
    for k in range(8):
        stores.append(pltpu.make_async_copy(chunk.at[k, :, 0:HALF], packed.at[k, :, 0:HALF], one_sem.at[k]))
        stores.append(pltpu.make_async_copy(chunk.at[k, :, HALF:], packed.at[(k + turn) % 8, :, HALF:], two_sem.at[k]))
    for load in loads:
        load.start()
    for k in range(8):
        loads[k].wait()

        def block(z, n):
            lane = pl.multiple_of(((r + n) % 4) * T, T)
            return vin[k, z, :, pl.ds(lane, T)]

        for z in range(2):
            chunk[k, z, 0:T, :] = block(z, off)
            chunk[k, z, T:2 * T, :] = block(z, off + 1)
            third = block(z, 2)
            turned = third.T[64:T]
            chunk[k, z, 2 * T:, :] = jnp.where(r < 2, third[0:64], -turned if z else turned)
        stores[2 * k].start()
        stores[2 * k + 1].start()
    for store in stores:
        store.wait()


def gain_solve(flags_in, near_in, far1, far2, re_in, im_in, out,
               flags, near, far, m_re, m_im, cc, halves, diag, sem):
    cp, j = lax.axis_index("row"), lax.axis_index("col")
    active = lax.axis_index("chan") % 2

    @pl.when(j == active)
    def _():
        first = [
            pltpu.make_async_copy(flags_in, flags, sem.at[0]),
            pltpu.make_async_copy(near_in, near, sem.at[1]),
            pltpu.make_async_copy(re_in, m_re, sem.at[2]),
            pltpu.make_async_copy(im_in, m_im, sem.at[3]),
        ]
        second = [
            pltpu.make_async_copy(far1, far.at[:, :, 0:HALF], sem.at[4]),
            pltpu.make_async_copy(far2, far.at[:, :, HALF:], sem.at[5]),
        ]
        for copy in first + second:
            copy.start()
        solve(cp, j, flags, near, far, m_re, m_im, out, cc, halves, diag, first, second)

    @pl.when(j != active)
    def _():
        out[...] = jnp.zeros_like(out)


def solve(cp, j, flags, near, far, m_re, m_im, out, cc, halves, diag, first, second):
    eye = lax.broadcasted_iota(jnp.int32, (T, T), 0) == lax.broadcasted_iota(jnp.int32, (T, T), 1)

    def products(row, col, vr, vi):
        rs = pl.ds(pl.multiple_of(row * T, T), T)
        cs = pl.ds(pl.multiple_of(col * T, T), T)
        mr = m_re[rs, cs]
        mi = m_im[rs, cs]
        return vr * mr + vi * mi, vr * mi - vi * mr, mr * mr + mi * mi

    def put(row, col, parts):
        cs = pl.ds(pl.multiple_of(col * T, T), T)
        for n, part in enumerate(parts):
            cc[pl.ds(pl.multiple_of(n * 1024 + row * T, T), T), cs] = part.astype(BF16)

    def fill(row, col, vr, vi):
        put(row, col, products(row, col, vr, vi))
        put(col, row, products(col, row, vr.T, -vi.T))

    for buf, jj in ((near, j), (far, 1 - j)):
        side = 0 if buf is near else 1
        for copy in second if side else first:
            copy.wait()

        def diagonal(r, _):
            a = 4 * jj + r
            parts = products(a, a, buf[a, 0, 0:T, :], buf[a, 1, 0:T, :])
            for n, part in enumerate(parts):
                diag[pl.ds(8 * n + a, 1), :] = jnp.sum(jnp.where(eye, part, 0.0), axis=0, keepdims=True)
            put(a, a, [jnp.where(eye, 0.0, part) for part in parts])
            fill(a, 4 * jj + (r + 1) % 4, buf[a, 0, T:2 * T, :], buf[a, 1, T:2 * T, :])
            for z in range(2):
                halves[z, 2 * side + r % 2, pl.ds(pl.multiple_of((r // 2) * 64, 64), 64), :] = buf[a, z, 2 * T:, :]
            return 0

        lax.fori_loop(0, 4, diagonal, 0)

        def across(p, _):
            fill(4 * jj + p, 4 * jj + p + 2, halves[0, 2 * side + p], halves[1, 2 * side + p])
            return 0

        lax.fori_loop(0, 2, across, 0)
        off = jnp.where(jj == 0, 1, 0)

        def outer(r, _):
            a = 4 * (1 - jj) + r
            fill(a, 4 * jj + (r + off) % 4, buf[a, 0, 0:T, :], buf[a, 1, 0:T, :])
            fill(a, 4 * jj + (r + off + 1) % 4, buf[a, 0, T:2 * T, :], buf[a, 1, T:2 * T, :])
            return 0

        lax.fori_loop(0, 4, outer, 0)

    w = flags[pl.ds(cp // 2, 1), :].astype(F32)

    def row_of(n):
        return jnp.concatenate([diag[8 * n + t:8 * n + t + 1, :] for t in range(8)], 1)

    d_re, d_im, d_den = row_of(0), row_of(1), row_of(2)
    sub = lax.broadcasted_iota(jnp.int32, (16, 1024), 0)

    def split(x):
        return x, x - x.astype(BF16).astype(F32)

    def stack(*rows):
        out = jnp.zeros((16, 1024), F32)
        for n, x in rows:
            out = jnp.where(sub == n, x, out)
        return out

    def one(step, carry):
        g_re, g_im = carry
        hr, hr_lo = split(w * g_re)
        hi, hi_lo = split(w * g_im)
        hd, hd_lo = split(w * (g_re * g_re + g_im * g_im))
        left = jnp.concatenate(
            [
                stack((0, hr), (1, hi), (3, hr_lo), (4, hi_lo)),
                stack((0, -hi), (1, hr), (3, -hi_lo), (4, hr_lo)),
                stack((2, hd), (5, hd_lo)),
            ],
            1,
        ).astype(BF16)
        sums = dot(left, cc[...], ((1,), (0,)))
        num_re = sums[0:1] + sums[3:4] + (hr * d_re - hi * d_im)
        num_im = sums[1:2] + sums[4:5] + (hr * d_im + hi * d_re)
        den = sums[2:3] + sums[5:6] + hd * d_den
        scale = w / (den + 1.0 - w)
        n_re = num_re * scale
        n_im = num_im * scale
        odd = (step % 2) == 1
        return (
            jnp.where(odd, 0.5 * (n_re + g_re), n_re),
            jnp.where(odd, 0.5 * (n_im + g_im), n_im),
        )

    g_re, g_im = lax.fori_loop(0, ITERS, one, (w, jnp.zeros((1, 1024), F32)))
    for n in range(out.shape[0]):
        out[n, 0:1, :] = g_re
        out[n, 1:2, :] = g_im


def residual(vis, m_re, m_im, gall, res, gains, v, mr_all, mi_all, o, v_sem, re_sem, im_sem, out_sem):
    i, j = lax.axis_index("row"), lax.axis_index("col")
    active = lax.axis_index("chan") % 2
    loads = []
    stores = []
    for cp in range(8):
        loads.append(
            [
                pltpu.make_async_copy(vis.at[:, cp], v.at[cp], v_sem.at[cp]),
                pltpu.make_async_copy(m_re.at[cp], mr_all.at[cp], re_sem.at[cp]),
                pltpu.make_async_copy(m_im.at[cp], mi_all.at[cp], im_sem.at[cp]),
            ]
        )
        stores.append(pltpu.make_async_copy(o.at[cp], res.at[:, cp], out_sem.at[cp]))
    for group in loads:
        for copy in group:
            copy.start()
    for n in range(8):
        for z in range(2):
            gains[z, n // 2, n % 2:n % 2 + 1, :] = gall[2 * n + active, z:z + 1, :]
    for cp in range(8):
        for copy in loads[cp]:
            copy.wait()
        src = 2 * cp + active

        def lanes_of(z, t):
            return gall[src, z:z + 1, pl.ds(pl.multiple_of(t * T, T), T)]

        gpr = jnp.broadcast_to(lanes_of(0, i), (T, T)).T
        gpi = jnp.broadcast_to(lanes_of(1, i), (T, T)).T
        for q in range(4):
            lanes = slice(q * T, (q + 1) * T)
            gqr = lanes_of(0, 4 * j + q)
            gqi = lanes_of(1, 4 * j + q)
            mr = mr_all[cp, :, lanes]
            mi = mi_all[cp, :, lanes]
            ar = mr * gqr + mi * gqi
            ai = mi * gqr - mr * gqi
            o[cp, 0, :, lanes] = v[cp, 0, :, lanes] - (gpr * ar - gpi * ai)
            o[cp, 1, :, lanes] = v[cp, 1, :, lanes] - (gpr * ai + gpi * ar)
        stores[cp].start()
    for store in stores:
        store.wait()


SMEM = pl.BlockSpec(memory_space=pltpu.SMEM)
VMEM = pl.BlockSpec(memory_space=pltpu.VMEM)
ANY = pl.BlockSpec(memory_space=pl.ANY)


def vmem(mib):
    return pltpu.CompilerParams(vmem_limit_bytes=mib << 20)


def shape(*dims):
    return jax.ShapeDtypeStruct(dims, F32)


def body(rows, cols, chans, visibilities, stations, pixels, flux, freqs, flags):
    vis = visibilities.reshape(2, 8, T, 512)
    st = stations.reshape(2, 8, T)
    pix = pixels.reshape(8, T)
    fx = flux.reshape(8, 8, T)

    with jax.named_scope("pack"):
        packed = pl.pallas_call(
            pack,
            out_shape=shape(8, 2, 2 * HALF, T),
            in_specs=[ANY],
            out_specs=ANY,
            scratch_shapes=[
                pltpu.VMEM((8, 2, T, 512), F32),
                pltpu.VMEM((8, 2, 2 * HALF, T), F32),
                pltpu.SemaphoreType.DMA((8,)),
                pltpu.SemaphoreType.DMA((8,)),
                pltpu.SemaphoreType.DMA((8,)),
            ],
            compiler_params=vmem(60),
            cost_estimate=pl.CostEstimate(flops=1 << 20, bytes_accessed=7 << 20, transcendentals=0),
        )(vis)
    with jax.named_scope("to_the_rows"):
        near = lax.all_to_all(packed, "row", 0, 0, tiled=True)

    with jax.named_scope("own_model"):
        m_re, m_im = pl.pallas_call(
            own_model,
            out_shape=(shape(1024, 1024),) * 2,
            in_specs=[SMEM, VMEM, VMEM, VMEM],
            out_specs=(ANY,) * 2,
            scratch_shapes=[
                pltpu.VMEM((1024, T), F32),
                pltpu.VMEM((1024, T), F32),
                pltpu.VMEM((1024, 2048), BF16),
                pltpu.VMEM((1024, 3072), BF16),
                pltpu.VMEM((2, 1024, 1024), F32),
                pltpu.SemaphoreType.DMA((2, 4)),
            ],
            compiler_params=vmem(24),
            cost_estimate=pl.CostEstimate(flops=8 << 30, bytes_accessed=8 << 20, transcendentals=8 << 20),
        )(freqs, st, pix, fx)
    with jax.named_scope("to_the_active_column"):
        near, m_re, m_im = lax.optimization_barrier((near, m_re, m_im))
        far = []
        for half, turn in enumerate((0, rows // 2)):
            pairs = []
            for z in range(chans):
                to = z % 2
                for r in range(rows):
                    src = (r * cols + 1 - to) * chans + z
                    dst = ((r + turn) % rows * cols + to) * chans + z
                    pairs.append((src, dst))
            piece = near[:, :, half * HALF:(half + 1) * HALF]
            far.append(lax.ppermute(piece, ("row", "col", "chan"), pairs))
    with jax.named_scope("block_model"):
        b_re, b_im = pl.pallas_call(
            block_model,
            out_shape=(shape(8, T, 512),) * 2,
            in_specs=[SMEM, VMEM, VMEM, VMEM],
            out_specs=(ANY,) * 2,
            scratch_shapes=[
                pltpu.VMEM((T, T), F32),
                pltpu.VMEM((T, T), F32),
                pltpu.VMEM((1024, T), F32),
                pltpu.VMEM((1024, T), F32),
                pltpu.VMEM((256, 2048), BF16),
                pltpu.VMEM((3072, 512), BF16),
                pltpu.VMEM((2, 8, T, 512), F32),
                pltpu.SemaphoreType.DMA((2, 4)),
            ],
            compiler_params=vmem(14),
            cost_estimate=pl.CostEstimate(flops=8 << 30, bytes_accessed=4 << 20, transcendentals=8 << 20),
        )(freqs, st, pix, fx)
    far[0], far[1], b_re, b_im = lax.optimization_barrier((far[0], far[1], b_re, b_im))

    with jax.named_scope("gain_solve"):
        g = pl.pallas_call(
            gain_solve,
            out_shape=shape(rows * cols, 2, 1024),
            in_specs=[ANY] * 6,
            out_specs=VMEM,
            scratch_shapes=[
                pltpu.VMEM((4, 1024), jnp.int32),
                pltpu.VMEM((8, 2, 2 * HALF, T), F32),
                pltpu.VMEM((8, 2, 2 * HALF, T), F32),
                pltpu.VMEM((1024, 1024), F32),
                pltpu.VMEM((1024, 1024), F32),
                pltpu.VMEM((3072, 1024), BF16),
                pltpu.VMEM((2, 4, T, T), F32),
                pltpu.VMEM((24, T), F32),
                pltpu.SemaphoreType.DMA((6,)),
            ],
            compiler_params=vmem(26),
            cost_estimate=pl.CostEstimate(flops=800 << 20, bytes_accessed=14 << 20, transcendentals=0),
        )(flags, near, *far, m_re, m_im)

    with jax.named_scope("gather_gains"):
        gall = lax.all_to_all(g, ("row", "col"), 0, 0, tiled=True)

    with jax.named_scope("residual"):
        res, gains = pl.pallas_call(
            residual,
            out_shape=(shape(2, 8, T, 512), shape(2, 4, 2, 1024)),
            in_specs=[ANY, ANY, ANY, VMEM],
            out_specs=(ANY, VMEM),
            scratch_shapes=[
                pltpu.VMEM((8, 2, T, 512), F32),
                pltpu.VMEM((8, T, 512), F32),
                pltpu.VMEM((8, T, 512), F32),
                pltpu.VMEM((8, 2, T, 512), F32),
            ]
            + [pltpu.SemaphoreType.DMA((8,))] * 4,
            compiler_params=vmem(18),
            cost_estimate=pl.CostEstimate(flops=32 << 20, bytes_accessed=12 << 20, transcendentals=0),
        )(vis, b_re, b_im, gall)
    return gains, res.reshape(2, 4, 2, T, 512)


def solution(mesh):
    in_specs = (
        P(None, "chan", None, "row", "col"),
        P(None, "chan"),
        P("chan"),
        P("chan", None, None),
        P("chan"),
        P("chan", None),
    )
    out_specs = (P(None, "chan", None, None), P(None, "chan", None, "row", "col"))
    run = functools.partial(body, mesh.shape["row"], mesh.shape["col"], mesh.shape["chan"])
    return jax.shard_map(run, mesh=mesh, in_specs=in_specs, out_specs=out_specs, check_vma=False)
```

time: 126 us -> 99.4 us (0.79)
  Pallas kernels: 70.9 us -> 54.3 us
  waiting for transfers between devices: 25.3 us -> 14.4 us
  local copies, waits for them, and re-layouts: 2.8 us -> 4.22 us
  blocking collectives: 17 us -> 15.7 us
    pallas_call x4, Pallas kernels: 54.1 us -> 42.1 us  [the longest x1 18.4 us: body(): pl.pallas_call(block_model, out_shape=(shape(8, T, 512),) * 2, in_specs=[...]
    ppermute x1 -> x2, waiting for transfers between devices: 11 us -> 1.02 us  [body(): far.append(lax.ppermute(piece, ('row', 'col', 'chan'), pairs))]
    pallas_call x1, Pallas kernels: 16.8 us -> 12.2 us  [body(): pl.pallas_call(gain_solve, out_shape=shape(rows * cols, 2, 1024), in_spec...]
    unnamed x9 -> x21, local copies, waits for them, and re-layouts: 2.16 us -> 4.02 us
    ppermute x1 -> x2, starting transfers between devices: 1.28 us -> 2.58 us  [body(): far.append(lax.ppermute(piece, ('row', 'col', 'chan'), pairs))]
    all_to_all x1, blocking collectives: 17 us -> 15.7 us  [body(): gall = lax.all_to_all(g, ('row', 'col'), 0, 0, tiled=True)]
  transfers between devices with their start and end apart: 2 -> 3, of which waited for: 2 -> 2; matrix products, arithmetic and copies ran while one was open for 1% -> 0% of each run, Pallas kernels for 32% -> 35%
where the time goes in v2:
time: 99.4 us; the launch traced here: 99.1 us
  Pallas kernels  54.3 us (55%)
  blocking collectives  15.7 us (16%)
  waiting for transfers between devices  14.4 us (14%)
  starting transfers between devices  9.66 us (10%)
  local copies, waits for them, and re-layouts  4.22 us (4%)
    pallas_call x1, Pallas kernels, body(): pl.pallas_call(block_model, out_shape=(shape(8, T, 512),) * 2, in_specs=[...  18.4 us
    pallas_call x1, Pallas kernels, body(): pl.pallas_call(own_model, out_shape=(shape(1024, 1024),) * 2, in_specs=[S...  16.6 us
    all_to_all x1, blocking collectives, body(): gall = lax.all_to_all(g, ('row', 'col'), 0, 0, tiled=True)  15.7 us
    all_to_all x1, waiting for transfers between devices, body(): near = lax.all_to_all(packed, 'row', 0, 0, tiled=True)  13.4 us
    pallas_call x1, Pallas kernels, body(): pl.pallas_call(gain_solve, out_shape=shape(rows * cols, 2, 1024), in_spec...  12.2 us
    all_to_all x1, starting transfers between devices, body(): near = lax.all_to_all(packed, 'row', 0, 0, tiled=True)  7.07 us
    unnamed x21, local copies, waits for them, and re-layouts  4.02 us
    pallas_call x1, Pallas kernels, body(): pl.pallas_call(residual, out_shape=(shape(2, 8, T, 512), shape(2, 4, 2, 1...  3.65 us
  transfers between devices with their start and end apart: 3, of which 2 were waited for; matrix products, arithmetic and copies ran while one was open for 0% of the time, Pallas kernels for 35%

profile of v2, /device:TPU:32, one launch (start us, length us, event | category | flops | bytes accessed | tf_op | source)
XLA Modules:
  0.0 99.1 jit_solution(1145825852048719978)
XLA Ops:
  0.6 3.5 %pack.1 = f32[8,2,320,128]{3,2,1,0:T(8,128)} custom-call(f32[2,8,128,512]{3,2,1,0:T(8,128)} %bitcast.7), custom_call_target="tpu_custom_call" | custom-call | flops 1048576 | bytes 7340032 | tf_op jit(solution)/shard_map/pack/pallas_call | solution.py:390
  4.1 0.0 copy-start.9
  4.1 0.0 copy-start.8
  4.2 0.0 copy-start.6
  4.2 0.0 copy-start.7
  4.2 7.1 %all-to-all-start = ((f32[8,2,320,128]{3,2,1,0:T(8,128)}), f32[8,2,320,128]{3,2,1,0:T(8,128)S(1)}, u32[]{:S(2)}, u32[]{:S(2)}) async-start(f32[8,2,320,128]{3,2,1,0:T(8,128)} %pack.1), calls=%async_computation | async-start | bytes 5242880 | tf_op jit(solution)/shard_map/to_the_rows/all_to_all | solution.py:406
  11.3 0.0 copy-done.9
  11.3 16.6 %own_model.1 = (f32[1024,1024]{1,0:T(8,128)S(1)}, f32[1024,1024]{1,0:T(8,128)S(1)}) custom-call(f32[4]{0:T(128)S(1)} %copy-done.7, f32[2,8,128]{2,1,0:T(8,128)S(1)} %bitcast.9, s32[8,128]{1,0:T(8,128)S(1)} %bitcast.11, f32[8,8,128]{2,1,0:T(8,128)S(1)} %reshape.22.flux), custom_call_target="tpu_custom_call" | custom-call | flops 8589934592 | bytes 8388608 | tf_op jit(solution)/shard_map/own_model/pallas_call | solution.py:409
  27.9 0.0 copy-start.1
  27.9 2.0 %copy-done.1 = f32[1024,1024]{1,0:T(8,128)} copy-done((f32[1024,1024]{1,0:T(8,128)}, f32[1024,1024]{1,0:T(8,128)S(1)}, u32[]{:S(2)}) %copy-start.1) | copy-done | bytes 4194328
  29.9 2.0 %copy-done.3 = f32[1024,1024]{1,0:T(8,128)} copy-done((f32[1024,1024]{1,0:T(8,128)}, f32[1024,1024]{1,0:T(8,128)S(1)}, u32[]{:S(2)}) %copy-start.3) | copy-done | bytes 4194328
  31.9 13.4 %all-to-all-done.near_in = f32[8,2,320,128]{3,2,1,0:T(8,128)S(1)} async-done(((f32[8,2,320,128]{3,2,1,0:T(8,128)}), f32[8,2,320,128]{3,2,1,0:T(8,128)S(1)}, u32[]{:S(2)}, u32[]{:S(2)}) %all-to-all-start) | async-done | bytes 2621472 | tf_op jit(solution)/shard_map/to_the_rows/all_to_all | solution.py:406
  45.3 0.2 fusion
  45.5 1.3 %collective-permute-start = (f32[8,2,160,128]{3,2,1,0:T(8,128)S(1)}, f32[8,2,160,128]{3,2,1,0:T(8,128)S(1)}, u32[]{:S(2)}, u32[]{:S(2)}) collective-permute-start(f32[8,2,160,128]{3,2,1,0:T(8,128)S(1)} %get-tuple-element.29), channel_id=1, source_target_pairs={{16,0},{48,32},{80,64},{112,96},{144,128},{176,160},{208,192},{240... | collective-permute-start | bytes 3932168 | tf_op jit(solution)/shard_map/to_the_active_column/ppermute | solution.py:437
  46.8 0.0 copy-start.5
  46.8 1.3 %collective-permute-start.1 = (f32[8,2,160,128]{3,2,1,0:T(8,128)S(1)}, f32[8,2,160,128]{3,2,1,0:T(8,128)S(1)}, u32[]{:S(2)}, u32[]{:S(2)}) collective-permute-start(f32[8,2,160,128]{3,2,1,0:T(8,128)S(1)} %get-tuple-element.28), channel_id=1, source_target_pairs={{16,128},{48,160},{80,192},{112,224},{144,0},{176,32},{208,64},{24... | collective-permute-start | bytes 3932168 | tf_op jit(solution)/shard_map/to_the_active_column/ppermute | solution.py:437
  48.1 0.0 copy-start.2
  48.1 18.4 %block_model.1 = (f32[8,128,512]{2,1,0:T(8,128)S(1)}, f32[8,128,512]{2,1,0:T(8,128)S(1)}) custom-call(f32[4]{0:T(128)S(1)} %copy-done.7, f32[2,8,128]{2,1,0:T(8,128)S(1)} %bitcast.10, s32[8,128]{1,0:T(8,128)S(1)} %bitcast.12, f32[8,8,128]{2,1,0:T(8,128)S(1)} %reshape.22.flux), custom_call_target="tpu_custom_call" | custom-call | flops 8589934592 | bytes 4194304 | tf_op jit(solution)/shard_map/block_model/pallas_call | solution.py:439
  66.5 0.0 collective-permute-done.far1
  66.5 1.0 %collective-permute-done.1.far2 = f32[8,2,160,128]{3,2,1,0:T(8,128)S(1)} collective-permute-done((f32[8,2,160,128]{3,2,1,0:T(8,128)S(1)}, f32[8,2,160,128]{3,2,1,0:T(8,128)S(1)}, u32[]{:S(2)}, u32[]{:S(2)}) %collective-permute-start.1) | collective-permute-done | bytes 1310752 | tf_op jit(solution)/shard_map/to_the_active_column/ppermute | solution.py:437
  67.5 0.0 copy-start
  67.5 12.2 %gain_solve.1 = f32[16,2,1024]{2,1,0:T(2,128)S(1)} custom-call(s32[4,1024]{1,0:T(4,128)S(1)} %copy-done.5, f32[8,2,320,128]{3,2,1,0:T(8,128)S(1)} %all-to-all-done.near_in, f32[8,2,160,128]{3,2,1,0:T(8,128)S(1)} %collective-permute-done.far1, f32[8,2,160,128]{3,2,1,0:T(8,128)S(1)} %collective-permute-done.1.far2, f32[1024,1024]{1,0:T(8,128)S(1)} %copy-done.2, ...), custom_call_target="tpu_custom_call" | custom-call | flops 838860800 | bytes 14680064 | tf_op jit(solution)/shard_map/gain_solve/pallas_call | solution.py:460
  79.8 15.7 %all_to_all.10.gall = f32[16,2,1024]{2,1,0:T(2,128)S(1)} all-to-all(f32[16,2,1024]{2,1,0:T(2,128)S(1)} %gain_solve.1), channel_id=1, replica_groups=mesh['row'=8,'col'=2,'chan'=16] {'row','col'}, dimensions={0} | all-to-all | bytes 262144 | tf_op jit(solution)/shard_map/gather_gains/all_to_all | solution.py:481
  95.4 3.6 %residual.1 = (f32[2,8,128,512]{3,2,1,0:T(8,128)}, f32[2,4,2,1024]{3,2,1,0:T(2,128)}) custom-call(f32[2,8,128,512]{3,2,1,0:T(8,128)S(1)} %bitcast.8, f32[8,128,512]{2,1,0:T(8,128)S(1)} %get-tuple-element.20.m_re, f32[8,128,512]{2,1,0:T(8,128)S(1)} %get-tuple-element.21.m_im, f32[16,2,1024]{2,1,0:T(2,128)S(1)} %all_to_all.10.gall), custom_call_target="tpu_custom_call" | custom-call | flops 33554432 | bytes 12582912 | tf_op jit(solution)/shard_map/residual/pallas_call | solution.py:484
  (11 shorter events, 0.0 us)
Async XLA Ops:
  4.1 7.1 %copy-start.9 = (f32[2,1024]{1,0:T(2,128)S(1)}, f32[2,1024]{1,0:T(2,128)}, u32[]{:S(2)}) copy-start(f32[2,1024]{1,0:T(2,128)} %param.7) | copy-start | bytes 24580
  4.1 7.1 %copy-start.8 = (f32[4,2,1024]{2,1,0:T(2,128)S(1)}, f32[4,2,1024]{2,1,0:T(2,128)}, u32[]{:S(2)}) copy-start(f32[4,2,1024]{2,1,0:T(2,128)} %param.9) | copy-start | bytes 98308
  4.2 7.2 %copy-start.6 = (s32[1024]{0:T(1024)S(1)}, s32[1024]{0:T(1024)}, u32[]{:S(2)}) copy-start(s32[1024]{0:T(1024)} %param.8) | copy-start | bytes 12292
  4.2 7.2 %copy-start.7 = (f32[4]{0:T(128)S(1)}, f32[4]{0:T(128)}, u32[]{:S(2)}) copy-start(f32[4]{0:T(128)} %freqs.3) | copy-start | bytes 52
  4.2 41.1 %all-to-all-start = ((f32[8,2,320,128]{3,2,1,0:T(8,128)}), f32[8,2,320,128]{3,2,1,0:T(8,128)S(1)}, u32[]{:S(2)}, u32[]{:S(2)}) async-start(f32[8,2,320,128]{3,2,1,0:T(8,128)} %pack.1), calls=%async_computation | async-start | bytes 5242880 | tf_op jit(solution)/shard_map/to_the_rows/all_to_all | solution.py:406
  27.9 2.0 %copy-start.1 = (f32[1024,1024]{1,0:T(8,128)}, f32[1024,1024]{1,0:T(8,128)S(1)}, u32[]{:S(2)}) copy-start(f32[1024,1024]{1,0:T(8,128)S(1)} %get-tuple-element.24.re_in) | copy-start | bytes 12582916
  29.9 2.0 %copy-start.3 = (f32[1024,1024]{1,0:T(8,128)}, f32[1024,1024]{1,0:T(8,128)S(1)}, u32[]{:S(2)}) copy-start(f32[1024,1024]{1,0:T(8,128)S(1)} %get-tuple-element.25.im_in) | copy-start | bytes 12582916
  45.5 21.0 %collective-permute-start = (f32[8,2,160,128]{3,2,1,0:T(8,128)S(1)}, f32[8,2,160,128]{3,2,1,0:T(8,128)S(1)}, u32[]{:S(2)}, u32[]{:S(2)}) collective-permute-start(f32[8,2,160,128]{3,2,1,0:T(8,128)S(1)} %get-tuple-element.29), channel_id=1, source_target_pairs={{16,0},{48,32},{80,64},{112,96},{144,128},{176,160},{208,192},{240... | collective-permute-start | bytes 3932168 | tf_op jit(solution)/shard_map/to_the_active_column/ppermute | solution.py:437
  46.8 20.7 %copy-start.5 = (s32[4,1024]{1,0:T(4,128)S(1)}, s32[4,1024]{1,0:T(4,128)}, u32[]{:S(2)}) copy-start(s32[4,1024]{1,0:T(4,128)} %flags_in.1) | copy-start | bytes 49156
  46.8 20.7 %collective-permute-start.1 = (f32[8,2,160,128]{3,2,1,0:T(8,128)S(1)}, f32[8,2,160,128]{3,2,1,0:T(8,128)S(1)}, u32[]{:S(2)}, u32[]{:S(2)}) collective-permute-start(f32[8,2,160,128]{3,2,1,0:T(8,128)S(1)} %get-tuple-element.28), channel_id=1, source_target_pairs={{16,128},{48,160},{80,192},{112,224},{144,0},{176,32},{208,64},{24... | collective-permute-start | bytes 3932168 | tf_op jit(solution)/shard_map/to_the_active_column/ppermute | solution.py:437
  48.1 19.4 %copy-start.2 = (f32[1024,1024]{1,0:T(8,128)S(1)}, f32[1024,1024]{1,0:T(8,128)}, u32[]{:S(2)}) copy-start(f32[1024,1024]{1,0:T(8,128)} %copy-done.1) | copy-start | bytes 12582916
  48.1 19.4 %copy-start.4 = (f32[1024,1024]{1,0:T(8,128)S(1)}, f32[1024,1024]{1,0:T(8,128)}, u32[]{:S(2)}) copy-start(f32[1024,1024]{1,0:T(8,128)} %copy-done.3) | copy-start | bytes 12582916
  67.5 27.9 %copy-start = (f32[2,4,2,128,512]{4,3,2,1,0:T(8,128)S(1)}, f32[2,4,2,128,512]{4,3,2,1,0:T(8,128)}, u32[]{:S(2)}) copy-start(f32[2,4,2,128,512]{4,3,2,1,0:T(8,128)} %param.6) | copy-start | bytes 12582916

commit v3 on v2

--- a/solution.py
+++ b/solution.py
@@ -12,11 +12,11 @@
 T = 128
 
 SIN = (4.442867982256445, -7.307445413087933, 3.5948021037170865, -0.7844036262695797)
-COS = (1.4142134965650144, -6.978850988238961, 5.739461170681741, -1.8835629873024078, 0.3106981918128224)
+COS = (1.4142040804669562, -6.977642056688731, 5.715238393830307, -1.728348659759922)
 MAGIC = 12582912.0
 F32 = jnp.float32
 BF16 = jnp.bfloat16
-HALF = 160
+ROWS = 288
 
 
 def poly(y, coeffs):
@@ -100,7 +100,7 @@
                 copy.wait()
 
 
-def block_model(freqs, st, pix, flux, blk_re, blk_im, rub, rvb, lb, mb, left, right, bo, sem):
+def block_model(first, freqs, st, pix, flux, blk_re, blk_im, rub, rvb, lb, mb, left, right, bo, sem):
     i, j = lax.axis_index("row"), lax.axis_index("col")
     lv, mv = lm_rows(pix[...])
     spread(lv, lb)
@@ -113,8 +113,8 @@
         return [pltpu.make_async_copy(bo.at[z, rs], (blk_re, blk_im)[z].at[rs], sem.at[z, ch]) for z in range(2)]
 
     def chan(ch, _):
-        f = freqs[ch]
-        fluxes = [flux[2 * ch + p] for p in range(2)]
+        f = freqs[first + ch]
+        fluxes = [flux[2 * (first + ch) + p] for p in range(2)]
         us = [st[0, pl.ds(4 * j + q, 1), :] * f for q in range(4)]
         vs = [st[1, pl.ds(4 * j + q, 1), :] * f for q in range(4)]
 
@@ -128,8 +128,10 @@
                 for p in range(2):
                     w = fluxes[p][k:k + 1, :]
                     rs = pl.ds(pl.multiple_of(r + p * T, 16), 16)
-                    left[rs, lo:hi] = (c * w).astype(BF16)
-                    left[rs, 1024 + lo:1024 + hi] = (s * w).astype(BF16)
+                    sw = (s * w).astype(BF16)
+                    left[rs, lo:hi] = -sw
+                    left[rs, 1024 + lo:1024 + hi] = (c * w).astype(BF16)
+                    left[rs, 2048 + lo:2048 + hi] = sw
             return 0
 
         lax.fori_loop(0, 8, rows, 0)
@@ -140,88 +142,118 @@
             mk = mb[pl.ds(r, 16), :]
             for q in range(4):
                 c, s = cos_sin(lk * us[q] + mk * vs[q])
-                cb = c.astype(BF16)
                 lanes = slice(q * T, (q + 1) * T)
-                right[pl.ds(r, 16), lanes] = cb
+                right[pl.ds(r, 16), lanes] = c.astype(BF16)
                 right[pl.ds(pl.multiple_of(r + 1024, 16), 16), lanes] = s.astype(BF16)
-                right[pl.ds(pl.multiple_of(r + 2048, 16), 16), lanes] = -cb
             return 0
 
         lax.fori_loop(0, 64, cols, 0, unroll=2)
         for n in range(2):
             lanes = slice(n * 256, (n + 1) * 256)
             for z in range(2):
-                out = dot(left[...], right[z * 1024:z * 1024 + 2048, lanes], ((1,), (0,)))
+                out = dot(left[:, (1 - z) * 1024:(1 - z) * 1024 + 2048], right[:, lanes], ((1,), (0,)))
                 for p in range(2):
                     bo[z, 2 * ch + p, :, lanes] = out[p * T:(p + 1) * T]
         for copy in copies(ch):
             copy.start()
         return 0
 
-    lax.fori_loop(0, 4, chan, 0)
-    for ch in range(4):
+    lax.fori_loop(0, 2, chan, 0)
+    for ch in range(2):
         for copy in copies(ch):
             copy.wait()
+
+
+DIAGONAL, SOLVING, PASSING = range(3)
 
 
 def pack(vis, packed, vin, chunk, in_sem, one_sem, two_sem):
     i, j = lax.axis_index("row"), lax.axis_index("col")
     r, half = i % 4, i // 4
-    off = jnp.where((half == 1) & (j == 0), 1, 0)
-    turn = jnp.where(j == lax.axis_index("chan") % 2, 0, 4)
+    solving = j == lax.axis_index("chan") % 2
+    turn = jnp.where(solving, 0, 4)
     loads = [pltpu.make_async_copy(vis.at[:, k], vin.at[k], in_sem.at[k]) for k in range(8)]
     stores = []
     for k in range(8):
-        stores.append(pltpu.make_async_copy(chunk.at[k, :, 0:HALF], packed.at[k, :, 0:HALF], one_sem.at[k]))
-        stores.append(pltpu.make_async_copy(chunk.at[k, :, HALF:], packed.at[(k + turn) % 8, :, HALF:], two_sem.at[k]))
+        stores.append(pltpu.make_async_copy(chunk.at[k, :, 0:T], packed.at[k, :, 0:T], one_sem.at[k]))
+        stores.append(
+            pltpu.make_async_copy(chunk.at[k, :, T:], packed.at[(k + turn) % 8, :, T:], two_sem.at[k])
+        )
     for load in loads:
         load.start()
-    for k in range(8):
-        loads[k].wait()
-
-        def block(z, n):
-            lane = pl.multiple_of(((r + n) % 4) * T, T)
-            return vin[k, z, :, pl.ds(lane, T)]
-
-        for z in range(2):
-            chunk[k, z, 0:T, :] = block(z, off)
-            chunk[k, z, T:2 * T, :] = block(z, off + 1)
-            third = block(z, 2)
-            turned = third.T[64:T]
-            chunk[k, z, 2 * T:, :] = jnp.where(r < 2, third[0:64], -turned if z else turned)
-        stores[2 * k].start()
-        stores[2 * k + 1].start()
+    left = lax.broadcasted_iota(jnp.int32, (32, T), 1) < 64
+
+    def run(place):
+        for k in range(8):
+            loads[k].wait()
+
+            def block(z, n):
+                lane = pl.multiple_of(((r + n) % 4) * T, T)
+                return vin[k, z, :, pl.ds(lane, T)]
+
+            for z in range(2):
+                if place == DIAGONAL:
+                    chunk[k, z, 0:T, :] = block(z, 1)
+                    third = block(z, 2)
+                    turned = third.T[64:T]
+                    chunk[k, z, T:T + 64, :] = jnp.where(r < 2, third[0:64], -turned if z else turned)
+                    own = block(z, 0)
+                    chunk[k, z, T + 64:2 * T, :] = own[0:64]
+                    chunk[k, z, 2 * T:, :] = jnp.where(left, pltpu.roll(own[64:96], 64, 1), own[96:T])
+                else:
+                    off = jnp.where(half == 1, 1, 0)
+                    chunk[k, z, 0:T, :] = block(z, off)
+                    second = block(z, off + 1)
+                    if place == SOLVING:
+                        chunk[k, z, T:2 * T, :] = second
+                        chunk[k, z, 2 * T:, :] = block(z, off + 2)[0:32]
+                    else:
+                        turned = second.T[32:T]
+                        chunk[k, z, T:T + 96, :] = -turned if z else turned
+                        chunk[k, z, T + 96:, :] = jnp.zeros((64, T), F32)
+            stores[2 * k].start()
+            stores[2 * k + 1].start()
+
+    @pl.when(half == j)
+    def _():
+        run(DIAGONAL)
+
+    @pl.when((half != j) & solving)
+    def _():
+        run(SOLVING)
+
+    @pl.when((half != j) & jnp.logical_not(solving))
+    def _():
+        run(PASSING)
+
     for store in stores:
         store.wait()
 
 
-def gain_solve(flags_in, near_in, far1, far2, re_in, im_in, out,
-               flags, near, far, m_re, m_im, cc, halves, diag, sem):
+def gain_solve(flags, near, far1, far2, m_re, m_im, out, cc, halves, diag):
     cp, j = lax.axis_index("row"), lax.axis_index("col")
     active = lax.axis_index("chan") % 2
 
     @pl.when(j == active)
     def _():
-        first = [
-            pltpu.make_async_copy(flags_in, flags, sem.at[0]),
-            pltpu.make_async_copy(near_in, near, sem.at[1]),
-            pltpu.make_async_copy(re_in, m_re, sem.at[2]),
-            pltpu.make_async_copy(im_in, m_im, sem.at[3]),
-        ]
-        second = [
-            pltpu.make_async_copy(far1, far.at[:, :, 0:HALF], sem.at[4]),
-            pltpu.make_async_copy(far2, far.at[:, :, HALF:], sem.at[5]),
-        ]
-        for copy in first + second:
-            copy.start()
-        solve(cp, j, flags, near, far, m_re, m_im, out, cc, halves, diag, first, second)
+        solve(cp, j, flags, near, far1, far2, m_re, m_im, out, cc, halves, diag)
 
     @pl.when(j != active)
     def _():
         out[...] = jnp.zeros_like(out)
 
 
-def solve(cp, j, flags, near, far, m_re, m_im, out, cc, halves, diag, first, second):
+def solve(cp, j, flags, near, far1, far2, m_re, m_im, out, cc, halves, diag):
+
+    def of_near(diagonal, a, z, lo, hi):
+        return near[a, z, lo:hi, :]
+
+    def of_far(diagonal, a, z, lo, hi):
+        if hi <= T:
+            return far1[a, z, lo:hi, :]
+        start = lo - T + (0 if diagonal else ROWS - T)
+        return far2[a % 4, z, start:start + hi - lo, :]
+    low = lax.broadcasted_iota(jnp.int32, (64, T), 1) < 64
     eye = lax.broadcasted_iota(jnp.int32, (T, T), 0) == lax.broadcasted_iota(jnp.int32, (T, T), 1)
 
     def products(row, col, vr, vi):
@@ -240,38 +272,52 @@
         put(row, col, products(row, col, vr, vi))
         put(col, row, products(col, row, vr.T, -vi.T))
 
-    for buf, jj in ((near, j), (far, 1 - j)):
-        side = 0 if buf is near else 1
-        for copy in second if side else first:
-            copy.wait()
-
-        def diagonal(r, _):
+    for side, (part_of, jj) in enumerate(((of_near, j), (of_far, 1 - j))):
+        off = jnp.where(jj == 0, 1, 0)
+
+        def own_block(a, z):
+            top = part_of(True, a, z, T + 64, 2 * T)
+            turned = jnp.concatenate([top, top], 0).T[64:T]
+            last = part_of(True, a, z, 2 * T, ROWS)
+            right = jnp.concatenate([pltpu.roll(last, 64, 1), last], 0)
+            return jnp.concatenate([top, jnp.where(low, -turned if z else turned, right)], 0)
+
+        def sources(r, _):
             a = 4 * jj + r
-            parts = products(a, a, buf[a, 0, 0:T, :], buf[a, 1, 0:T, :])
+            parts = products(a, a, own_block(a, 0), own_block(a, 1))
             for n, part in enumerate(parts):
                 diag[pl.ds(8 * n + a, 1), :] = jnp.sum(jnp.where(eye, part, 0.0), axis=0, keepdims=True)
             put(a, a, [jnp.where(eye, 0.0, part) for part in parts])
-            fill(a, 4 * jj + (r + 1) % 4, buf[a, 0, T:2 * T, :], buf[a, 1, T:2 * T, :])
+            fill(a, 4 * jj + (r + 1) % 4, part_of(True, a, 0, 0, T), part_of(True, a, 1, 0, T))
             for z in range(2):
-                halves[z, 2 * side + r % 2, pl.ds(pl.multiple_of((r // 2) * 64, 64), 64), :] = buf[a, z, 2 * T:, :]
+                rs = pl.ds(pl.multiple_of((r // 2) * 64, 64), 64)
+                halves[z, 2 * side + r % 2, rs, :] = part_of(True, a, z, T, T + 64)
+            b = 4 * (1 - jj) + r
+            fill(b, 4 * jj + (r + off) % 4, part_of(False, b, 0, 0, T), part_of(False, b, 1, 0, T))
+            if side == 0:
+                fill(b, 4 * jj + (r + off + 1) % 4, part_of(False, b, 0, T, 2 * T), part_of(False, b, 1, T, 2 * T))
+                for z in range(2):
+                    halves[z, 4 + r, 0:32, :] = part_of(False, b, z, 2 * T, ROWS)
+            else:
+                for z in range(2):
+                    halves[z, 4 + (r + off + 1) % 4, 32:T, :] = part_of(False, b, z, T, T + 96)
             return 0
 
-        lax.fori_loop(0, 4, diagonal, 0)
+        lax.fori_loop(0, 4, sources, 0)
 
         def across(p, _):
             fill(4 * jj + p, 4 * jj + p + 2, halves[0, 2 * side + p], halves[1, 2 * side + p])
             return 0
 
         lax.fori_loop(0, 2, across, 0)
-        off = jnp.where(jj == 0, 1, 0)
-
-        def outer(r, _):
-            a = 4 * (1 - jj) + r
-            fill(a, 4 * jj + (r + off) % 4, buf[a, 0, 0:T, :], buf[a, 1, 0:T, :])
-            fill(a, 4 * jj + (r + off + 1) % 4, buf[a, 0, T:2 * T, :], buf[a, 1, T:2 * T, :])
-            return 0
-
-        lax.fori_loop(0, 4, outer, 0)
+
+    near_off = jnp.where(j == 0, 1, 0)
+
+    def thirds(r, _):
+        fill(4 * (1 - j) + r, 4 * j + (r + near_off + 2) % 4, halves[0, 4 + r], halves[1, 4 + r])
+        return 0
+
+    lax.fori_loop(0, 4, thirds, 0)
 
     w = flags[pl.ds(cp // 2, 1), :].astype(F32)
 
@@ -322,29 +368,15 @@
         out[n, 1:2, :] = g_im
 
 
-def residual(vis, m_re, m_im, gall, res, gains, v, mr_all, mi_all, o, v_sem, re_sem, im_sem, out_sem):
+def residual(vis, re_early, im_early, re_late, im_late, gall, res, gains, o, out_sem):
     i, j = lax.axis_index("row"), lax.axis_index("col")
     active = lax.axis_index("chan") % 2
-    loads = []
-    stores = []
-    for cp in range(8):
-        loads.append(
-            [
-                pltpu.make_async_copy(vis.at[:, cp], v.at[cp], v_sem.at[cp]),
-                pltpu.make_async_copy(m_re.at[cp], mr_all.at[cp], re_sem.at[cp]),
-                pltpu.make_async_copy(m_im.at[cp], mi_all.at[cp], im_sem.at[cp]),
-            ]
-        )
-        stores.append(pltpu.make_async_copy(o.at[cp], res.at[:, cp], out_sem.at[cp]))
-    for group in loads:
-        for copy in group:
-            copy.start()
+    stores = [pltpu.make_async_copy(o.at[cp], res.at[:, cp], out_sem.at[cp]) for cp in range(8)]
     for n in range(8):
         for z in range(2):
             gains[z, n // 2, n % 2:n % 2 + 1, :] = gall[2 * n + active, z:z + 1, :]
     for cp in range(8):
-        for copy in loads[cp]:
-            copy.wait()
+        m_re, m_im = (re_early, im_early) if cp < 4 else (re_late, im_late)
         src = 2 * cp + active
 
         def lanes_of(z, t):
@@ -356,12 +388,12 @@
             lanes = slice(q * T, (q + 1) * T)
             gqr = lanes_of(0, 4 * j + q)
             gqi = lanes_of(1, 4 * j + q)
-            mr = mr_all[cp, :, lanes]
-            mi = mi_all[cp, :, lanes]
+            mr = m_re[cp % 4, :, lanes]
+            mi = m_im[cp % 4, :, lanes]
             ar = mr * gqr + mi * gqi
             ai = mi * gqr - mr * gqi
-            o[cp, 0, :, lanes] = v[cp, 0, :, lanes] - (gpr * ar - gpi * ai)
-            o[cp, 1, :, lanes] = v[cp, 1, :, lanes] - (gpr * ai + gpi * ar)
+            o[cp, 0, :, lanes] = vis[0, cp, :, lanes] - (gpr * ar - gpi * ai)
+            o[cp, 1, :, lanes] = vis[1, cp, :, lanes] - (gpr * ai + gpi * ar)
         stores[cp].start()
     for store in stores:
         store.wait()
@@ -389,12 +421,12 @@
     with jax.named_scope("pack"):
         packed = pl.pallas_call(
             pack,
-            out_shape=shape(8, 2, 2 * HALF, T),
+            out_shape=shape(8, 2, ROWS, T),
             in_specs=[ANY],
             out_specs=ANY,
             scratch_shapes=[
                 pltpu.VMEM((8, 2, T, 512), F32),
-                pltpu.VMEM((8, 2, 2 * HALF, T), F32),
+                pltpu.VMEM((8, 2, ROWS, T), F32),
                 pltpu.SemaphoreType.DMA((8,)),
                 pltpu.SemaphoreType.DMA((8,)),
                 pltpu.SemaphoreType.DMA((8,)),
@@ -419,13 +451,44 @@
                 pltpu.VMEM((2, 1024, 1024), F32),
                 pltpu.SemaphoreType.DMA((2, 4)),
             ],
-            compiler_params=vmem(24),
+            compiler_params=vmem(60),
             cost_estimate=pl.CostEstimate(flops=8 << 30, bytes_accessed=8 << 20, transcendentals=8 << 20),
         )(freqs, st, pix, fx)
+    def block(first):
+        return pl.pallas_call(
+            functools.partial(block_model, first),
+            out_shape=(shape(4, T, 512),) * 2,
+            in_specs=[SMEM, VMEM, VMEM, VMEM],
+            out_specs=(ANY,) * 2,
+            scratch_shapes=[
+                pltpu.VMEM((T, T), F32),
+                pltpu.VMEM((T, T), F32),
+                pltpu.VMEM((1024, T), F32),
+                pltpu.VMEM((1024, T), F32),
+                pltpu.VMEM((256, 3072), BF16),
+                pltpu.VMEM((2048, 512), BF16),
+                pltpu.VMEM((2, 4, T, 512), F32),
+                pltpu.SemaphoreType.DMA((2, 2)),
+            ],
+            compiler_params=vmem(14),
+            cost_estimate=pl.CostEstimate(flops=4 << 30, bytes_accessed=2 << 20, transcendentals=4 << 20),
+        )(freqs, st, pix, fx)
+
     with jax.named_scope("to_the_active_column"):
-        near, m_re, m_im = lax.optimization_barrier((near, m_re, m_im))
+        near, m_re, m_im, *early = lax.optimization_barrier((near, m_re, m_im, *block(0)))
+        mine = 4 * lax.axis_index("col")
+        pieces = [
+            near[:, :, 0:T],
+            jnp.concatenate(
+                [
+                    lax.dynamic_slice_in_dim(near, mine, 4)[:, :, T:ROWS],
+                    lax.dynamic_slice_in_dim(near, 4 - mine, 4)[:, :, T:T + 96],
+                ],
+                2,
+            ),
+        ]
         far = []
-        for half, turn in enumerate((0, rows // 2)):
+        for piece, turn in zip(pieces, (0, rows // 2)):
             pairs = []
             for z in range(chans):
                 to = z % 2
@@ -433,45 +496,22 @@
                     src = (r * cols + 1 - to) * chans + z
                     dst = ((r + turn) % rows * cols + to) * chans + z
                     pairs.append((src, dst))
-            piece = near[:, :, half * HALF:(half + 1) * HALF]
             far.append(lax.ppermute(piece, ("row", "col", "chan"), pairs))
+
     with jax.named_scope("block_model"):
-        b_re, b_im = pl.pallas_call(
-            block_model,
-            out_shape=(shape(8, T, 512),) * 2,
-            in_specs=[SMEM, VMEM, VMEM, VMEM],
-            out_specs=(ANY,) * 2,
-            scratch_shapes=[
-                pltpu.VMEM((T, T), F32),
-                pltpu.VMEM((T, T), F32),
-                pltpu.VMEM((1024, T), F32),
-                pltpu.VMEM((1024, T), F32),
-                pltpu.VMEM((256, 2048), BF16),
-                pltpu.VMEM((3072, 512), BF16),
-                pltpu.VMEM((2, 8, T, 512), F32),
-                pltpu.SemaphoreType.DMA((2, 4)),
-            ],
-            compiler_params=vmem(14),
-            cost_estimate=pl.CostEstimate(flops=8 << 30, bytes_accessed=4 << 20, transcendentals=8 << 20),
-        )(freqs, st, pix, fx)
-    far[0], far[1], b_re, b_im = lax.optimization_barrier((far[0], far[1], b_re, b_im))
+        late = block(2)
+    far[0], far[1], *late = lax.optimization_barrier((far[0], far[1], *late))
 
     with jax.named_scope("gain_solve"):
         g = pl.pallas_call(
             gain_solve,
             out_shape=shape(rows * cols, 2, 1024),
-            in_specs=[ANY] * 6,
+            in_specs=[VMEM] * 6,
             out_specs=VMEM,
             scratch_shapes=[
-                pltpu.VMEM((4, 1024), jnp.int32),
-                pltpu.VMEM((8, 2, 2 * HALF, T), F32),
-                pltpu.VMEM((8, 2, 2 * HALF, T), F32),
-                pltpu.VMEM((1024, 1024), F32),
-                pltpu.VMEM((1024, 1024), F32),
                 pltpu.VMEM((3072, 1024), BF16),
-                pltpu.VMEM((2, 4, T, T), F32),
+                pltpu.VMEM((2, 8, T, T), F32),
                 pltpu.VMEM((24, T), F32),
-                pltpu.SemaphoreType.DMA((6,)),
             ],
             compiler_params=vmem(26),
             cost_estimate=pl.CostEstimate(flops=800 << 20, bytes_accessed=14 << 20, transcendentals=0),
@@ -484,18 +524,12 @@
         res, gains = pl.pallas_call(
             residual,
             out_shape=(shape(2, 8, T, 512), shape(2, 4, 2, 1024)),
-            in_specs=[ANY, ANY, ANY, VMEM],
+            in_specs=[VMEM] * 6,
             out_specs=(ANY, VMEM),
-            scratch_shapes=[
-                pltpu.VMEM((8, 2, T, 512), F32),
-                pltpu.VMEM((8, T, 512), F32),
-                pltpu.VMEM((8, T, 512), F32),
-                pltpu.VMEM((8, 2, T, 512), F32),
-            ]
-            + [pltpu.SemaphoreType.DMA((8,))] * 4,
+            scratch_shapes=[pltpu.VMEM((8, 2, T, 512), F32), pltpu.SemaphoreType.DMA((8,))],
             compiler_params=vmem(18),
             cost_estimate=pl.CostEstimate(flops=32 << 20, bytes_accessed=12 << 20, transcendentals=0),
-        )(vis, b_re, b_im, gall)
+        )(vis, *early, *late, gall)
     return gains, res.reshape(2, 4, 2, T, 512)
 
 

time: 99.4 us -> 90.6 us (0.911)
  waiting for transfers between devices: 14.4 us -> 10.8 us
  local copies, waits for them, and re-layouts: 4.22 us -> 1.25 us
  blocking collectives: 15.7 us -> 13.8 us
    all_to_all x1, waiting for transfers between devices: 13.4 us -> 3.57 us  [body(): near = lax.all_to_all(packed, 'row', 0, 0, tiled=True)]
    ppermute x2, waiting for transfers between devices: 1.02 us -> 7.28 us  [body(): far.append(lax.ppermute(piece, ('row', 'col', 'chan'), pairs))]
    unnamed x21 -> x33, local copies, waits for them, and re-layouts: 4.02 us -> 1.04 us
    all_to_all x1, blocking collectives: 15.7 us -> 13.8 us  [body(): gall = lax.all_to_all(g, ('row', 'col'), 0, 0, tiled=True)]
    pallas_call x2 -> x3, Pallas kernels: 21.9 us -> 22 us  [the longest x2 18.6 us: block(): pl.pallas_call(functools.partial(block_model, first), out_shape=(shape(4,...]
  transfers between devices with their start and end apart: 3 -> 3, of which waited for: 2 -> 3; matrix products, arithmetic and copies ran while one was open for 0% -> 0% of each run, Pallas kernels for 35% -> 40%
where the time goes in v3:
time: 90.6 us; the launch traced here: 90.3 us
  Pallas kernels  53.5 us (59%)
  blocking collectives  13.8 us (15%)
  waiting for transfers between devices  10.8 us (12%)
  starting transfers between devices  9.89 us (11%)
  local copies, waits for them, and re-layouts  1.25 us (1%)
  between operations  0.95 us (1%)
    pallas_call x2, Pallas kernels, block(): pl.pallas_call(functools.partial(block_model, first), out_shape=(shape(4,...  18.6 us
    pallas_call x1, Pallas kernels, body(): pl.pallas_call(own_model, out_shape=(shape(1024, 1024),) * 2, in_specs=[S...  17.2 us
    all_to_all x1, blocking collectives, body(): gall = lax.all_to_all(g, ('row', 'col'), 0, 0, tiled=True)  13.8 us
    pallas_call x1, Pallas kernels, body(): pl.pallas_call(gain_solve, out_shape=shape(rows * cols, 2, 1024), in_spec...  11.4 us
    ppermute x2, waiting for transfers between devices, body(): far.append(lax.ppermute(piece, ('row', 'col', 'chan'), pairs))  7.28 us
    all_to_all x1, starting transfers between devices, body(): near = lax.all_to_all(packed, 'row', 0, 0, tiled=True)  7.04 us
    all_to_all x1, waiting for transfers between devices, body(): near = lax.all_to_all(packed, 'row', 0, 0, tiled=True)  3.57 us
    pallas_call x1, Pallas kernels, body(): pl.pallas_call(pack, out_shape=shape(8, 2, ROWS, T), in_specs=[ANY], out_...  3.4 us
  transfers between devices with their start and end apart: 3, of which 3 were waited for; matrix products, arithmetic and copies ran while one was open for 0% of the time, Pallas kernels for 40%

profile of v3, /device:TPU:32, one launch (start us, length us, event | category | flops | bytes accessed | tf_op | source)
XLA Modules:
  0.0 90.3 jit_solution(11575126730613738546)
XLA Ops:
  0.6 0.0 copy-start.10
  0.7 0.0 copy-start.12
  0.7 3.4 %pack.1 = f32[8,2,288,128]{3,2,1,0:T(8,128)} custom-call(f32[2,8,128,512]{3,2,1,0:T(8,128)} %bitcast.7), custom_call_target="tpu_custom_call" | custom-call | flops 1048576 | bytes 7340032 | tf_op jit(solution)/shard_map/pack/pallas_call | solution.py:422
  4.1 7.0 %all-to-all-start = ((f32[8,2,288,128]{3,2,1,0:T(8,128)}), f32[8,2,288,128]{3,2,1,0:T(8,128)S(1)}, u32[]{:S(2)}, u32[]{:S(2)}) async-start(f32[8,2,288,128]{3,2,1,0:T(8,128)} %pack.1), calls=%async_computation | async-start | bytes 4718592 | tf_op jit(solution)/shard_map/to_the_rows/all_to_all | solution.py:438
  11.2 0.0 copy-start.5
  11.2 9.3 %to_the_active_column.1 = (f32[4,128,512]{2,1,0:T(8,128)S(1)}, f32[4,128,512]{2,1,0:T(8,128)S(1)}) custom-call(f32[4]{0:T(128)S(1)} %copy-done.12, f32[2,8,128]{2,1,0:T(8,128)S(1)} %bitcast.9, s32[8,128]{1,0:T(8,128)S(1)} %bitcast.13, f32[8,8,128]{2,1,0:T(8,128)S(1)} %reshape.22.flux), custom_call_target="tpu_custom_call" | custom-call | flops 4294967296 | bytes 2097152 | tf_op jit(solution)/shard_map/to_the_active_column/pallas_call | solution.py:458
  20.6 1.0 %copy-done.3 = f32[4,128,512]{2,1,0:T(8,128)} copy-done((f32[4,128,512]{2,1,0:T(8,128)}, f32[4,128,512]{2,1,0:T(8,128)S(1)}, u32[]{:S(2)}) %copy-start.3) | copy-done | bytes 1048600
  21.5 17.2 %own_model.1 = (f32[1024,1024]{1,0:T(8,128)}, f32[1024,1024]{1,0:T(8,128)}) custom-call(f32[4]{0:T(128)} %freqs.5, f32[2,8,128]{2,1,0:T(8,128)} %bitcast.10, s32[8,128]{1,0:T(8,128)} %bitcast.12, f32[8,8,128]{2,1,0:T(8,128)} %copy-done.5), custom_call_target="tpu_custom_call" | custom-call | flops 8589934592 | bytes 8388608 | tf_op jit(solution)/shard_map/own_model/pallas_call | solution.py:441
  38.7 0.0 copy-start.6
  38.7 0.0 copy-start.11
  38.7 0.0 copy-start.13
  38.7 3.6 %all-to-all-done.near = f32[8,2,288,128]{3,2,1,0:T(8,128)S(1)} async-done(((f32[8,2,288,128]{3,2,1,0:T(8,128)}), f32[8,2,288,128]{3,2,1,0:T(8,128)S(1)}, u32[]{:S(2)}, u32[]{:S(2)}) %all-to-all-start) | async-done | bytes 2359328 | tf_op jit(solution)/shard_map/to_the_rows/all_to_all | solution.py:438
  42.3 0.1 slice.9
  42.4 1.3 %collective-permute-start = (f32[8,2,128,128]{3,2,1,0:T(8,128)S(1)}, f32[8,2,128,128]{3,2,1,0:T(8,128)S(1)}, u32[]{:S(2)}, u32[]{:S(2)}) collective-permute-start(f32[8,2,128,128]{3,2,1,0:T(8,128)S(1)} %slice.9), channel_id=1, source_target_pairs={{16,0},{48,32},{80,64},{112,96},{144,128},{176,160},{208,192},{240... | collective-permute-start | bytes 3145736 | tf_op jit(solution)/shard_map/to_the_active_column/ppermute | solution.py:499
  43.7 0.1 constant_dynamic-slice_fusion.1
  43.8 0.1 pad_maximum_fusion
  43.9 0.0 copy-start.7
  43.9 1.6 %collective-permute-start.1 = (f32[4,2,256,128]{3,2,1,0:T(8,128)S(1)}, f32[4,2,256,128]{3,2,1,0:T(8,128)S(1)}, u32[]{:S(2)}, u32[]{:S(2)}) collective-permute-start(f32[4,2,256,128]{3,2,1,0:T(8,128)S(1)} %pad_maximum_fusion), channel_id=1, source_target_pairs={{16,128},{48,160},{80,192},{112,224},{144,0},{176,32},{208,64},{24... | collective-permute-start | bytes 3145736 | tf_op jit(solution)/shard_map/to_the_active_column/ppermute | solution.py:499
  45.5 9.3 %block_model.1 = (f32[4,128,512]{2,1,0:T(8,128)S(1)}, f32[4,128,512]{2,1,0:T(8,128)S(1)}) custom-call(f32[4]{0:T(128)S(1)} %copy-done.13, f32[2,8,128]{2,1,0:T(8,128)S(1)} %bitcast.11, s32[8,128]{1,0:T(8,128)S(1)} %bitcast.14, f32[8,8,128]{2,1,0:T(8,128)S(1)} %copy-done.6), custom_call_target="tpu_custom_call" | custom-call | flops 4294967296 | bytes 2097152 | tf_op jit(solution)/shard_map/block_model/pallas_call | solution.py:458
  54.8 4.3 %collective-permute-done.far1 = f32[8,2,128,128]{3,2,1,0:T(8,128)S(1)} collective-permute-done((f32[8,2,128,128]{3,2,1,0:T(8,128)S(1)}, f32[8,2,128,128]{3,2,1,0:T(8,128)S(1)}, u32[]{:S(2)}, u32[]{:S(2)}) %collective-permute-start) | collective-permute-done | bytes 1048608 | tf_op jit(solution)/shard_map/to_the_active_column/ppermute | solution.py:499
  59.1 3.0 %collective-permute-done.1.far2 = f32[4,2,256,128]{3,2,1,0:T(8,128)S(1)} collective-permute-done((f32[4,2,256,128]{3,2,1,0:T(8,128)S(1)}, f32[4,2,256,128]{3,2,1,0:T(8,128)S(1)}, u32[]{:S(2)}, u32[]{:S(2)}) %collective-permute-start.1) | collective-permute-done | bytes 1048608 | tf_op jit(solution)/shard_map/to_the_active_column/ppermute | solution.py:499
  62.1 11.4 %gain_solve.1 = f32[16,2,1024]{2,1,0:T(2,128)S(1)} custom-call(s32[4,1024]{1,0:T(4,128)S(1)} %copy-done.7, f32[8,2,288,128]{3,2,1,0:T(8,128)S(1)} %all-to-all-done.near, f32[8,2,128,128]{3,2,1,0:T(8,128)S(1)} %collective-permute-done.far1, f32[4,2,256,128]{3,2,1,0:T(8,128)S(1)} %collective-permute-done.1.far2, f32[1024,1024]{1,0:T(8,128)S(1)} %copy-done.1, ...), custom_call_target="tpu_custom_call" | custom-call | flops 838860800 | bytes 14680064 | tf_op jit(solution)/shard_map/gain_solve/pallas_call | solution.py:506
  73.6 13.8 %all_to_all.10.gall = f32[16,2,1024]{2,1,0:T(2,128)S(1)} all-to-all(f32[16,2,1024]{2,1,0:T(2,128)S(1)} %gain_solve.1), channel_id=1, replica_groups=mesh['row'=8,'col'=2,'chan'=16] {'row','col'}, dimensions={0} | all-to-all | bytes 262144 | tf_op jit(solution)/shard_map/gather_gains/all_to_all | solution.py:521
  87.4 2.9 %residual.1 = (f32[2,8,128,512]{3,2,1,0:T(8,128)}, f32[2,4,2,1024]{3,2,1,0:T(2,128)}) custom-call(f32[2,8,128,512]{3,2,1,0:T(8,128)S(1)} %bitcast.8, f32[4,128,512]{2,1,0:T(8,128)S(1)} %get-tuple-element.23.re_early, f32[4,128,512]{2,1,0:T(8,128)S(1)} %copy-done.4, f32[4,128,512]{2,1,0:T(8,128)S(1)} %get-tuple-element.28.re_late, ...), custom_call_target="tpu_custom_call" | custom-call | flops 33554432 | bytes 12582912 | tf_op jit(solution)/shard_map/residual/pallas_call | solution.py:524
  (27 shorter events, 0.1 us)
Async XLA Ops:
  0.6 10.5 %copy-start.15 = (f32[2,1024]{1,0:T(2,128)S(1)}, f32[2,1024]{1,0:T(2,128)}, u32[]{:S(2)}) copy-start(f32[2,1024]{1,0:T(2,128)} %param.7) | copy-start | bytes 24580
  0.6 10.5 %copy-start.14 = (f32[4,2,1024]{2,1,0:T(2,128)S(1)}, f32[4,2,1024]{2,1,0:T(2,128)}, u32[]{:S(2)}) copy-start(f32[4,2,1024]{2,1,0:T(2,128)} %param.9) | copy-start | bytes 98308
  0.6 10.6 %copy-start.10 = (s32[1024]{0:T(1024)S(1)}, s32[1024]{0:T(1024)}, u32[]{:S(2)}) copy-start(s32[1024]{0:T(1024)} %param.8) | copy-start | bytes 12292
  0.7 10.6 %copy-start.12 = (f32[4]{0:T(128)S(1)}, f32[4]{0:T(128)}, u32[]{:S(2)}) copy-start(f32[4]{0:T(128)} %freqs.5) | copy-start | bytes 52
  4.1 38.2 %all-to-all-start = ((f32[8,2,288,128]{3,2,1,0:T(8,128)}), f32[8,2,288,128]{3,2,1,0:T(8,128)S(1)}, u32[]{:S(2)}, u32[]{:S(2)}) async-start(f32[8,2,288,128]{3,2,1,0:T(8,128)} %pack.1), calls=%async_computation | async-start | bytes 4718592 | tf_op jit(solution)/shard_map/to_the_rows/all_to_all | solution.py:438
  11.1 9.4 %copy-start.8 = (f32[1,2,8,128]{3,2,1,0:T(8,128)}, f32[1,2,8,128]{3,2,1,0:T(8,128)S(1)}, u32[]{:S(2)}) copy-start(f32[1,2,8,128]{3,2,1,0:T(8,128)S(1)} %copy.10) | copy-start | bytes 24580
  11.2 9.3 %copy-start.5 = (f32[8,8,128]{2,1,0:T(8,128)}, f32[8,8,128]{2,1,0:T(8,128)S(1)}, u32[]{:S(2)}) copy-start(f32[8,8,128]{2,1,0:T(8,128)S(1)} %reshape.22.flux) | copy-start | bytes 98308
  20.5 1.0 %copy-start.3 = (f32[4,128,512]{2,1,0:T(8,128)}, f32[4,128,512]{2,1,0:T(8,128)S(1)}, u32[]{:S(2)}) copy-start(f32[4,128,512]{2,1,0:T(8,128)S(1)} %get-tuple-element.24.im_early) | copy-start | bytes 3145732
  38.7 6.8 %copy-start.6 = (f32[8,8,128]{2,1,0:T(8,128)S(1)}, f32[8,8,128]{2,1,0:T(8,128)}, u32[]{:S(2)}) copy-start(f32[8,8,128]{2,1,0:T(8,128)} %copy-done.5) | copy-start | bytes 98308
  38.7 6.8 %copy-start.9 = (f32[1,2,8,128]{3,2,1,0:T(8,128)S(1)}, f32[1,2,8,128]{3,2,1,0:T(8,128)}, u32[]{:S(2)}) copy-start(f32[1,2,8,128]{3,2,1,0:T(8,128)} %copy-done.8) | copy-start | bytes 24580
  38.7 6.8 %copy-start.11 = (s32[1024]{0:T(1024)S(1)}, s32[1024]{0:T(1024)}, u32[]{:S(2)}) copy-start(s32[1024]{0:T(1024)} %param.8) | copy-start | bytes 12292
  38.7 6.8 %copy-start.13 = (f32[4]{0:T(128)S(1)}, f32[4]{0:T(128)}, u32[]{:S(2)}) copy-start(f32[4]{0:T(128)} %freqs.5) | copy-start | bytes 52
  42.4 16.7 %collective-permute-start = (f32[8,2,128,128]{3,2,1,0:T(8,128)S(1)}, f32[8,2,128,128]{3,2,1,0:T(8,128)S(1)}, u32[]{:S(2)}, u32[]{:S(2)}) collective-permute-start(f32[8,2,128,128]{3,2,1,0:T(8,128)S(1)} %slice.9), channel_id=1, source_target_pairs={{16,0},{48,32},{80,64},{112,96},{144,128},{176,160},{208,192},{240... | collective-permute-start | bytes 3145736 | tf_op jit(solution)/shard_map/to_the_active_column/ppermute | solution.py:499
  43.9 18.2 %copy-start.1 = (f32[1024,1024]{1,0:T(8,128)S(1)}, f32[1024,1024]{1,0:T(8,128)}, u32[]{:S(2)}) copy-start(f32[1024,1024]{1,0:T(8,128)} %get-tuple-element.32.m_re) | copy-start | bytes 12582916
  43.9 18.2 %copy-start.2 = (f32[1024,1024]{1,0:T(8,128)S(1)}, f32[1024,1024]{1,0:T(8,128)}, u32[]{:S(2)}) copy-start(f32[1024,1024]{1,0:T(8,128)} %get-tuple-element.33.m_im) | copy-start | bytes 12582916
  43.9 18.2 %copy-start.7 = (s32[4,1024]{1,0:T(4,128)S(1)}, s32[4,1024]{1,0:T(4,128)}, u32[]{:S(2)}) copy-start(s32[4,1024]{1,0:T(4,128)} %flags.1) | copy-start | bytes 49156
  43.9 18.2 %collective-permute-start.1 = (f32[4,2,256,128]{3,2,1,0:T(8,128)S(1)}, f32[4,2,256,128]{3,2,1,0:T(8,128)S(1)}, u32[]{:S(2)}, u32[]{:S(2)}) collective-permute-start(f32[4,2,256,128]{3,2,1,0:T(8,128)S(1)} %pad_maximum_fusion), channel_id=1, source_target_pairs={{16,128},{48,160},{80,192},{112,224},{144,0},{176,32},{208,64},{24... | collective-permute-start | bytes 3145736 | tf_op jit(solution)/shard_map/to_the_active_column/ppermute | solution.py:499
  62.1 25.3 %copy-start = (f32[2,4,2,128,512]{4,3,2,1,0:T(8,128)S(1)}, f32[2,4,2,128,512]{4,3,2,1,0:T(8,128)}, u32[]{:S(2)}) copy-start(f32[2,4,2,128,512]{4,3,2,1,0:T(8,128)} %param.6) | copy-start | bytes 12582916
  62.1 25.2 %copy-start.4 = (f32[4,128,512]{2,1,0:T(8,128)S(1)}, f32[4,128,512]{2,1,0:T(8,128)}, u32[]{:S(2)}) copy-start(f32[4,128,512]{2,1,0:T(8,128)} %copy-done.3) | copy-start | bytes 3145732

commit v4 on v3

--- a/solution.py
+++ b/solution.py
@@ -230,95 +230,147 @@
         store.wait()
 
 
-def gain_solve(flags, near, far1, far2, m_re, m_im, out, cc, halves, diag):
-    cp, j = lax.axis_index("row"), lax.axis_index("col")
-    active = lax.axis_index("chan") % 2
-
-    @pl.when(j == active)
-    def _():
-        solve(cp, j, flags, near, far1, far2, m_re, m_im, out, cc, halves, diag)
-
-    @pl.when(j != active)
-    def _():
-        out[...] = jnp.zeros_like(out)
-
-
-def solve(cp, j, flags, near, far1, far2, m_re, m_im, out, cc, halves, diag):
-
-    def of_near(diagonal, a, z, lo, hi):
-        return near[a, z, lo:hi, :]
-
-    def of_far(diagonal, a, z, lo, hi):
+def is_solver():
+    return lax.axis_index("col") == lax.axis_index("chan") % 2
+
+
+class Filler:
+    def __init__(self, side, part_of, m_re, m_im, cc, halves, diag):
+        self.refs = m_re, m_im, cc, halves, diag
+        self.side, self.part_of = side, part_of
+
+    def products(self, row, col, vr, vi):
+        m_re, m_im = self.refs[:2]
+        rs = pl.ds(pl.multiple_of(row * T, T), T)
+        cs = pl.ds(pl.multiple_of(col * T, T), T)
+        mr = m_re[rs, cs]
+        mi = m_im[rs, cs]
+        return vr * mr + vi * mi, vr * mi - vi * mr
+
+    def put(self, row, col, parts):
+        cc = self.refs[2]
+        cs = pl.ds(pl.multiple_of(col * T, T), T)
+        for n, part in enumerate(parts):
+            cc[pl.ds(pl.multiple_of(n * 1024 + row * T, T), T), cs] = part.astype(BF16)
+
+    def fill(self, row, col, vr, vi):
+        self.put(row, col, self.products(row, col, vr, vi))
+        self.put(col, row, self.products(col, row, vr.T, -vi.T))
+
+    def own_block(self, a, z):
+        low = lax.broadcasted_iota(jnp.int32, (64, T), 1) < 64
+        top = self.part_of(True, a, z, T + 64, 2 * T)
+        turned = jnp.concatenate([top, top], 0).T[64:T]
+        last = self.part_of(True, a, z, 2 * T, ROWS)
+        right = jnp.concatenate([pltpu.roll(last, 64, 1), last], 0)
+        return jnp.concatenate([top, jnp.where(low, -turned if z else turned, right)], 0)
+
+    def run(self):
+        part_of, fill = self.part_of, self.fill
+        halves, diag = self.refs[3:]
+        jj = (lax.axis_index("col") + self.side) % 2
+        off = jnp.where(jj == 0, 1, 0)
+        eye = on_diagonal()
+
+        def sources(r, _):
+            a = 4 * jj + r
+            parts = self.products(a, a, self.own_block(a, 0), self.own_block(a, 1))
+            for n, part in enumerate(parts):
+                diag[pl.ds(8 * n + a, 1), :] = jnp.sum(jnp.where(eye, part, 0.0), axis=0, keepdims=True)
+            self.put(a, a, [jnp.where(eye, 0.0, part) for part in parts])
+            fill(a, 4 * jj + (r + 1) % 4, part_of(True, a, 0, 0, T), part_of(True, a, 1, 0, T))
+            for z in range(2):
+                rs = pl.ds(pl.multiple_of((r // 2) * 64, 64), 64)
+                halves[z, r % 2, rs, :] = part_of(True, a, z, T, T + 64)
+            b = 4 * (1 - jj) + r
+            fill(b, 4 * jj + (r + off) % 4, part_of(False, b, 0, 0, T), part_of(False, b, 1, 0, T))
+            if self.side == 0:
+                fill(b, 4 * jj + (r + off + 1) % 4, part_of(False, b, 0, T, 2 * T), part_of(False, b, 1, T, 2 * T))
+            else:
+                for z in range(2):
+                    halves[z, 2 + (r + off + 1) % 4, 32:T, :] = part_of(False, b, z, T, T + 96)
+            return 0
+
+        lax.fori_loop(0, 4, sources, 0)
+
+        def across(p, _):
+            fill(4 * jj + p, 4 * jj + p + 2, halves[0, p], halves[1, p])
+            return 0
+
+        lax.fori_loop(0, 2, across, 0)
+
+
+def on_diagonal():
+    return lax.broadcasted_iota(jnp.int32, (T, T), 0) == lax.broadcasted_iota(jnp.int32, (T, T), 1)
+
+
+def of_near(near):
+    return lambda diagonal, a, z, lo, hi: near[a, z, lo:hi, :]
+
+
+def of_far(far1, far2):
+    def part_of(diagonal, a, z, lo, hi):
         if hi <= T:
             return far1[a, z, lo:hi, :]
         start = lo - T + (0 if diagonal else ROWS - T)
         return far2[a % 4, z, start:start + hi - lo, :]
-    low = lax.broadcasted_iota(jnp.int32, (64, T), 1) < 64
-    eye = lax.broadcasted_iota(jnp.int32, (T, T), 0) == lax.broadcasted_iota(jnp.int32, (T, T), 1)
-
-    def products(row, col, vr, vi):
-        rs = pl.ds(pl.multiple_of(row * T, T), T)
-        cs = pl.ds(pl.multiple_of(col * T, T), T)
-        mr = m_re[rs, cs]
-        mi = m_im[rs, cs]
-        return vr * mr + vi * mi, vr * mi - vi * mr, mr * mr + mi * mi
-
-    def put(row, col, parts):
-        cs = pl.ds(pl.multiple_of(col * T, T), T)
-        for n, part in enumerate(parts):
-            cc[pl.ds(pl.multiple_of(n * 1024 + row * T, T), T), cs] = part.astype(BF16)
-
-    def fill(row, col, vr, vi):
-        put(row, col, products(row, col, vr, vi))
-        put(col, row, products(col, row, vr.T, -vi.T))
-
-    for side, (part_of, jj) in enumerate(((of_near, j), (of_far, 1 - j))):
-        off = jnp.where(jj == 0, 1, 0)
-
-        def own_block(a, z):
-            top = part_of(True, a, z, T + 64, 2 * T)
-            turned = jnp.concatenate([top, top], 0).T[64:T]
-            last = part_of(True, a, z, 2 * T, ROWS)
-            right = jnp.concatenate([pltpu.roll(last, 64, 1), last], 0)
-            return jnp.concatenate([top, jnp.where(low, -turned if z else turned, right)], 0)
-
-        def sources(r, _):
-            a = 4 * jj + r
-            parts = products(a, a, own_block(a, 0), own_block(a, 1))
-            for n, part in enumerate(parts):
-                diag[pl.ds(8 * n + a, 1), :] = jnp.sum(jnp.where(eye, part, 0.0), axis=0, keepdims=True)
-            put(a, a, [jnp.where(eye, 0.0, part) for part in parts])
-            fill(a, 4 * jj + (r + 1) % 4, part_of(True, a, 0, 0, T), part_of(True, a, 1, 0, T))
-            for z in range(2):
-                rs = pl.ds(pl.multiple_of((r // 2) * 64, 64), 64)
-                halves[z, 2 * side + r % 2, rs, :] = part_of(True, a, z, T, T + 64)
-            b = 4 * (1 - jj) + r
-            fill(b, 4 * jj + (r + off) % 4, part_of(False, b, 0, 0, T), part_of(False, b, 1, 0, T))
-            if side == 0:
-                fill(b, 4 * jj + (r + off + 1) % 4, part_of(False, b, 0, T, 2 * T), part_of(False, b, 1, T, 2 * T))
-                for z in range(2):
-                    halves[z, 4 + r, 0:32, :] = part_of(False, b, z, 2 * T, ROWS)
-            else:
-                for z in range(2):
-                    halves[z, 4 + (r + off + 1) % 4, 32:T, :] = part_of(False, b, z, T, T + 96)
+
+    return part_of
+
+
+def prepare(near, m_re, m_im, cc, diag, halves):
+    @pl.when(is_solver())
+    def _():
+        eye = on_diagonal()
+
+        def powers(a, _):
+            rs = pl.ds(pl.multiple_of(a * T, T), T)
+            out = pl.ds(pl.multiple_of(2048 + a * T, T), T)
+            for t in range(8):
+                lanes = slice(t * T, (t + 1) * T)
+                mr = m_re[rs, lanes]
+                mi = m_im[rs, lanes]
+                cc[out, lanes] = (mr * mr + mi * mi).astype(BF16)
+            lanes = pl.ds(pl.multiple_of(a * T, T), T)
+            mr = m_re[rs, lanes]
+            mi = m_im[rs, lanes]
+            den = mr * mr + mi * mi
+            diag[pl.ds(16 + a, 1), :] = jnp.sum(jnp.where(eye, den, 0.0), axis=0, keepdims=True)
+            cc[out, lanes] = jnp.where(eye, 0.0, den).astype(BF16)
             return 0
 
-        lax.fori_loop(0, 4, sources, 0)
-
-        def across(p, _):
-            fill(4 * jj + p, 4 * jj + p + 2, halves[0, 2 * side + p], halves[1, 2 * side + p])
-            return 0
-
-        lax.fori_loop(0, 2, across, 0)
-
+        lax.fori_loop(0, 8, powers, 0)
+        Filler(0, of_near(near), m_re, m_im, cc, halves, diag).run()
+
+
+def gain_solve(flags, part, part_diag, near, far1, far2, m_re, m_im, out, cc, halves, diag, sem):
+    @pl.when(is_solver())
+    def _():
+        copy = pltpu.make_async_copy(part, cc, sem)
+        copy.start()
+        diag[...] = part_diag[...]
+        copy.wait()
+        solve(flags, near, far1, far2, m_re, m_im, out, cc, halves, diag)
+
+    @pl.when(jnp.logical_not(is_solver()))
+    def _():
+        out[...] = jnp.zeros_like(out)
+
+
+def solve(flags, near, far1, far2, m_re, m_im, out, cc, halves, diag):
+    cp, j = lax.axis_index("row"), lax.axis_index("col")
+    filler = Filler(1, of_far(far1, far2), m_re, m_im, cc, halves, diag)
+    filler.run()
     near_off = jnp.where(j == 0, 1, 0)
 
     def thirds(r, _):
-        fill(4 * (1 - j) + r, 4 * j + (r + near_off + 2) % 4, halves[0, 4 + r], halves[1, 4 + r])
+        a = 4 * (1 - j) + r
+        for z in range(2):
+            halves[z, 2 + r, 0:32, :] = near[a, z, 2 * T:ROWS, :]
+        filler.fill(a, 4 * j + (r + near_off + 2) % 4, halves[0, 2 + r], halves[1, 2 + r])
         return 0
 
     lax.fori_loop(0, 4, thirds, 0)
-
     w = flags[pl.ds(cp // 2, 1), :].astype(F32)
 
     def row_of(n):
@@ -500,22 +552,33 @@
 
     with jax.named_scope("block_model"):
         late = block(2)
-    far[0], far[1], *late = lax.optimization_barrier((far[0], far[1], *late))
+    with jax.named_scope("prepare"):
+        part, part_diag = pl.pallas_call(
+            prepare,
+            out_shape=(jax.ShapeDtypeStruct((3072, 1024), BF16), shape(24, T)),
+            in_specs=[VMEM] * 3,
+            out_specs=(VMEM, VMEM),
+            scratch_shapes=[pltpu.VMEM((2, 2, T, T), F32)],
+            compiler_params=vmem(18),
+            cost_estimate=pl.CostEstimate(flops=16 << 20, bytes_accessed=16 << 20, transcendentals=0),
+        )(near, m_re, m_im)
+    far[0], far[1], part, *late = lax.optimization_barrier((far[0], far[1], part, *late))
 
     with jax.named_scope("gain_solve"):
         g = pl.pallas_call(
             gain_solve,
             out_shape=shape(rows * cols, 2, 1024),
-            in_specs=[VMEM] * 6,
+            in_specs=[VMEM] * 8,
             out_specs=VMEM,
             scratch_shapes=[
                 pltpu.VMEM((3072, 1024), BF16),
-                pltpu.VMEM((2, 8, T, T), F32),
+                pltpu.VMEM((2, 6, T, T), F32),
                 pltpu.VMEM((24, T), F32),
+                pltpu.SemaphoreType.DMA,
             ],
-            compiler_params=vmem(26),
+            compiler_params=vmem(27),
             cost_estimate=pl.CostEstimate(flops=800 << 20, bytes_accessed=14 << 20, transcendentals=0),
-        )(flags, near, *far, m_re, m_im)
+        )(flags, part, part_diag, near, *far, m_re, m_im)
 
     with jax.named_scope("gather_gains"):
         gall = lax.all_to_all(g, ("row", "col"), 0, 0, tiled=True)
@@ -527,7 +590,7 @@
             in_specs=[VMEM] * 6,
             out_specs=(ANY, VMEM),
             scratch_shapes=[pltpu.VMEM((8, 2, T, 512), F32), pltpu.SemaphoreType.DMA((8,))],
-            compiler_params=vmem(18),
+            compiler_params=vmem(14),
             cost_estimate=pl.CostEstimate(flops=32 << 20, bytes_accessed=12 << 20, transcendentals=0),
         )(vis, *early, *late, gall)
     return gains, res.reshape(2, 4, 2, T, 512)

time: 90.6 us -> 88.9 us (0.981)
  waiting for transfers between devices: 10.8 us -> 8.3 us
    ppermute x2, waiting for transfers between devices: 7.28 us -> 4.76 us  [body(): far.append(lax.ppermute(piece, ('row', 'col', 'chan'), pairs))]
    pallas_call x0 -> x1, Pallas kernels: none -> 2.48 us  [body(): pl.pallas_call(prepare, out_shape=(jax.ShapeDtypeStruct((3072, 1024), BF1...]
    pallas_call x1, Pallas kernels: 11.4 us -> 9.85 us  [body(): pl.pallas_call(gain_solve, out_shape=shape(rows * cols, 2, 1024), in_spec...]
  transfers between devices with their start and end apart: 3 -> 3, of which waited for: 3 -> 3; matrix products, arithmetic and copies ran while one was open for 0% -> 0% of each run, Pallas kernels for 40% -> 43%
where the time goes in v4:
time: 88.9 us; the launch traced here: 88.6 us
  Pallas kernels  54.4 us (61%)
  blocking collectives  13.8 us (16%)
  starting transfers between devices  9.89 us (11%)
  waiting for transfers between devices  8.3 us (9%)
  local copies, waits for them, and re-layouts  1.24 us (1%)
  between operations  0.95 us (1%)
    pallas_call x2, Pallas kernels, block(): pl.pallas_call(functools.partial(block_model, first), out_shape=(shape(4,...  18.6 us
    pallas_call x1, Pallas kernels, body(): pl.pallas_call(own_model, out_shape=(shape(1024, 1024),) * 2, in_specs=[S...  17.2 us
    all_to_all x1, blocking collectives, body(): gall = lax.all_to_all(g, ('row', 'col'), 0, 0, tiled=True)  13.8 us
    pallas_call x1, Pallas kernels, body(): pl.pallas_call(gain_solve, out_shape=shape(rows * cols, 2, 1024), in_spec...  9.85 us
    all_to_all x1, starting transfers between devices, body(): near = lax.all_to_all(packed, 'row', 0, 0, tiled=True)  7.04 us
    ppermute x2, waiting for transfers between devices, body(): far.append(lax.ppermute(piece, ('row', 'col', 'chan'), pairs))  4.76 us
    all_to_all x1, waiting for transfers between devices, body(): near = lax.all_to_all(packed, 'row', 0, 0, tiled=True)  3.54 us
    pallas_call x1, Pallas kernels, body(): pl.pallas_call(pack, out_shape=shape(8, 2, ROWS, T), in_specs=[ANY], out_...  3.4 us
  transfers between devices with their start and end apart: 3, of which 3 were waited for; matrix products, arithmetic and copies ran while one was open for 0% of the time, Pallas kernels for 43%

profile of v4, /device:TPU:32, one launch (start us, length us, event | category | flops | bytes accessed | tf_op | source)
XLA Modules:
  0.0 88.6 jit_solution(8290825627265449127)
XLA Ops:
  0.6 0.0 copy-start.10
  0.7 0.0 copy-start.12
  0.7 3.4 %pack.1 = f32[8,2,288,128]{3,2,1,0:T(8,128)} custom-call(f32[2,8,128,512]{3,2,1,0:T(8,128)} %bitcast.7), custom_call_target="tpu_custom_call" | custom-call | flops 1048576 | bytes 7340032 | tf_op jit(solution)/shard_map/pack/pallas_call | solution.py:474
  4.1 7.0 %all-to-all-start = ((f32[8,2,288,128]{3,2,1,0:T(8,128)}), f32[8,2,288,128]{3,2,1,0:T(8,128)S(1)}, u32[]{:S(2)}, u32[]{:S(2)}) async-start(f32[8,2,288,128]{3,2,1,0:T(8,128)} %pack.1), calls=%async_computation | async-start | bytes 4718592 | tf_op jit(solution)/shard_map/to_the_rows/all_to_all | solution.py:490
  11.2 0.0 copy-start.5
  11.2 9.3 %to_the_active_column.1 = (f32[4,128,512]{2,1,0:T(8,128)S(1)}, f32[4,128,512]{2,1,0:T(8,128)S(1)}) custom-call(f32[4]{0:T(128)S(1)} %copy-done.12, f32[2,8,128]{2,1,0:T(8,128)S(1)} %bitcast.9, s32[8,128]{1,0:T(8,128)S(1)} %bitcast.13, f32[8,8,128]{2,1,0:T(8,128)S(1)} %reshape.22.flux), custom_call_target="tpu_custom_call" | custom-call | flops 4294967296 | bytes 2097152 | tf_op jit(solution)/shard_map/to_the_active_column/pallas_call | solution.py:510
  20.5 1.0 %copy-done.3 = f32[4,128,512]{2,1,0:T(8,128)} copy-done((f32[4,128,512]{2,1,0:T(8,128)}, f32[4,128,512]{2,1,0:T(8,128)S(1)}, u32[]{:S(2)}) %copy-start.3) | copy-done | bytes 1048600
  21.5 17.2 %own_model.1 = (f32[1024,1024]{1,0:T(8,128)}, f32[1024,1024]{1,0:T(8,128)}) custom-call(f32[4]{0:T(128)} %freqs.5, f32[2,8,128]{2,1,0:T(8,128)} %bitcast.10, s32[8,128]{1,0:T(8,128)} %bitcast.12, f32[8,8,128]{2,1,0:T(8,128)} %copy-done.5), custom_call_target="tpu_custom_call" | custom-call | flops 8589934592 | bytes 8388608 | tf_op jit(solution)/shard_map/own_model/pallas_call | solution.py:493
  38.7 0.0 copy-start.6
  38.7 0.0 copy-start.11
  38.7 0.0 copy-start.13
  38.8 3.5 %all-to-all-done.near = f32[8,2,288,128]{3,2,1,0:T(8,128)S(1)} async-done(((f32[8,2,288,128]{3,2,1,0:T(8,128)}), f32[8,2,288,128]{3,2,1,0:T(8,128)S(1)}, u32[]{:S(2)}, u32[]{:S(2)}) %all-to-all-start) | async-done | bytes 2359328 | tf_op jit(solution)/shard_map/to_the_rows/all_to_all | solution.py:490
  42.3 0.1 slice.9
  42.4 1.3 %collective-permute-start = (f32[8,2,128,128]{3,2,1,0:T(8,128)S(1)}, f32[8,2,128,128]{3,2,1,0:T(8,128)S(1)}, u32[]{:S(2)}, u32[]{:S(2)}) collective-permute-start(f32[8,2,128,128]{3,2,1,0:T(8,128)S(1)} %slice.9), channel_id=1, source_target_pairs={{16,0},{48,32},{80,64},{112,96},{144,128},{176,160},{208,192},{240... | collective-permute-start | bytes 3145736 | tf_op jit(solution)/shard_map/to_the_active_column/ppermute | solution.py:551
  43.7 0.1 constant_dynamic-slice_fusion.1
  43.8 0.1 pad_maximum_fusion
  43.9 1.6 %collective-permute-start.1 = (f32[4,2,256,128]{3,2,1,0:T(8,128)S(1)}, f32[4,2,256,128]{3,2,1,0:T(8,128)S(1)}, u32[]{:S(2)}, u32[]{:S(2)}) collective-permute-start(f32[4,2,256,128]{3,2,1,0:T(8,128)S(1)} %pad_maximum_fusion), channel_id=1, source_target_pairs={{16,128},{48,160},{80,192},{112,224},{144,0},{176,32},{208,64},{24... | collective-permute-start | bytes 3145736 | tf_op jit(solution)/shard_map/to_the_active_column/ppermute | solution.py:551
  45.5 9.3 %block_model.1 = (f32[4,128,512]{2,1,0:T(8,128)S(1)}, f32[4,128,512]{2,1,0:T(8,128)S(1)}) custom-call(f32[4]{0:T(128)S(1)} %copy-done.13, f32[2,8,128]{2,1,0:T(8,128)S(1)} %bitcast.11, s32[8,128]{1,0:T(8,128)S(1)} %bitcast.14, f32[8,8,128]{2,1,0:T(8,128)S(1)} %copy-done.6), custom_call_target="tpu_custom_call" | custom-call | flops 4294967296 | bytes 2097152 | tf_op jit(solution)/shard_map/block_model/pallas_call | solution.py:510
  54.8 2.5 %prepare.1 = (bf16[3072,1024]{1,0:T(8,128)(2,1)S(1)}, f32[24,128]{1,0:T(8,128)S(1)}) custom-call(f32[8,2,288,128]{3,2,1,0:T(8,128)S(1)} %all-to-all-done.near, f32[1024,1024]{1,0:T(8,128)S(1)} %copy-done.1, f32[1024,1024]{1,0:T(8,128)S(1)} %copy-done.2), custom_call_target="tpu_custom_call" | custom-call | flops 16777216 | bytes 16777216 | tf_op jit(solution)/shard_map/prepare/pallas_call | solution.py:556
  57.3 1.8 %collective-permute-done.far1 = f32[8,2,128,128]{3,2,1,0:T(8,128)S(1)} collective-permute-done((f32[8,2,128,128]{3,2,1,0:T(8,128)S(1)}, f32[8,2,128,128]{3,2,1,0:T(8,128)S(1)}, u32[]{:S(2)}, u32[]{:S(2)}) %collective-permute-start) | collective-permute-done | bytes 1048608 | tf_op jit(solution)/shard_map/to_the_active_column/ppermute | solution.py:551
  59.1 3.0 %collective-permute-done.1.far2 = f32[4,2,256,128]{3,2,1,0:T(8,128)S(1)} collective-permute-done((f32[4,2,256,128]{3,2,1,0:T(8,128)S(1)}, f32[4,2,256,128]{3,2,1,0:T(8,128)S(1)}, u32[]{:S(2)}, u32[]{:S(2)}) %collective-permute-start.1) | collective-permute-done | bytes 1048608 | tf_op jit(solution)/shard_map/to_the_active_column/ppermute | solution.py:551
  62.1 9.9 %gain_solve.1 = f32[16,2,1024]{2,1,0:T(2,128)S(1)} custom-call(s32[4,1024]{1,0:T(4,128)S(1)} %copy-done.7, bf16[3072,1024]{1,0:T(8,128)(2,1)S(1)} %get-tuple-element.36.part, f32[24,128]{1,0:T(8,128)S(1)} %get-tuple-element.37.part_diag, f32[8,2,288,128]{3,2,1,0:T(8,128)S(1)} %all-to-all-done.near, f32[8,2,128,128]{3,2,1,0:T(8,128)S(1)} %collective-permute-done.far1, ...), custom_call_target="tpu_custom_call" | custom-call | flops 838860800 | bytes 14680064 | tf_op jit(solution)/shard_map/gain_solve/pallas_call | solution.py:568
  71.9 13.8 %all_to_all.10.gall = f32[16,2,1024]{2,1,0:T(2,128)S(1)} all-to-all(f32[16,2,1024]{2,1,0:T(2,128)S(1)} %gain_solve.1), channel_id=1, replica_groups=mesh['row'=8,'col'=2,'chan'=16] {'row','col'}, dimensions={0} | all-to-all | bytes 262144 | tf_op jit(solution)/shard_map/gather_gains/all_to_all | solution.py:584
  85.7 2.9 %residual.1 = (f32[2,8,128,512]{3,2,1,0:T(8,128)}, f32[2,4,2,1024]{3,2,1,0:T(2,128)}) custom-call(f32[2,8,128,512]{3,2,1,0:T(8,128)S(1)} %bitcast.8, f32[4,128,512]{2,1,0:T(8,128)S(1)} %get-tuple-element.26.re_early, f32[4,128,512]{2,1,0:T(8,128)S(1)} %copy-done.4, f32[4,128,512]{2,1,0:T(8,128)S(1)} %get-tuple-element.34.re_late, ...), custom_call_target="tpu_custom_call" | custom-call | flops 33554432 | bytes 12582912 | tf_op jit(solution)/shard_map/residual/pallas_call | solution.py:587
  (28 shorter events, 0.1 us)
Async XLA Ops:
  0.6 10.5 %copy-start.15 = (f32[2,1024]{1,0:T(2,128)S(1)}, f32[2,1024]{1,0:T(2,128)}, u32[]{:S(2)}) copy-start(f32[2,1024]{1,0:T(2,128)} %param.7) | copy-start | bytes 24580
  0.6 10.5 %copy-start.14 = (f32[4,2,1024]{2,1,0:T(2,128)S(1)}, f32[4,2,1024]{2,1,0:T(2,128)}, u32[]{:S(2)}) copy-start(f32[4,2,1024]{2,1,0:T(2,128)} %param.9) | copy-start | bytes 98308
  0.6 10.6 %copy-start.10 = (s32[1024]{0:T(1024)S(1)}, s32[1024]{0:T(1024)}, u32[]{:S(2)}) copy-start(s32[1024]{0:T(1024)} %param.8) | copy-start | bytes 12292
  0.7 10.6 %copy-start.12 = (f32[4]{0:T(128)S(1)}, f32[4]{0:T(128)}, u32[]{:S(2)}) copy-start(f32[4]{0:T(128)} %freqs.5) | copy-start | bytes 52
  4.1 38.2 %all-to-all-start = ((f32[8,2,288,128]{3,2,1,0:T(8,128)}), f32[8,2,288,128]{3,2,1,0:T(8,128)S(1)}, u32[]{:S(2)}, u32[]{:S(2)}) async-start(f32[8,2,288,128]{3,2,1,0:T(8,128)} %pack.1), calls=%async_computation | async-start | bytes 4718592 | tf_op jit(solution)/shard_map/to_the_rows/all_to_all | solution.py:490
  11.1 9.4 %copy-start.8 = (f32[1,2,8,128]{3,2,1,0:T(8,128)}, f32[1,2,8,128]{3,2,1,0:T(8,128)S(1)}, u32[]{:S(2)}) copy-start(f32[1,2,8,128]{3,2,1,0:T(8,128)S(1)} %copy.10) | copy-start | bytes 24580
  11.2 9.3 %copy-start.5 = (f32[8,8,128]{2,1,0:T(8,128)}, f32[8,8,128]{2,1,0:T(8,128)S(1)}, u32[]{:S(2)}) copy-start(f32[8,8,128]{2,1,0:T(8,128)S(1)} %reshape.22.flux) | copy-start | bytes 98308
  20.5 1.0 %copy-start.3 = (f32[4,128,512]{2,1,0:T(8,128)}, f32[4,128,512]{2,1,0:T(8,128)S(1)}, u32[]{:S(2)}) copy-start(f32[4,128,512]{2,1,0:T(8,128)S(1)} %get-tuple-element.27.im_early) | copy-start | bytes 3145732
  38.7 6.7 %copy-start.6 = (f32[8,8,128]{2,1,0:T(8,128)S(1)}, f32[8,8,128]{2,1,0:T(8,128)}, u32[]{:S(2)}) copy-start(f32[8,8,128]{2,1,0:T(8,128)} %copy-done.5) | copy-start | bytes 98308
  38.7 6.7 %copy-start.9 = (f32[1,2,8,128]{3,2,1,0:T(8,128)S(1)}, f32[1,2,8,128]{3,2,1,0:T(8,128)}, u32[]{:S(2)}) copy-start(f32[1,2,8,128]{3,2,1,0:T(8,128)} %copy-done.8) | copy-start | bytes 24580
  38.7 6.7 %copy-start.11 = (s32[1024]{0:T(1024)S(1)}, s32[1024]{0:T(1024)}, u32[]{:S(2)}) copy-start(s32[1024]{0:T(1024)} %param.8) | copy-start | bytes 12292
  38.7 6.7 %copy-start.13 = (f32[4]{0:T(128)S(1)}, f32[4]{0:T(128)}, u32[]{:S(2)}) copy-start(f32[4]{0:T(128)} %freqs.5) | copy-start | bytes 52
  42.4 16.7 %collective-permute-start = (f32[8,2,128,128]{3,2,1,0:T(8,128)S(1)}, f32[8,2,128,128]{3,2,1,0:T(8,128)S(1)}, u32[]{:S(2)}, u32[]{:S(2)}) collective-permute-start(f32[8,2,128,128]{3,2,1,0:T(8,128)S(1)} %slice.9), channel_id=1, source_target_pairs={{16,0},{48,32},{80,64},{112,96},{144,128},{176,160},{208,192},{240... | collective-permute-start | bytes 3145736 | tf_op jit(solution)/shard_map/to_the_active_column/ppermute | solution.py:551
  43.9 10.9 %copy-start.1 = (f32[1024,1024]{1,0:T(8,128)S(1)}, f32[1024,1024]{1,0:T(8,128)}, u32[]{:S(2)}) copy-start(f32[1024,1024]{1,0:T(8,128)} %get-tuple-element.29.m_re) | copy-start | bytes 12582916
  43.9 10.9 %copy-start.2 = (f32[1024,1024]{1,0:T(8,128)S(1)}, f32[1024,1024]{1,0:T(8,128)}, u32[]{:S(2)}) copy-start(f32[1024,1024]{1,0:T(8,128)} %get-tuple-element.30.m_im) | copy-start | bytes 12582916
  43.9 18.2 %collective-permute-start.1 = (f32[4,2,256,128]{3,2,1,0:T(8,128)S(1)}, f32[4,2,256,128]{3,2,1,0:T(8,128)S(1)}, u32[]{:S(2)}, u32[]{:S(2)}) collective-permute-start(f32[4,2,256,128]{3,2,1,0:T(8,128)S(1)} %pad_maximum_fusion), channel_id=1, source_target_pairs={{16,128},{48,160},{80,192},{112,224},{144,0},{176,32},{208,64},{24... | collective-permute-start | bytes 3145736 | tf_op jit(solution)/shard_map/to_the_active_column/ppermute | solution.py:551
  54.8 7.3 %copy-start.7 = (s32[4,1024]{1,0:T(4,128)S(1)}, s32[4,1024]{1,0:T(4,128)}, u32[]{:S(2)}) copy-start(s32[4,1024]{1,0:T(4,128)} %flags.1) | copy-start | bytes 49156
  62.1 23.6 %copy-start = (f32[2,4,2,128,512]{4,3,2,1,0:T(8,128)S(1)}, f32[2,4,2,128,512]{4,3,2,1,0:T(8,128)}, u32[]{:S(2)}) copy-start(f32[2,4,2,128,512]{4,3,2,1,0:T(8,128)} %param.6) | copy-start | bytes 12582916
  62.1 23.6 %copy-start.4 = (f32[4,128,512]{2,1,0:T(8,128)S(1)}, f32[4,128,512]{2,1,0:T(8,128)}, u32[]{:S(2)}) copy-start(f32[4,128,512]{2,1,0:T(8,128)} %copy-done.3) | copy-start | bytes 3145732

commit v5 on v4

--- a/solution.py
+++ b/solution.py
@@ -16,7 +16,9 @@
 MAGIC = 12582912.0
 F32 = jnp.float32
 BF16 = jnp.bfloat16
-ROWS = 288
+ROWS = 272
+SPLIT = 136
+THIRD = 16
 
 
 def poly(y, coeffs):
@@ -172,24 +174,30 @@
     r, half = i % 4, i // 4
     solving = j == lax.axis_index("chan") % 2
     turn = jnp.where(solving, 0, 4)
-    loads = [pltpu.make_async_copy(vis.at[:, k], vin.at[k], in_sem.at[k]) for k in range(8)]
+    base = jnp.where((half == 1) & (j == 0), 1, 0)
+    lanes = [pl.ds(pl.multiple_of((r + base + n) % 4 * T, T), T) for n in range(3)]
+    loads = [
+        pltpu.make_async_copy(vis.at[:, k, :, lanes[n]], vin.at[k, n], in_sem.at[k, n])
+        for k in range(8)
+        for n in range(3)
+    ]
     stores = []
     for k in range(8):
-        stores.append(pltpu.make_async_copy(chunk.at[k, :, 0:T], packed.at[k, :, 0:T], one_sem.at[k]))
+        stores.append(pltpu.make_async_copy(chunk.at[k, :, 0:SPLIT], packed.at[k, :, 0:SPLIT], one_sem.at[k]))
         stores.append(
-            pltpu.make_async_copy(chunk.at[k, :, T:], packed.at[(k + turn) % 8, :, T:], two_sem.at[k])
+            pltpu.make_async_copy(chunk.at[k, :, SPLIT:], packed.at[(k + turn) % 8, :, SPLIT:], two_sem.at[k])
         )
     for load in loads:
         load.start()
-    left = lax.broadcasted_iota(jnp.int32, (32, T), 1) < 64
+    lane = lax.broadcasted_iota(jnp.int32, (32, T), 1)
 
     def run(place):
         for k in range(8):
-            loads[k].wait()
+            for load in loads[3 * k:3 * k + 3]:
+                load.wait()
 
             def block(z, n):
-                lane = pl.multiple_of(((r + n) % 4) * T, T)
-                return vin[k, z, :, pl.ds(lane, T)]
+                return vin[k, n, z]
 
             for z in range(2):
                 if place == DIAGONAL:
@@ -198,19 +206,19 @@
                     turned = third.T[64:T]
                     chunk[k, z, T:T + 64, :] = jnp.where(r < 2, third[0:64], -turned if z else turned)
                     own = block(z, 0)
-                    chunk[k, z, T + 64:2 * T, :] = own[0:64]
-                    chunk[k, z, 2 * T:, :] = jnp.where(left, pltpu.roll(own[64:96], 64, 1), own[96:T])
+                    chunk[k, z, 192:224, :] = own[0:32]
+                    chunk[k, z, 224:256, :] = jnp.where(lane < 32, pltpu.roll(own[96:T], 32, 1), own[32:64])
+                    chunk[k, z, 256:, :] = jnp.where(lane[0:16] < 64, pltpu.roll(own[80:96], 64, 1), own[64:80])
                 else:
-                    off = jnp.where(half == 1, 1, 0)
-                    chunk[k, z, 0:T, :] = block(z, off)
-                    second = block(z, off + 1)
+                    chunk[k, z, 0:T, :] = block(z, 0)
+                    second = block(z, 1)
                     if place == SOLVING:
                         chunk[k, z, T:2 * T, :] = second
-                        chunk[k, z, 2 * T:, :] = block(z, off + 2)[0:32]
+                        chunk[k, z, 2 * T:, :] = block(z, 2)[0:THIRD]
                     else:
-                        turned = second.T[32:T]
-                        chunk[k, z, T:T + 96, :] = -turned if z else turned
-                        chunk[k, z, T + 96:, :] = jnp.zeros((64, T), F32)
+                        turned = second.T[THIRD:T]
+                        chunk[k, z, T:2 * T - THIRD, :] = -turned if z else turned
+                        chunk[k, z, 2 * T - THIRD:, :] = jnp.zeros((2 * THIRD, T), F32)
             stores[2 * k].start()
             stores[2 * k + 1].start()
 
@@ -258,12 +266,14 @@
         self.put(col, row, self.products(col, row, vr.T, -vi.T))
 
     def own_block(self, a, z):
-        low = lax.broadcasted_iota(jnp.int32, (64, T), 1) < 64
-        top = self.part_of(True, a, z, T + 64, 2 * T)
-        turned = jnp.concatenate([top, top], 0).T[64:T]
-        last = self.part_of(True, a, z, 2 * T, ROWS)
-        right = jnp.concatenate([pltpu.roll(last, 64, 1), last], 0)
-        return jnp.concatenate([top, jnp.where(low, -turned if z else turned, right)], 0)
+        row = lax.broadcasted_iota(jnp.int32, (T, T), 0)
+        lane = lax.broadcasted_iota(jnp.int32, (T, T), 1)
+        one = self.part_of(True, a, z, 192, 224)
+        two = self.part_of(True, a, z, 224, 256)
+        three = self.part_of(True, a, z, 256, ROWS)
+        upper = jnp.concatenate([one, two, three, pltpu.roll(three, 64, 1), pltpu.roll(two, 96, 1)], 0)
+        turned = upper.T
+        return jnp.where((lane >> 5) >= (row >> 5), upper, -turned if z else turned)
 
     def run(self):
         part_of, fill = self.part_of, self.fill
@@ -288,7 +298,7 @@
                 fill(b, 4 * jj + (r + off + 1) % 4, part_of(False, b, 0, T, 2 * T), part_of(False, b, 1, T, 2 * T))
             else:
                 for z in range(2):
-                    halves[z, 2 + (r + off + 1) % 4, 32:T, :] = part_of(False, b, z, T, T + 96)
+                    halves[z, 2 + (r + off + 1) % 4, THIRD:T, :] = part_of(False, b, z, T, 2 * T - THIRD)
             return 0
 
         lax.fori_loop(0, 4, sources, 0)
@@ -310,10 +320,14 @@
 
 def of_far(far1, far2):
     def part_of(diagonal, a, z, lo, hi):
-        if hi <= T:
-            return far1[a, z, lo:hi, :]
-        start = lo - T + (0 if diagonal else ROWS - T)
-        return far2[a % 4, z, start:start + hi - lo, :]
+        parts = []
+        if lo < SPLIT:
+            parts.append(far1[a, z, lo:min(hi, SPLIT), :])
+        if hi > SPLIT:
+            start = max(lo, SPLIT)
+            at = start - SPLIT + (0 if diagonal else ROWS - SPLIT)
+            parts.append(far2[a % 4, z, at:at + hi - start, :])
+        return parts[0] if len(parts) == 1 else jnp.concatenate(parts, 0)
 
     return part_of
 
@@ -346,18 +360,18 @@
 def gain_solve(flags, part, part_diag, near, far1, far2, m_re, m_im, out, cc, halves, diag, sem):
     @pl.when(is_solver())
     def _():
-        copy = pltpu.make_async_copy(part, cc, sem)
+        copy = pltpu.make_async_copy(part.at[0:2048], cc, sem)
         copy.start()
         diag[...] = part_diag[...]
         copy.wait()
-        solve(flags, near, far1, far2, m_re, m_im, out, cc, halves, diag)
+        solve(flags, part, near, far1, far2, m_re, m_im, out, cc, halves, diag)
 
     @pl.when(jnp.logical_not(is_solver()))
     def _():
         out[...] = jnp.zeros_like(out)
 
 
-def solve(flags, near, far1, far2, m_re, m_im, out, cc, halves, diag):
+def solve(flags, part, near, far1, far2, m_re, m_im, out, cc, halves, diag):
     cp, j = lax.axis_index("row"), lax.axis_index("col")
     filler = Filler(1, of_far(far1, far2), m_re, m_im, cc, halves, diag)
     filler.run()
@@ -366,7 +380,7 @@
     def thirds(r, _):
         a = 4 * (1 - j) + r
         for z in range(2):
-            halves[z, 2 + r, 0:32, :] = near[a, z, 2 * T:ROWS, :]
+            halves[z, 2 + r, 0:THIRD, :] = near[a, z, 2 * T:ROWS, :]
         filler.fill(a, 4 * j + (r + near_off + 2) % 4, halves[0, 2 + r], halves[1, 2 + r])
         return 0
 
@@ -397,11 +411,11 @@
             [
                 stack((0, hr), (1, hi), (3, hr_lo), (4, hi_lo)),
                 stack((0, -hi), (1, hr), (3, -hi_lo), (4, hr_lo)),
-                stack((2, hd), (5, hd_lo)),
             ],
             1,
         ).astype(BF16)
-        sums = dot(left, cc[...], ((1,), (0,)))
+        powers = stack((2, hd), (5, hd_lo)).astype(BF16)
+        sums = dot(left, cc[...], ((1,), (0,))) + dot(powers, part[2048:3072, :], ((1,), (0,)))
         num_re = sums[0:1] + sums[3:4] + (hr * d_re - hi * d_im)
         num_im = sums[1:2] + sums[4:5] + (hr * d_im + hi * d_re)
         den = sums[2:3] + sums[5:6] + hd * d_den
@@ -477,9 +491,9 @@
             in_specs=[ANY],
             out_specs=ANY,
             scratch_shapes=[
-                pltpu.VMEM((8, 2, T, 512), F32),
+                pltpu.VMEM((8, 3, 2, T, T), F32),
                 pltpu.VMEM((8, 2, ROWS, T), F32),
-                pltpu.SemaphoreType.DMA((8,)),
+                pltpu.SemaphoreType.DMA((8, 3)),
                 pltpu.SemaphoreType.DMA((8,)),
                 pltpu.SemaphoreType.DMA((8,)),
             ],
@@ -530,11 +544,11 @@
         near, m_re, m_im, *early = lax.optimization_barrier((near, m_re, m_im, *block(0)))
         mine = 4 * lax.axis_index("col")
         pieces = [
-            near[:, :, 0:T],
+            near[:, :, 0:SPLIT],
             jnp.concatenate(
                 [
-                    lax.dynamic_slice_in_dim(near, mine, 4)[:, :, T:ROWS],
-                    lax.dynamic_slice_in_dim(near, 4 - mine, 4)[:, :, T:T + 96],
+                    lax.dynamic_slice_in_dim(near, mine, 4)[:, :, SPLIT:ROWS],
+                    lax.dynamic_slice_in_dim(near, 4 - mine, 4)[:, :, SPLIT:2 * T - THIRD],
                 ],
                 2,
             ),
@@ -571,7 +585,7 @@
             in_specs=[VMEM] * 8,
             out_specs=VMEM,
             scratch_shapes=[
-                pltpu.VMEM((3072, 1024), BF16),
+                pltpu.VMEM((2048, 1024), BF16),
                 pltpu.VMEM((2, 6, T, T), F32),
                 pltpu.VMEM((24, T), F32),
                 pltpu.SemaphoreType.DMA,

time: 88.9 us -> 86.4 us (0.972)
  waiting for transfers between devices: 8.3 us -> 6.14 us
    all_to_all x1, waiting for transfers between devices: 3.54 us -> 2.33 us  [body(): near = lax.all_to_all(packed, 'row', 0, 0, tiled=True)]
    ppermute x2, waiting for transfers between devices: 4.76 us -> 3.8 us  [body(): far.append(lax.ppermute(piece, ('row', 'col', 'chan'), pairs))]
  transfers between devices with their start and end apart: 3 -> 3, of which waited for: 3 -> 2; matrix products, arithmetic and copies ran while one was open for 0% -> 0% of each run, Pallas kernels for 43% -> 45%
where the time goes in v5:
time: 86.4 us; the launch traced here: 86 us
  Pallas kernels  54.6 us (63%)
  blocking collectives  13.4 us (16%)
  starting transfers between devices  9.62 us (11%)
  waiting for transfers between devices  6.14 us (7%)
  local copies, waits for them, and re-layouts  1.23 us (1%)
  between operations  0.96 us (1%)
    pallas_call x2, Pallas kernels, block(): pl.pallas_call(functools.partial(block_model, first), out_shape=(shape(4,...  18.6 us
    pallas_call x1, Pallas kernels, body(): pl.pallas_call(own_model, out_shape=(shape(1024, 1024),) * 2, in_specs=[S...  17.2 us
    all_to_all x1, blocking collectives, body(): gall = lax.all_to_all(g, ('row', 'col'), 0, 0, tiled=True)  13.4 us
    pallas_call x1, Pallas kernels, body(): pl.pallas_call(gain_solve, out_shape=shape(rows * cols, 2, 1024), in_spec...  9.91 us
    all_to_all x1, starting transfers between devices, body(): near = lax.all_to_all(packed, 'row', 0, 0, tiled=True)  6.9 us
    ppermute x2, waiting for transfers between devices, body(): far.append(lax.ppermute(piece, ('row', 'col', 'chan'), pairs))  3.8 us
    pallas_call x1, Pallas kernels, body(): pl.pallas_call(pack, out_shape=shape(8, 2, ROWS, T), in_specs=[ANY], out_...  3.29 us
    pallas_call x1, Pallas kernels, body(): pl.pallas_call(residual, out_shape=(shape(2, 8, T, 512), shape(2, 4, 2, 1...  2.91 us
  transfers between devices with their start and end apart: 3, of which 2 were waited for; matrix products, arithmetic and copies ran while one was open for 0% of the time, Pallas kernels for 45%

profile of v5, /device:TPU:32, one launch (start us, length us, event | category | flops | bytes accessed | tf_op | source)
XLA Modules:
  0.0 86.0 jit_solution(16775818127895970786)
XLA Ops:
  0.6 3.3 %pack.1 = f32[8,2,272,128]{3,2,1,0:T(8,128)} custom-call(f32[2,8,128,512]{3,2,1,0:T(8,128)} %bitcast.7), custom_call_target="tpu_custom_call" | custom-call | flops 1048576 | bytes 7340032 | tf_op jit(solution)/shard_map/pack/pallas_call | solution.py:488
  3.9 0.0 copy-start.15
  3.9 0.0 copy-start.14
  4.0 0.0 copy-start.10
  4.0 0.0 copy-start.12
  4.0 6.9 %all-to-all-start = ((f32[8,2,272,128]{3,2,1,0:T(8,128)}), f32[8,2,272,128]{3,2,1,0:T(8,128)S(1)}, u32[]{:S(2)}, u32[]{:S(2)}) async-start(f32[8,2,272,128]{3,2,1,0:T(8,128)} %pack.1), calls=%async_computation | async-start | bytes 4456448 | tf_op jit(solution)/shard_map/to_the_rows/all_to_all | solution.py:504
  11.0 0.0 copy-start.5
  11.0 9.3 %to_the_active_column.1 = (f32[4,128,512]{2,1,0:T(8,128)S(1)}, f32[4,128,512]{2,1,0:T(8,128)S(1)}) custom-call(f32[4]{0:T(128)S(1)} %copy-done.12, f32[2,8,128]{2,1,0:T(8,128)S(1)} %bitcast.9, s32[8,128]{1,0:T(8,128)S(1)} %bitcast.13, f32[8,8,128]{2,1,0:T(8,128)S(1)} %reshape.22.flux), custom_call_target="tpu_custom_call" | custom-call | flops 4294967296 | bytes 2097152 | tf_op jit(solution)/shard_map/to_the_active_column/pallas_call | solution.py:524
  20.3 1.0 %copy-done.3 = f32[4,128,512]{2,1,0:T(8,128)} copy-done((f32[4,128,512]{2,1,0:T(8,128)}, f32[4,128,512]{2,1,0:T(8,128)S(1)}, u32[]{:S(2)}) %copy-start.3) | copy-done | bytes 1048600
  21.3 17.2 %own_model.1 = (f32[1024,1024]{1,0:T(8,128)}, f32[1024,1024]{1,0:T(8,128)}) custom-call(f32[4]{0:T(128)} %freqs.5, f32[2,8,128]{2,1,0:T(8,128)} %bitcast.10, s32[8,128]{1,0:T(8,128)} %bitcast.12, f32[8,8,128]{2,1,0:T(8,128)} %copy-done.5), custom_call_target="tpu_custom_call" | custom-call | flops 8589934592 | bytes 8388608 | tf_op jit(solution)/shard_map/own_model/pallas_call | solution.py:507
  38.5 2.3 %all-to-all-done.near = f32[8,2,272,128]{3,2,1,0:T(8,128)S(1)} async-done(((f32[8,2,272,128]{3,2,1,0:T(8,128)}), f32[8,2,272,128]{3,2,1,0:T(8,128)S(1)}, u32[]{:S(2)}, u32[]{:S(2)}) %all-to-all-start) | async-done | bytes 2228256 | tf_op jit(solution)/shard_map/to_the_rows/all_to_all | solution.py:504
  40.8 0.1 slice.9
  40.9 0.0 copy-start.6
  40.9 0.0 copy-start.11
  40.9 1.4 %collective-permute-start = (f32[8,2,136,128]{3,2,1,0:T(8,128)S(1)}, f32[8,2,136,128]{3,2,1,0:T(8,128)S(1)}, u32[]{:S(2)}, u32[]{:S(2)}) collective-permute-start(f32[8,2,136,128]{3,2,1,0:T(8,128)S(1)} %slice.9), channel_id=1, source_target_pairs={{16,0},{48,32},{80,64},{112,96},{144,128},{176,160},{208,192},{240... | collective-permute-start | bytes 3342344 | tf_op jit(solution)/shard_map/to_the_active_column/ppermute | solution.py:565
  42.4 0.1 pad_maximum_fusion
  42.5 1.3 %collective-permute-start.1 = (f32[4,2,240,128]{3,2,1,0:T(8,128)S(1)}, f32[4,2,240,128]{3,2,1,0:T(8,128)S(1)}, u32[]{:S(2)}, u32[]{:S(2)}) collective-permute-start(f32[4,2,240,128]{3,2,1,0:T(8,128)S(1)} %pad_maximum_fusion), channel_id=1, source_target_pairs={{16,128},{48,160},{80,192},{112,224},{144,0},{176,32},{208,64},{24... | collective-permute-start | bytes 2949128 | tf_op jit(solution)/shard_map/to_the_active_column/ppermute | solution.py:565
  43.9 9.3 %block_model.1 = (f32[4,128,512]{2,1,0:T(8,128)S(1)}, f32[4,128,512]{2,1,0:T(8,128)S(1)}) custom-call(f32[4]{0:T(128)S(1)} %copy-done.13, f32[2,8,128]{2,1,0:T(8,128)S(1)} %bitcast.11, s32[8,128]{1,0:T(8,128)S(1)} %bitcast.14, f32[8,8,128]{2,1,0:T(8,128)S(1)} %copy-done.6), custom_call_target="tpu_custom_call" | custom-call | flops 4294967296 | bytes 2097152 | tf_op jit(solution)/shard_map/block_model/pallas_call | solution.py:524
  53.2 0.0 copy-start.7
  53.2 2.7 %prepare.1 = (bf16[3072,1024]{1,0:T(8,128)(2,1)S(1)}, f32[24,128]{1,0:T(8,128)S(1)}) custom-call(f32[8,2,272,128]{3,2,1,0:T(8,128)S(1)} %all-to-all-done.near, f32[1024,1024]{1,0:T(8,128)S(1)} %copy-done.1, f32[1024,1024]{1,0:T(8,128)S(1)} %copy-done.2), custom_call_target="tpu_custom_call" | custom-call | flops 16777216 | bytes 16777216 | tf_op jit(solution)/shard_map/prepare/pallas_call | solution.py:570
  55.9 3.8 %collective-permute-done.1.far2 = f32[4,2,240,128]{3,2,1,0:T(8,128)S(1)} collective-permute-done((f32[4,2,240,128]{3,2,1,0:T(8,128)S(1)}, f32[4,2,240,128]{3,2,1,0:T(8,128)S(1)}, u32[]{:S(2)}, u32[]{:S(2)}) %collective-permute-start.1) | collective-permute-done | bytes 983072 | tf_op jit(solution)/shard_map/to_the_active_column/ppermute | solution.py:565
  59.7 9.9 %gain_solve.1 = f32[16,2,1024]{2,1,0:T(2,128)S(1)} custom-call(s32[4,1024]{1,0:T(4,128)S(1)} %copy-done.7, bf16[3072,1024]{1,0:T(8,128)(2,1)S(1)} %get-tuple-element.36.part, f32[24,128]{1,0:T(8,128)S(1)} %get-tuple-element.37.part_diag, f32[8,2,272,128]{3,2,1,0:T(8,128)S(1)} %all-to-all-done.near, f32[8,2,136,128]{3,2,1,0:T(8,128)S(1)} %collective-permute-done.far1, ...), custom_call_target="tpu_custom_call" | custom-call | flops 838860800 | bytes 14680064 | tf_op jit(solution)/shard_map/gain_solve/pallas_call | solution.py:582
  69.7 13.4 %all_to_all.10.gall = f32[16,2,1024]{2,1,0:T(2,128)S(1)} all-to-all(f32[16,2,1024]{2,1,0:T(2,128)S(1)} %gain_solve.1), channel_id=1, replica_groups=mesh['row'=8,'col'=2,'chan'=16] {'row','col'}, dimensions={0} | all-to-all | bytes 262144 | tf_op jit(solution)/shard_map/gather_gains/all_to_all | solution.py:598
  83.1 2.9 %residual.1 = (f32[2,8,128,512]{3,2,1,0:T(8,128)}, f32[2,4,2,1024]{3,2,1,0:T(2,128)}) custom-call(f32[2,8,128,512]{3,2,1,0:T(8,128)S(1)} %bitcast.8, f32[4,128,512]{2,1,0:T(8,128)S(1)} %get-tuple-element.26.re_early, f32[4,128,512]{2,1,0:T(8,128)S(1)} %copy-done.4, f32[4,128,512]{2,1,0:T(8,128)S(1)} %get-tuple-element.34.re_late, ...), custom_call_target="tpu_custom_call" | custom-call | flops 33554432 | bytes 12582912 | tf_op jit(solution)/shard_map/residual/pallas_call | solution.py:601
  (28 shorter events, 0.2 us)
Async XLA Ops:
  3.9 7.0 %copy-start.15 = (f32[2,1024]{1,0:T(2,128)S(1)}, f32[2,1024]{1,0:T(2,128)}, u32[]{:S(2)}) copy-start(f32[2,1024]{1,0:T(2,128)} %param.7) | copy-start | bytes 24580
  3.9 7.0 %copy-start.14 = (f32[4,2,1024]{2,1,0:T(2,128)S(1)}, f32[4,2,1024]{2,1,0:T(2,128)}, u32[]{:S(2)}) copy-start(f32[4,2,1024]{2,1,0:T(2,128)} %param.9) | copy-start | bytes 98308
  4.0 7.0 %copy-start.10 = (s32[1024]{0:T(1024)S(1)}, s32[1024]{0:T(1024)}, u32[]{:S(2)}) copy-start(s32[1024]{0:T(1024)} %param.8) | copy-start | bytes 12292
  4.0 7.0 %copy-start.12 = (f32[4]{0:T(128)S(1)}, f32[4]{0:T(128)}, u32[]{:S(2)}) copy-start(f32[4]{0:T(128)} %freqs.5) | copy-start | bytes 52
  4.0 36.8 %all-to-all-start = ((f32[8,2,272,128]{3,2,1,0:T(8,128)}), f32[8,2,272,128]{3,2,1,0:T(8,128)S(1)}, u32[]{:S(2)}, u32[]{:S(2)}) async-start(f32[8,2,272,128]{3,2,1,0:T(8,128)} %pack.1), calls=%async_computation | async-start | bytes 4456448 | tf_op jit(solution)/shard_map/to_the_rows/all_to_all | solution.py:504
  10.9 9.4 %copy-start.8 = (f32[1,2,8,128]{3,2,1,0:T(8,128)}, f32[1,2,8,128]{3,2,1,0:T(8,128)S(1)}, u32[]{:S(2)}) copy-start(f32[1,2,8,128]{3,2,1,0:T(8,128)S(1)} %copy.10) | copy-start | bytes 24580
  11.0 9.3 %copy-start.5 = (f32[8,8,128]{2,1,0:T(8,128)}, f32[8,8,128]{2,1,0:T(8,128)S(1)}, u32[]{:S(2)}) copy-start(f32[8,8,128]{2,1,0:T(8,128)S(1)} %reshape.22.flux) | copy-start | bytes 98308
  20.3 1.0 %copy-start.3 = (f32[4,128,512]{2,1,0:T(8,128)}, f32[4,128,512]{2,1,0:T(8,128)S(1)}, u32[]{:S(2)}) copy-start(f32[4,128,512]{2,1,0:T(8,128)S(1)} %get-tuple-element.27.im_early) | copy-start | bytes 3145732
  40.9 3.0 %copy-start.6 = (f32[8,8,128]{2,1,0:T(8,128)S(1)}, f32[8,8,128]{2,1,0:T(8,128)}, u32[]{:S(2)}) copy-start(f32[8,8,128]{2,1,0:T(8,128)} %copy-done.5) | copy-start | bytes 98308
  40.9 3.0 %copy-start.9 = (f32[1,2,8,128]{3,2,1,0:T(8,128)S(1)}, f32[1,2,8,128]{3,2,1,0:T(8,128)}, u32[]{:S(2)}) copy-start(f32[1,2,8,128]{3,2,1,0:T(8,128)} %copy-done.8) | copy-start | bytes 24580
  40.9 3.0 %copy-start.11 = (s32[1024]{0:T(1024)S(1)}, s32[1024]{0:T(1024)}, u32[]{:S(2)}) copy-start(s32[1024]{0:T(1024)} %param.8) | copy-start | bytes 12292
  40.9 3.0 %copy-start.13 = (f32[4]{0:T(128)S(1)}, f32[4]{0:T(128)}, u32[]{:S(2)}) copy-start(f32[4]{0:T(128)} %freqs.5) | copy-start | bytes 52
  40.9 18.8 %collective-permute-start = (f32[8,2,136,128]{3,2,1,0:T(8,128)S(1)}, f32[8,2,136,128]{3,2,1,0:T(8,128)S(1)}, u32[]{:S(2)}, u32[]{:S(2)}) collective-permute-start(f32[8,2,136,128]{3,2,1,0:T(8,128)S(1)} %slice.9), channel_id=1, source_target_pairs={{16,0},{48,32},{80,64},{112,96},{144,128},{176,160},{208,192},{240... | collective-permute-start | bytes 3342344 | tf_op jit(solution)/shard_map/to_the_active_column/ppermute | solution.py:565
  42.5 17.2 %collective-permute-start.1 = (f32[4,2,240,128]{3,2,1,0:T(8,128)S(1)}, f32[4,2,240,128]{3,2,1,0:T(8,128)S(1)}, u32[]{:S(2)}, u32[]{:S(2)}) collective-permute-start(f32[4,2,240,128]{3,2,1,0:T(8,128)S(1)} %pad_maximum_fusion), channel_id=1, source_target_pairs={{16,128},{48,160},{80,192},{112,224},{144,0},{176,32},{208,64},{24... | collective-permute-start | bytes 2949128 | tf_op jit(solution)/shard_map/to_the_active_column/ppermute | solution.py:565
  43.9 9.3 %copy-start.1 = (f32[1024,1024]{1,0:T(8,128)S(1)}, f32[1024,1024]{1,0:T(8,128)}, u32[]{:S(2)}) copy-start(f32[1024,1024]{1,0:T(8,128)} %get-tuple-element.29.m_re) | copy-start | bytes 12582916
  43.9 9.3 %copy-start.2 = (f32[1024,1024]{1,0:T(8,128)S(1)}, f32[1024,1024]{1,0:T(8,128)}, u32[]{:S(2)}) copy-start(f32[1024,1024]{1,0:T(8,128)} %get-tuple-element.30.m_im) | copy-start | bytes 12582916
  53.2 6.5 %copy-start.7 = (s32[4,1024]{1,0:T(4,128)S(1)}, s32[4,1024]{1,0:T(4,128)}, u32[]{:S(2)}) copy-start(s32[4,1024]{1,0:T(4,128)} %flags.1) | copy-start | bytes 49156
  59.7 23.4 %copy-start = (f32[2,4,2,128,512]{4,3,2,1,0:T(8,128)S(1)}, f32[2,4,2,128,512]{4,3,2,1,0:T(8,128)}, u32[]{:S(2)}) copy-start(f32[2,4,2,128,512]{4,3,2,1,0:T(8,128)} %param.6) | copy-start | bytes 12582916
  59.7 23.4 %copy-start.4 = (f32[4,128,512]{2,1,0:T(8,128)S(1)}, f32[4,128,512]{2,1,0:T(8,128)}, u32[]{:S(2)}) copy-start(f32[4,128,512]{2,1,0:T(8,128)} %copy-done.3) | copy-start | bytes 3145732

commit v6 on v5

--- a/solution.py
+++ b/solution.py
@@ -275,11 +275,10 @@
         turned = upper.T
         return jnp.where((lane >> 5) >= (row >> 5), upper, -turned if z else turned)
 
-    def run(self):
+    def inner(self):
         part_of, fill = self.part_of, self.fill
         halves, diag = self.refs[3:]
         jj = (lax.axis_index("col") + self.side) % 2
-        off = jnp.where(jj == 0, 1, 0)
         eye = on_diagonal()
 
         def sources(r, _):
@@ -292,6 +291,23 @@
             for z in range(2):
                 rs = pl.ds(pl.multiple_of((r // 2) * 64, 64), 64)
                 halves[z, r % 2, rs, :] = part_of(True, a, z, T, T + 64)
+            return 0
+
+        lax.fori_loop(0, 4, sources, 0)
+
+        def across(p, _):
+            fill(4 * jj + p, 4 * jj + p + 2, halves[0, p], halves[1, p])
+            return 0
+
+        lax.fori_loop(0, 2, across, 0)
+
+    def outer(self):
+        part_of, fill = self.part_of, self.fill
+        halves = self.refs[3]
+        jj = (lax.axis_index("col") + self.side) % 2
+        off = jnp.where(jj == 0, 1, 0)
+
+        def sources(r, _):
             b = 4 * (1 - jj) + r
             fill(b, 4 * jj + (r + off) % 4, part_of(False, b, 0, 0, T), part_of(False, b, 1, 0, T))
             if self.side == 0:
@@ -302,12 +318,6 @@
             return 0
 
         lax.fori_loop(0, 4, sources, 0)
-
-        def across(p, _):
-            fill(4 * jj + p, 4 * jj + p + 2, halves[0, p], halves[1, p])
-            return 0
-
-        lax.fori_loop(0, 2, across, 0)
 
 
 def on_diagonal():
@@ -354,27 +364,39 @@
             return 0
 
         lax.fori_loop(0, 8, powers, 0)
-        Filler(0, of_near(near), m_re, m_im, cc, halves, diag).run()
+        filler = Filler(0, of_near(near), m_re, m_im, cc, halves, diag)
+        filler.inner()
+        filler.outer()
 
 
 def gain_solve(flags, part, part_diag, near, far1, far2, m_re, m_im, out, cc, halves, diag, sem):
     @pl.when(is_solver())
     def _():
-        copy = pltpu.make_async_copy(part.at[0:2048], cc, sem)
-        copy.start()
+        j = lax.axis_index("col")
+        copies = []
+        for n in range(2):
+            mine = pl.ds(pl.multiple_of(n * 1024 + 512 * j, 512), 512)
+            other = pl.ds(pl.multiple_of(n * 1024 + 512 * (1 - j), 512), 512)
+            lanes = pl.ds(pl.multiple_of(512 * j, 512), 512)
+            copies.append(pltpu.make_async_copy(part.at[mine], cc.at[mine], sem.at[n, 0]))
+            copies.append(pltpu.make_async_copy(part.at[other, lanes], cc.at[other, lanes], sem.at[n, 1]))
+        for copy in copies:
+            copy.start()
         diag[...] = part_diag[...]
-        copy.wait()
-        solve(flags, part, near, far1, far2, m_re, m_im, out, cc, halves, diag)
+        solve(copies, flags, part, near, far1, far2, m_re, m_im, out, cc, halves, diag)
 
     @pl.when(jnp.logical_not(is_solver()))
     def _():
         out[...] = jnp.zeros_like(out)
 
 
-def solve(flags, part, near, far1, far2, m_re, m_im, out, cc, halves, diag):
+def solve(copies, flags, part, near, far1, far2, m_re, m_im, out, cc, halves, diag):
     cp, j = lax.axis_index("row"), lax.axis_index("col")
     filler = Filler(1, of_far(far1, far2), m_re, m_im, cc, halves, diag)
-    filler.run()
+    filler.inner()
+    for copy in copies:
+        copy.wait()
+    filler.outer()
     near_off = jnp.where(j == 0, 1, 0)
 
     def thirds(r, _):
@@ -588,7 +610,7 @@
                 pltpu.VMEM((2048, 1024), BF16),
                 pltpu.VMEM((2, 6, T, T), F32),
                 pltpu.VMEM((24, T), F32),
-                pltpu.SemaphoreType.DMA,
+                pltpu.SemaphoreType.DMA((2, 2)),
             ],
             compiler_params=vmem(27),
             cost_estimate=pl.CostEstimate(flops=800 << 20, bytes_accessed=14 << 20, transcendentals=0),

time: 86.4 us -> 86.6 us (level)
  no operation moved by 1% of the time
where the time goes in v6:
time: 86.6 us; the launch traced here: 86.2 us
  Pallas kernels  54.9 us (63%)
  blocking collectives  13.4 us (15%)
  starting transfers between devices  9.62 us (11%)
  waiting for transfers between devices  5.98 us (7%)
  local copies, waits for them, and re-layouts  1.23 us (1%)
  between operations  0.96 us (1%)
    pallas_call x2, Pallas kernels, block(): pl.pallas_call(functools.partial(block_model, first), out_shape=(shape(4,...  18.6 us
    pallas_call x1, Pallas kernels, body(): pl.pallas_call(own_model, out_shape=(shape(1024, 1024),) * 2, in_specs=[S...  17.2 us
    all_to_all x1, blocking collectives, body(): gall = lax.all_to_all(g, ('row', 'col'), 0, 0, tiled=True)  13.4 us
    pallas_call x1, Pallas kernels, body(): pl.pallas_call(gain_solve, out_shape=shape(rows * cols, 2, 1024), in_spec...  10.1 us
    all_to_all x1, starting transfers between devices, body(): near = lax.all_to_all(packed, 'row', 0, 0, tiled=True)  6.9 us
    ppermute x2, waiting for transfers between devices, body(): far.append(lax.ppermute(piece, ('row', 'col', 'chan'), pairs))  3.64 us
    pallas_call x1, Pallas kernels, body(): pl.pallas_call(pack, out_shape=shape(8, 2, ROWS, T), in_specs=[ANY], out_...  3.29 us
    pallas_call x1, Pallas kernels, body(): pl.pallas_call(residual, out_shape=(shape(2, 8, T, 512), shape(2, 4, 2, 1...  2.91 us
  transfers between devices with their start and end apart: 3, of which 2 were waited for; matrix products, arithmetic and copies ran while one was open for 0% of the time, Pallas kernels for 45%

profile of v6, /device:TPU:32, one launch (start us, length us, event | category | flops | bytes accessed | tf_op | source)
XLA Modules:
  0.0 86.2 jit_solution(12503925763405460296)
XLA Ops:
  0.6 3.3 %pack.1 = f32[8,2,272,128]{3,2,1,0:T(8,128)} custom-call(f32[2,8,128,512]{3,2,1,0:T(8,128)} %bitcast.7), custom_call_target="tpu_custom_call" | custom-call | flops 1048576 | bytes 7340032 | tf_op jit(solution)/shard_map/pack/pallas_call | solution.py:510
  3.9 0.0 copy-start.15
  3.9 0.0 copy-start.14
  4.0 0.0 copy-start.10
  4.0 0.0 copy-start.12
  4.0 6.9 %all-to-all-start = ((f32[8,2,272,128]{3,2,1,0:T(8,128)}), f32[8,2,272,128]{3,2,1,0:T(8,128)S(1)}, u32[]{:S(2)}, u32[]{:S(2)}) async-start(f32[8,2,272,128]{3,2,1,0:T(8,128)} %pack.1), calls=%async_computation | async-start | bytes 4456448 | tf_op jit(solution)/shard_map/to_the_rows/all_to_all | solution.py:526
  11.0 0.0 copy-start.5
  11.0 9.3 %to_the_active_column.1 = (f32[4,128,512]{2,1,0:T(8,128)S(1)}, f32[4,128,512]{2,1,0:T(8,128)S(1)}) custom-call(f32[4]{0:T(128)S(1)} %copy-done.12, f32[2,8,128]{2,1,0:T(8,128)S(1)} %bitcast.9, s32[8,128]{1,0:T(8,128)S(1)} %bitcast.13, f32[8,8,128]{2,1,0:T(8,128)S(1)} %reshape.22.flux), custom_call_target="tpu_custom_call" | custom-call | flops 4294967296 | bytes 2097152 | tf_op jit(solution)/shard_map/to_the_active_column/pallas_call | solution.py:546
  20.3 1.0 %copy-done.3 = f32[4,128,512]{2,1,0:T(8,128)} copy-done((f32[4,128,512]{2,1,0:T(8,128)}, f32[4,128,512]{2,1,0:T(8,128)S(1)}, u32[]{:S(2)}) %copy-start.3) | copy-done | bytes 1048600
  21.3 17.2 %own_model.1 = (f32[1024,1024]{1,0:T(8,128)}, f32[1024,1024]{1,0:T(8,128)}) custom-call(f32[4]{0:T(128)} %freqs.5, f32[2,8,128]{2,1,0:T(8,128)} %bitcast.10, s32[8,128]{1,0:T(8,128)} %bitcast.12, f32[8,8,128]{2,1,0:T(8,128)} %copy-done.5), custom_call_target="tpu_custom_call" | custom-call | flops 8589934592 | bytes 8388608 | tf_op jit(solution)/shard_map/own_model/pallas_call | solution.py:529
  38.5 2.3 %all-to-all-done.near = f32[8,2,272,128]{3,2,1,0:T(8,128)S(1)} async-done(((f32[8,2,272,128]{3,2,1,0:T(8,128)}), f32[8,2,272,128]{3,2,1,0:T(8,128)S(1)}, u32[]{:S(2)}, u32[]{:S(2)}) %all-to-all-start) | async-done | bytes 2228256 | tf_op jit(solution)/shard_map/to_the_rows/all_to_all | solution.py:526
  40.8 0.1 slice.9
  40.9 0.0 copy-start.6
  40.9 0.0 copy-start.11
  40.9 1.4 %collective-permute-start = (f32[8,2,136,128]{3,2,1,0:T(8,128)S(1)}, f32[8,2,136,128]{3,2,1,0:T(8,128)S(1)}, u32[]{:S(2)}, u32[]{:S(2)}) collective-permute-start(f32[8,2,136,128]{3,2,1,0:T(8,128)S(1)} %slice.9), channel_id=1, source_target_pairs={{16,0},{48,32},{80,64},{112,96},{144,128},{176,160},{208,192},{240... | collective-permute-start | bytes 3342344 | tf_op jit(solution)/shard_map/to_the_active_column/ppermute | solution.py:587
  42.4 0.1 pad_maximum_fusion
  42.5 1.3 %collective-permute-start.1 = (f32[4,2,240,128]{3,2,1,0:T(8,128)S(1)}, f32[4,2,240,128]{3,2,1,0:T(8,128)S(1)}, u32[]{:S(2)}, u32[]{:S(2)}) collective-permute-start(f32[4,2,240,128]{3,2,1,0:T(8,128)S(1)} %pad_maximum_fusion), channel_id=1, source_target_pairs={{16,128},{48,160},{80,192},{112,224},{144,0},{176,32},{208,64},{24... | collective-permute-start | bytes 2949128 | tf_op jit(solution)/shard_map/to_the_active_column/ppermute | solution.py:587
  43.9 9.3 %block_model.1 = (f32[4,128,512]{2,1,0:T(8,128)S(1)}, f32[4,128,512]{2,1,0:T(8,128)S(1)}) custom-call(f32[4]{0:T(128)S(1)} %copy-done.13, f32[2,8,128]{2,1,0:T(8,128)S(1)} %bitcast.11, s32[8,128]{1,0:T(8,128)S(1)} %bitcast.14, f32[8,8,128]{2,1,0:T(8,128)S(1)} %copy-done.6), custom_call_target="tpu_custom_call" | custom-call | flops 4294967296 | bytes 2097152 | tf_op jit(solution)/shard_map/block_model/pallas_call | solution.py:546
  53.2 0.0 copy-start.7
  53.2 2.9 %prepare.1 = (bf16[3072,1024]{1,0:T(8,128)(2,1)S(1)}, f32[24,128]{1,0:T(8,128)S(1)}) custom-call(f32[8,2,272,128]{3,2,1,0:T(8,128)S(1)} %all-to-all-done.near, f32[1024,1024]{1,0:T(8,128)S(1)} %copy-done.1, f32[1024,1024]{1,0:T(8,128)S(1)} %copy-done.2), custom_call_target="tpu_custom_call" | custom-call | flops 16777216 | bytes 16777216 | tf_op jit(solution)/shard_map/prepare/pallas_call | solution.py:592
  56.1 3.6 %collective-permute-done.1.far2 = f32[4,2,240,128]{3,2,1,0:T(8,128)S(1)} collective-permute-done((f32[4,2,240,128]{3,2,1,0:T(8,128)S(1)}, f32[4,2,240,128]{3,2,1,0:T(8,128)S(1)}, u32[]{:S(2)}, u32[]{:S(2)}) %collective-permute-start.1) | collective-permute-done | bytes 983072 | tf_op jit(solution)/shard_map/to_the_active_column/ppermute | solution.py:587
  59.7 10.1 %gain_solve.1 = f32[16,2,1024]{2,1,0:T(2,128)S(1)} custom-call(s32[4,1024]{1,0:T(4,128)S(1)} %copy-done.7, bf16[3072,1024]{1,0:T(8,128)(2,1)S(1)} %get-tuple-element.36.part, f32[24,128]{1,0:T(8,128)S(1)} %get-tuple-element.37.part_diag, f32[8,2,272,128]{3,2,1,0:T(8,128)S(1)} %all-to-all-done.near, f32[8,2,136,128]{3,2,1,0:T(8,128)S(1)} %collective-permute-done.far1, ...), custom_call_target="tpu_custom_call" | custom-call | flops 838860800 | bytes 14680064 | tf_op jit(solution)/shard_map/gain_solve/pallas_call | solution.py:604
  69.8 13.4 %all_to_all.10.gall = f32[16,2,1024]{2,1,0:T(2,128)S(1)} all-to-all(f32[16,2,1024]{2,1,0:T(2,128)S(1)} %gain_solve.1), channel_id=1, replica_groups=mesh['row'=8,'col'=2,'chan'=16] {'row','col'}, dimensions={0} | all-to-all | bytes 262144 | tf_op jit(solution)/shard_map/gather_gains/all_to_all | solution.py:620
  83.3 2.9 %residual.1 = (f32[2,8,128,512]{3,2,1,0:T(8,128)}, f32[2,4,2,1024]{3,2,1,0:T(2,128)}) custom-call(f32[2,8,128,512]{3,2,1,0:T(8,128)S(1)} %bitcast.8, f32[4,128,512]{2,1,0:T(8,128)S(1)} %get-tuple-element.26.re_early, f32[4,128,512]{2,1,0:T(8,128)S(1)} %copy-done.4, f32[4,128,512]{2,1,0:T(8,128)S(1)} %get-tuple-element.34.re_late, ...), custom_call_target="tpu_custom_call" | custom-call | flops 33554432 | bytes 12582912 | tf_op jit(solution)/shard_map/residual/pallas_call | solution.py:623
  (28 shorter events, 0.2 us)
Async XLA Ops:
  3.9 7.0 %copy-start.15 = (f32[2,1024]{1,0:T(2,128)S(1)}, f32[2,1024]{1,0:T(2,128)}, u32[]{:S(2)}) copy-start(f32[2,1024]{1,0:T(2,128)} %param.7) | copy-start | bytes 24580
  3.9 7.0 %copy-start.14 = (f32[4,2,1024]{2,1,0:T(2,128)S(1)}, f32[4,2,1024]{2,1,0:T(2,128)}, u32[]{:S(2)}) copy-start(f32[4,2,1024]{2,1,0:T(2,128)} %param.9) | copy-start | bytes 98308
  4.0 7.0 %copy-start.10 = (s32[1024]{0:T(1024)S(1)}, s32[1024]{0:T(1024)}, u32[]{:S(2)}) copy-start(s32[1024]{0:T(1024)} %param.8) | copy-start | bytes 12292
  4.0 7.0 %copy-start.12 = (f32[4]{0:T(128)S(1)}, f32[4]{0:T(128)}, u32[]{:S(2)}) copy-start(f32[4]{0:T(128)} %freqs.5) | copy-start | bytes 52
  4.0 36.8 %all-to-all-start = ((f32[8,2,272,128]{3,2,1,0:T(8,128)}), f32[8,2,272,128]{3,2,1,0:T(8,128)S(1)}, u32[]{:S(2)}, u32[]{:S(2)}) async-start(f32[8,2,272,128]{3,2,1,0:T(8,128)} %pack.1), calls=%async_computation | async-start | bytes 4456448 | tf_op jit(solution)/shard_map/to_the_rows/all_to_all | solution.py:526
  10.9 9.4 %copy-start.8 = (f32[1,2,8,128]{3,2,1,0:T(8,128)}, f32[1,2,8,128]{3,2,1,0:T(8,128)S(1)}, u32[]{:S(2)}) copy-start(f32[1,2,8,128]{3,2,1,0:T(8,128)S(1)} %copy.10) | copy-start | bytes 24580
  11.0 9.3 %copy-start.5 = (f32[8,8,128]{2,1,0:T(8,128)}, f32[8,8,128]{2,1,0:T(8,128)S(1)}, u32[]{:S(2)}) copy-start(f32[8,8,128]{2,1,0:T(8,128)S(1)} %reshape.22.flux) | copy-start | bytes 98308
  20.3 1.0 %copy-start.3 = (f32[4,128,512]{2,1,0:T(8,128)}, f32[4,128,512]{2,1,0:T(8,128)S(1)}, u32[]{:S(2)}) copy-start(f32[4,128,512]{2,1,0:T(8,128)S(1)} %get-tuple-element.27.im_early) | copy-start | bytes 3145732
  40.9 3.0 %copy-start.6 = (f32[8,8,128]{2,1,0:T(8,128)S(1)}, f32[8,8,128]{2,1,0:T(8,128)}, u32[]{:S(2)}) copy-start(f32[8,8,128]{2,1,0:T(8,128)} %copy-done.5) | copy-start | bytes 98308
  40.9 3.0 %copy-start.9 = (f32[1,2,8,128]{3,2,1,0:T(8,128)S(1)}, f32[1,2,8,128]{3,2,1,0:T(8,128)}, u32[]{:S(2)}) copy-start(f32[1,2,8,128]{3,2,1,0:T(8,128)} %copy-done.8) | copy-start | bytes 24580
  40.9 3.0 %copy-start.11 = (s32[1024]{0:T(1024)S(1)}, s32[1024]{0:T(1024)}, u32[]{:S(2)}) copy-start(s32[1024]{0:T(1024)} %param.8) | copy-start | bytes 12292
  40.9 3.0 %copy-start.13 = (f32[4]{0:T(128)S(1)}, f32[4]{0:T(128)}, u32[]{:S(2)}) copy-start(f32[4]{0:T(128)} %freqs.5) | copy-start | bytes 52
  40.9 18.8 %collective-permute-start = (f32[8,2,136,128]{3,2,1,0:T(8,128)S(1)}, f32[8,2,136,128]{3,2,1,0:T(8,128)S(1)}, u32[]{:S(2)}, u32[]{:S(2)}) collective-permute-start(f32[8,2,136,128]{3,2,1,0:T(8,128)S(1)} %slice.9), channel_id=1, source_target_pairs={{16,0},{48,32},{80,64},{112,96},{144,128},{176,160},{208,192},{240... | collective-permute-start | bytes 3342344 | tf_op jit(solution)/shard_map/to_the_active_column/ppermute | solution.py:587
  42.5 17.2 %collective-permute-start.1 = (f32[4,2,240,128]{3,2,1,0:T(8,128)S(1)}, f32[4,2,240,128]{3,2,1,0:T(8,128)S(1)}, u32[]{:S(2)}, u32[]{:S(2)}) collective-permute-start(f32[4,2,240,128]{3,2,1,0:T(8,128)S(1)} %pad_maximum_fusion), channel_id=1, source_target_pairs={{16,128},{48,160},{80,192},{112,224},{144,0},{176,32},{208,64},{24... | collective-permute-start | bytes 2949128 | tf_op jit(solution)/shard_map/to_the_active_column/ppermute | solution.py:587
  43.9 9.3 %copy-start.1 = (f32[1024,1024]{1,0:T(8,128)S(1)}, f32[1024,1024]{1,0:T(8,128)}, u32[]{:S(2)}) copy-start(f32[1024,1024]{1,0:T(8,128)} %get-tuple-element.29.m_re) | copy-start | bytes 12582916
  43.9 9.3 %copy-start.2 = (f32[1024,1024]{1,0:T(8,128)S(1)}, f32[1024,1024]{1,0:T(8,128)}, u32[]{:S(2)}) copy-start(f32[1024,1024]{1,0:T(8,128)} %get-tuple-element.30.m_im) | copy-start | bytes 12582916
  53.2 6.5 %copy-start.7 = (s32[4,1024]{1,0:T(4,128)S(1)}, s32[4,1024]{1,0:T(4,128)}, u32[]{:S(2)}) copy-start(s32[4,1024]{1,0:T(4,128)} %flags.1) | copy-start | bytes 49156
  59.7 23.5 %copy-start = (f32[2,4,2,128,512]{4,3,2,1,0:T(8,128)S(1)}, f32[2,4,2,128,512]{4,3,2,1,0:T(8,128)}, u32[]{:S(2)}) copy-start(f32[2,4,2,128,512]{4,3,2,1,0:T(8,128)} %param.6) | copy-start | bytes 12582916
  59.7 23.5 %copy-start.4 = (f32[4,128,512]{2,1,0:T(8,128)S(1)}, f32[4,128,512]{2,1,0:T(8,128)}, u32[]{:S(2)}) copy-start(f32[4,128,512]{2,1,0:T(8,128)} %copy-done.3) | copy-start | bytes 3145732
